TPU v7x, 32 devices: a whole 2x2x4 slice. The times are simulated.
32 devices in a mesh: dp: 2 (over core), mp: 16 (over z, y, x).
Axes of the slice: x: 2, y: 2, z: 4, core: 2. Of those that a mesh axis runs over, the one named last changes fastest.
Arguments:
- queries: bfloat16 [4096, 768], P(('dp', 'mp')), may hold values from -30 to 30
- first_owner: int32 [4096, 1], P(('dp', 'mp')), may hold values from 0 to 15; in each aligned block of 128 rows (0 to 127, 128 to 255, ...) at most 16 rows name the same one
- first_row: int32 [4096], P(('dp', 'mp')), may hold values from 0 to 255
- tool_table: bfloat16 [4096, 768], P('mp'), may hold values from -6 to 6
- norm_gain: bfloat16 [768], replicated, may hold values from 0.25 to 1.75
- weight_in: bfloat16 [3072, 768], P('mp'), may hold values from -0.21875 to 0.21875
- bias_in: bfloat16 [3072], P('mp'), may hold values from -3 to 3
- weight_out: bfloat16 [3072, 768], P('mp'), may hold values from -0.109375 to 0.109375
- bias_out: bfloat16 [768], replicated, may hold values from -3 to 3
- tool_embeds: bfloat16 [128, 768], P('dp'), may hold values from -2 to 2
- positive: int32 [4096], P(('dp', 'mp')), may hold values from 0 to 127
Outputs:
- updated: bfloat16 [4096, 768], P(('dp', 'mp'))
- chain_loss: float32 [4096], P(('dp', 'mp'))
- query_grad: float32 [4096, 768], P(('dp', 'mp'))
- tool_grad: float32 [128, 768], P('dp')
Inputs may be any that keep to these rules, and one draw needn't show every extreme that they name: `first_owner`: among the 128 chains of one device at most 16 name the same owner, a bound that some block reaches of them.
All inputs are finite; a program needn't handle non-finite values.
Results may differ from a plain program's by a relative error of at most 0.0078.
Values may be sent and summed in bfloat16 or wider, within the bound.
No kernel may reach another device: no remote copies, remote signals or barrier semaphores. Data moves between devices by JAX's collectives and lax.ppermute only.
A program may use at most 64 MiB of HBM per device.

v0:
```python
import jax
import jax.numpy as jnp
import numpy as np
from jax import lax
from jax.sharding import PartitionSpec as P


def from_behind(block, axis, distance):
    devices = range(lax.axis_size(axis))
    route = [((i - distance) % len(devices), i) for i in devices]
    return lax.ppermute(block, axis, route)


def layer_normed(combined, norm_gain):
    row_mean = jnp.mean(combined, axis=1, keepdims=True)
    centred = combined - row_mean
    spread = jnp.mean(centred * centred, axis=1, keepdims=True)
    return (centred * lax.rsqrt(spread + 1e-05) * norm_gain.astype(jnp.float32)[None, :]).astype(
        jnp.bfloat16
    )


def hidden_terms(pieces, normed):
    in_piece, bias_piece, out_piece = pieces
    preact = lax.dot_general(
        normed, in_piece, (((1,), (1,)), ((), ())), preferred_element_type=jnp.float32
    )
    preact = preact + bias_piece.astype(jnp.float32)[None, :]
    activated = jax.nn.gelu(preact, approximate=True).astype(jnp.bfloat16)
    return jnp.dot(activated, out_piece, preferred_element_type=jnp.float32)


def local(
    queries,
    first_owner,
    first_row,
    tool_table,
    norm_gain,
    weight_in,
    bias_in,
    weight_out,
    bias_out,
    tool_embeds,
    positive,
):
    chain_count, feature_count = queries.shape
    groups = lax.axis_size("mp")
    cycle_size = lax.axis_size("dp")
    cycle_index = lax.axis_index("dp")
    capacity = 2 * chain_count // groups
    owner_ids = first_owner[:, 0]
    owner_marks = (owner_ids[:, None] == jnp.arange(groups, dtype=jnp.int32)[None, :]).astype(
        jnp.int32
    )
    rank_in_owner = jnp.sum((jnp.cumsum(owner_marks, axis=0) - owner_marks) * owner_marks, axis=1)
    slot_index = owner_ids * capacity + rank_in_owner
    request = (
        jnp.zeros((groups * capacity,), jnp.int32)
        .at[slot_index]
        .set(first_row)
        .reshape(groups, capacity)
    )
    table_rows = jnp.take(
        tool_table, lax.all_to_all(request, "mp", split_axis=0, concat_axis=0, tiled=True), axis=0
    )
    fetched = lax.all_to_all(table_rows, "mp", split_axis=0, concat_axis=0, tiled=True)
    first_rows = fetched.reshape(groups * capacity, feature_count)[slot_index]
    combined = queries.astype(jnp.float32) + first_rows.astype(jnp.float32)
    normed = layer_normed(combined, norm_gain)
    branch_sum = hidden_terms(
        (
            lax.all_gather(weight_in, "mp", axis=0, tiled=True),
            lax.all_gather(bias_in, "mp", axis=0, tiled=True),
            lax.all_gather(weight_out, "mp", axis=0, tiled=True),
        ),
        normed,
    )
    updated = (combined + branch_sum + bias_out.astype(jnp.float32)[None, :]).astype(jnp.bfloat16)
    block_rows = tool_embeds.shape[0]
    forward_hops = cycle_size - 1
    block_list = [tool_embeds]
    offset_list = [0]
    visiting = tool_embeds
    for hop_number in range(forward_hops):
        visiting = from_behind(visiting, "dp", 1)
        block_list.append(visiting)
        offset_list.append(hop_number + 1)
    all_tools = jnp.concatenate(block_list, axis=0)
    block_owner = (cycle_index - jnp.asarray(offset_list, jnp.int32)) % cycle_size
    column_ids = (
        block_owner[:, None] * block_rows + jnp.arange(block_rows, dtype=jnp.int32)[None, :]
    ).reshape(-1)
    scores = lax.dot_general(
        updated, all_tools, (((1,), (1,)), ((), ())), preferred_element_type=jnp.float32
    )
    row_max = jnp.max(scores, axis=1, keepdims=True)
    log_total = row_max + jnp.log(jnp.sum(jnp.exp(scores - row_max), axis=1, keepdims=True))
    is_positive = (column_ids[None, :] == positive[:, None]).astype(jnp.float32)
    chain_loss = log_total[:, 0] - jnp.sum(scores * is_positive, axis=1)
    weights_grad = (jnp.exp(scores - log_total) - is_positive).astype(jnp.bfloat16)
    query_grad = jnp.dot(weights_grad, all_tools, preferred_element_type=jnp.float32)
    position_of = np.zeros((cycle_size,), np.int32)
    for list_index, offset_value in enumerate(offset_list):
        position_of[offset_value] = list_index

    def block_term(offset_value):
        list_index = int(position_of[offset_value])
        columns = weights_grad[:, list_index * block_rows : (list_index + 1) * block_rows]
        return lax.dot_general(
            columns, updated, (((0,), (0,)), ((), ())), preferred_element_type=jnp.float32
        )

    partial_grad = jnp.zeros((block_rows, feature_count), jnp.float32)
    for hop_number in range(cycle_size - 1):
        partial_grad = partial_grad + block_term(hop_number + 1)
        partial_grad = from_behind(partial_grad.astype(jnp.bfloat16), "dp", 1).astype(
            partial_grad.dtype
        )
    partial_grad = partial_grad + block_term(0)
    grad_scale = (block_rows * cycle_size / (chain_count * groups * cycle_size)) ** 0.5
    tool_grad = lax.psum(partial_grad, "mp") * grad_scale
    return (updated, chain_loss, query_grad, tool_grad)


def solution(mesh):
    in_specs = (
        P(("dp", "mp"), None),
        P(("dp", "mp"), None),
        P(("dp", "mp")),
        P("mp", None),
        P(),
        P("mp", None),
        P("mp"),
        P("mp", None),
        P(),
        P("dp", None),
        P(("dp", "mp")),
    )
    out_specs = (P(("dp", "mp"), None), P(("dp", "mp")), P(("dp", "mp"), None), P("dp", None))
    return jax.shard_map(local, mesh=mesh, in_specs=in_specs, out_specs=out_specs, check_vma=False)
```

profile of v0, /device:TPU:0, one launch (start us, length us, event | category | flops | bytes accessed | tf_op | source)
XLA Modules:
  0.0 302.1 jit_solution(15448461498427537323)
XLA Ops:
  7.2 0.7 all-gather.3.cloned.1.call-update
  8.0 0.7 all-gather.5.cloned.1.call-update
  8.7 0.7 fusion.20
  9.4 0.2 reduce_window_sum.11
  9.6 0.8 select_reduce_fusion
  10.4 0.7 fusion.28
  11.1 1.1 scatter_custom_fusion
  12.2 0.1 all_to_all.13
  12.3 15.4 %all_to_all.20 = s32[16,1,16]{2,1,0:T(1,128)S(1)} all-to-all(s32[16,1,16]{2,1,0:T(1,128)S(1)} %all_to_all.13), channel_id=1, replica_groups=mesh['dp'=2,'mp'=16] {'mp'}, dimensions={0} | all-to-all | bytes 2048 | tf_op jit(solution)/shard_map/all_to_all | solution.py:64
  27.8 1.2 gather_fusion
  29.0 0.9 broadcast_select_fusion
  29.9 3.7 %all-to-all-start.1 = ((bf16[16,16,768]{2,1,0:T(8,128)(2,1)}), bf16[16,16,768]{2,1,0:T(8,128)(2,1)S(1)}, u32[]{:S(2)}, u32[]{:S(2)}) async-start(bf16[16,16,768]{2,1,0:T(8,128)(2,1)} %broadcast_select_fusion), calls=%async_computation.1 | async-start | bytes 786432 | tf_op jit(solution)/shard_map/all_to_all | solution.py:66
  33.8 0.6 dynamic-slice
  35.0 0.2 dynamic-update-slice
  35.3 43.7 %all-reduce = bf16[3072]{0:T(1024)(128)(2,1)S(1)} all-reduce(bf16[3072]{0:T(1024)(128)(2,1)S(1)} %dynamic-update-slice), channel_id=1, replica_groups=mesh['dp'=2,'mp'=16] {'mp'}, use_global_device_ids=true, to_apply=%add | all-reduce | flops 3072 | bytes 12288
  79.1 0.1 add.134
  79.2 0.9 gather_fusion.1
  80.1 0.1 fusion.10
  80.3 0.2 multiply_reduce_fusion
  80.5 16.1 %all-gather.3.cloned.1.call-done = bf16[3072,768]{1,0:T(8,128)(2,1)} async-done(((bf16[192,768]{1,0:T(8,128)(2,1)}), bf16[3072,768]{1,0:T(8,128)(2,1)}) %all-gather.3.cloned.1.call-update) | async-done | bytes 4718608 | tf_op jit(solution)/shard_map/all_gather | solution.py:72
  96.6 82.1 %all-gather.5.cloned.1.call-done = bf16[3072,768]{1,0:T(8,128)(2,1)} async-done(((bf16[192,768]{1,0:T(8,128)(2,1)}), bf16[3072,768]{1,0:T(8,128)(2,1)}) %all-gather.5.cloned.1.call-update) | async-done | bytes 4718608 | tf_op jit(solution)/shard_map/all_gather | solution.py:74
  178.7 6.2 %fusion.9 = bf16[128,768]{1,0:T(8,128)(2,1)S(1)} fusion(bf16[3072,768]{1,0:T(8,128)(2,1)} %all-gather.5.cloned.1.call-done, bf16[3072,768]{1,0:T(8,128)(2,1)} %all-gather.3.cloned.1.call-done, f32[3072]{0:T(1024)S(1)} %convert_element_type.44, bf16[128,768]{1,0:T(8,128)(2,1)S(1)} %gather_fusion.1, bf16[128,768]{1,0:T(8,128)(2,1)S(1)} %copy-done.2, ...), kind=kOutput, calls=%fused_computation.15 | convolution fusion | flops 1213169664 | bytes 10046464 | tf_op jit(solution)/shard_map/dot_general | solution.py:30
  185.0 0.2 fusion.36
  185.2 0.1 fusion.17
  185.3 0.5 fusion.35
  185.8 0.1 fusion.19
  185.9 0.2 convolution_convert_fusion
  186.2 1.3 collective-permute-done.1
  187.5 0.8 convert_add_fusion.3
  188.3 1.0 fusion.37
  189.3 104.6 %all-reduce.3.cloned.1.call-done = f32[64,768]{1,0:T(8,128)} async-done(((f32[64,768]{1,0:T(8,128)}), f32[64,768]{1,0:T(8,128)}) %all-reduce.3.cloned.1.call-update) | async-done | bytes 196624 | tf_op jit(solution)/shard_map/psum | solution.py:121
  293.9 1.6 broadcast_multiply_fusion
  (41 shorter events, 0.6 us)
Async XLA Ops:
  7.2 20.6 %copy-start = (bf16[256,768]{1,0:T(8,128)(2,1)S(1)}, bf16[256,768]{1,0:T(8,128)(2,1)}, u32[]{:S(2)}) copy-start(bf16[256,768]{1,0:T(8,128)(2,1)} %param.15) | copy-start | bytes 1179652
  7.2 89.5 %all-gather.3.cloned.1.call-start = ((), (), s32[]{:S(2)}) async-start(), calls=%async_computation.2 | async-start | bytes 5013504 | tf_op jit(solution)/shard_map/all_gather | solution.py:72
  7.9 170.8 %all-gather.5.cloned.1.call-start = ((), (), s32[]{:S(2)}) async-start(), calls=%async_computation.3 | async-start | bytes 5013504 | tf_op jit(solution)/shard_map/all_gather | solution.py:74
  29.0 4.7 %copy-start.3 = (bf16[64,768]{1,0:T(8,128)(2,1)S(1)}, bf16[64,768]{1,0:T(8,128)(2,1)}, u32[]{:S(2)}) copy-start(bf16[64,768]{1,0:T(8,128)(2,1)} %param.21) | copy-start | bytes 294916
  29.0 4.8 %copy-start.8 = (u32[32]{0:T(128)S(1)}, u32[32]{0:T(128)}, u32[]{:S(2)}) copy-start(u32[32]{0:T(128)} %constant.73) | copy-start | bytes 388
  29.0 6.0 %copy-start.7 = (bf16[192]{0:T(256)(128)(2,1)S(1)}, bf16[192]{0:T(256)(128)(2,1)}, u32[]{:S(2)}) copy-start(bf16[192]{0:T(256)(128)(2,1)} %param.18) | copy-start | bytes 1156
  29.0 50.0 %copy-start.5 = (bf16[768]{0:T(1024)(128)(2,1)S(1)}, bf16[768]{0:T(1024)(128)(2,1)}, u32[]{:S(2)}) copy-start(bf16[768]{0:T(1024)(128)(2,1)} %param.16) | copy-start | bytes 4612
  29.0 50.0 %copy-start.6 = (bf16[768]{0:T(1024)(128)(2,1)S(1)}, bf16[768]{0:T(1024)(128)(2,1)}, u32[]{:S(2)}) copy-start(bf16[768]{0:T(1024)(128)(2,1)} %param.20) | copy-start | bytes 4612
  29.9 50.2 %copy-start.2 = (bf16[128,768]{1,0:T(8,128)(2,1)S(1)}, bf16[128,768]{1,0:T(8,128)(2,1)}, u32[]{:S(2)}) copy-start(bf16[128,768]{1,0:T(8,128)(2,1)} %param.12) | copy-start | bytes 589828
  29.9 49.3 %all-to-all-start.1 = ((bf16[16,16,768]{2,1,0:T(8,128)(2,1)}), bf16[16,16,768]{2,1,0:T(8,128)(2,1)S(1)}, u32[]{:S(2)}, u32[]{:S(2)}) async-start(bf16[16,16,768]{2,1,0:T(8,128)(2,1)} %broadcast_select_fusion), calls=%async_computation.1 | async-start | bytes 786432 | tf_op jit(solution)/shard_map/all_to_all | solution.py:66
  33.6 260.3 %all-reduce.3.cloned.1.call-start = ((), (), s32[]{:S(2)}) async-start(), calls=%async_computation.4 | async-start | bytes 393216 | tf_op jit(solution)/shard_map/psum | solution.py:121
  33.7 45.6 %collective-permute-start = (bf16[64,768]{1,0:T(8,128)(2,1)S(1)}, bf16[64,768]{1,0:T(8,128)(2,1)S(1)}, u32[]{:S(2)}, u32[]{:S(2)}) collective-permute-start(bf16[64,768]{1,0:T(8,128)(2,1)S(1)} %copy-done.3), channel_id=1, source_target_pairs={{16,0},{0,16},{17,1},{1,17},{18,2},{2,18},{19,3},{3,19},{20,4},{4,... | collective-permute-start | bytes 294920 | tf_op jit(solution)/shard_map/ppermute | solution.py:11
  80.5 104.7 %copy-start.4 = (s32[128]{0:T(128)S(1)}, s32[128]{0:T(128)}, u32[]{:S(2)}) copy-start(s32[128]{0:T(128)} %param.22) | copy-start | bytes 1540
  184.9 110.6 %copy-start.1 = (bf16[128,768]{1,0:T(8,128)(2,1)}, bf16[128,768]{1,0:T(8,128)(2,1)S(1)}, u32[]{:S(2)}) copy-start(bf16[128,768]{1,0:T(8,128)(2,1)S(1)} %fusion.9) | copy-start | bytes 589828
  186.1 1.4 collective-permute-start.1
Sparse Core Ops, SparseCore 0:
  10.8 85.7 all-gather.2
  99.4 79.2 all-gather.4
  188.4 105.4 all-reduce.2
where the time goes:
time: 302 us
  waiting for transfers between devices  206 us (68%)
  blocking collectives  59.1 us (20%)
  between operations  14.7 us (5%)
  matrix products  8.45 us (3%)
  other arithmetic  6.05 us (2%)
  local copies, waits for them, and re-layouts  4.33 us (1%)
  starting transfers between devices  3.94 us (1%)
    psum x1, waiting for transfers between devices, local(): tool_grad = lax.psum(partial_grad, 'mp') * grad_scale  105 us
    all_gather x1, waiting for transfers between devices, local(): lax.all_gather(weight_out, 'mp', axis=0, tiled=True)  82.1 us
    unnamed x1, blocking collectives  43.7 us
    all_gather x1, waiting for transfers between devices, local(): lax.all_gather(weight_in, 'mp', axis=0, tiled=True)  16.1 us
    all_to_all x1, blocking collectives, local(): lax.all_to_all(request, 'mp', split_axis=0, concat_axis=0, tiled=True)  15.4 us
    dot_general x1, matrix products, hidden_terms(): return jnp.dot(activated, out_piece, preferred_element_type=jnp.float32)  6.22 us
  transfers between devices with their start and end apart: 6, of which 4 were waited for; matrix products, arithmetic and copies ran while one was open for 3% of the time, Pallas kernels for 0%

commit v1 on v0

v1 whole, which is shorter than its diff:
```python
import functools

import jax
import jax.numpy as jnp
from jax import lax
from jax.experimental import pallas as pl
from jax.experimental.pallas import tpu as pltpu
from jax.sharding import PartitionSpec as P

F32 = jnp.float32
BF16 = jnp.bfloat16
VMEM_BYTES = 48 * 1024 * 1024


def flipped(block, axis, mask):
    return lax.ppermute(block, axis, [(i, i ^ mask) for i in range(lax.axis_size(axis))])


def kernel_call(body, out_shape, *args, smem=()):
    return pl.pallas_call(
        body,
        out_shape=out_shape,
        in_specs=[
            pl.BlockSpec(memory_space=pltpu.SMEM if i in smem else pltpu.VMEM) for i in range(len(args))
        ],
        out_specs=jax.tree.map(lambda _: pl.BlockSpec(memory_space=pltpu.VMEM), out_shape),
        compiler_params=pltpu.CompilerParams(vmem_limit_bytes=VMEM_BYTES),
    )(*args)


def iota(shape, dimension):
    return lax.broadcasted_iota(jnp.int32, shape, dimension)


def slots_of(owner, groups, capacity):
    chains = owner.shape[0]
    marks = (owner == iota((chains, groups), 1)).astype(F32)
    before = (iota((chains, chains), 1) < iota((chains, chains), 0)).astype(BF16)
    counts = jnp.dot(before, marks.astype(BF16), preferred_element_type=F32)
    rank = jnp.sum(counts * marks, axis=1, keepdims=True)
    return marks, rank, owner.astype(F32) * capacity + rank


def request_body(groups, capacity, owner_ref, row_ref, bias_ref, message_ref):
    owner = owner_ref[...]
    chains = owner.shape[0]
    bias_count = bias_ref.shape[1]
    marks, rank, _ = slots_of(owner, groups, capacity)
    ranked = (rank.astype(jnp.int32) == iota((chains, capacity), 1)).astype(F32) * row_ref[...].astype(F32)
    request = lax.dot_general(
        marks.astype(BF16), ranked.astype(BF16), (((0,), (0,)), ((), ())), preferred_element_type=F32
    )
    message_ref[...] = jnp.zeros_like(message_ref)
    message_ref[:, :bias_count] = jnp.broadcast_to(bias_ref[...].astype(F32), (groups, bias_count))
    message_ref[:, bias_count : bias_count + capacity] = request


def serve_body(capacity, bias_count, message_ref, table_ref, rows_ref):
    groups = message_ref.shape[0]
    slots, held = groups * capacity, table_ref.shape[0]
    wanted = message_ref[:, bias_count : bias_count + capacity].astype(BF16)
    spread = (iota((slots, groups), 0) // capacity == iota((slots, groups), 1)).astype(BF16)
    by_rank = jnp.dot(spread, wanted, preferred_element_type=F32)
    mine = (iota((slots, capacity), 0) % capacity == iota((slots, capacity), 1)).astype(F32)
    row = jnp.sum(by_rank * mine, axis=1, keepdims=True).astype(jnp.int32)
    pick = (row == iota((slots, held), 1)).astype(BF16)
    rows_ref[...] = jnp.dot(pick, table_ref[...], preferred_element_type=F32).astype(BF16)


def select_body(groups, capacity, owner_ref, fetched_ref, rows_ref):
    owner = owner_ref[...]
    _, _, slot = slots_of(owner, groups, capacity)
    pick = (slot.astype(jnp.int32) == iota((owner.shape[0], groups * capacity), 1)).astype(BF16)
    rows_ref[...] = jnp.dot(pick, fetched_ref[...], preferred_element_type=F32).astype(BF16)


def norm_body(queries_ref, queries2_ref, rows_ref, rows2_ref, gain_ref, combined_ref, normed_ref):
    chains = queries_ref.shape[0]
    gain = gain_ref[...].astype(F32)
    for at, (q_ref, r_ref) in enumerate(((queries_ref, rows_ref), (queries2_ref, rows2_ref))):
        combined = q_ref[...].astype(F32) + r_ref[...].astype(F32)
        centred = combined - jnp.mean(combined, axis=1, keepdims=True)
        spread = jnp.mean(centred * centred, axis=1, keepdims=True)
        combined_ref[at * chains : (at + 1) * chains, :] = combined
        normed_ref[at * chains : (at + 1) * chains, :] = (centred * lax.rsqrt(spread + 1e-05) * gain).astype(BF16)


def gelu(u):
    return 0.5 * u * (1.0 + jnp.tanh(0.7978845608028654 * (u + 0.044715 * (u * u * u))))


def hidden_body(plan, me_ref, normed_ref, message_ref, *refs):
    pieces, total_ref = refs[:-1], refs[-1]
    normed = normed_ref[...]
    me = me_ref[0]
    total = None
    for place, (in_at, in_row), (out_at, out_row), units in plan:
        preact = lax.dot_general(
            normed,
            pieces[in_at][in_row : in_row + units, :],
            (((1,), (1,)), ((), ())),
            preferred_element_type=F32,
        )
        bias = message_ref[pl.ds(me ^ place, 1), :][:, :units]
        activated = gelu(preact + bias).astype(BF16)
        term = jnp.dot(activated, pieces[out_at][out_row : out_row + units, :], preferred_element_type=F32)
        total = term if total is None else total + term
    total_ref[...] = total


def score_body(
    own_blocks,
    combined_ref,
    partial_ref,
    partial2_ref,
    bias_ref,
    tools_ref,
    columns_ref,
    positive_ref,
    updated_ref,
    loss_ref,
    weights_ref,
    *grad_refs,
):
    chains = updated_ref.shape[0]
    block_rows = tools_ref.shape[0] // own_blocks[1]
    both = combined_ref.shape[0]
    branch = partial_ref[...] + jnp.concatenate([partial2_ref[chains:, :], partial2_ref[:chains, :]], axis=0)
    updated = (combined_ref[...] + branch + bias_ref[...].astype(F32)).astype(BF16)
    updated_ref[...] = updated[:chains, :]
    scores = lax.dot_general(updated, tools_ref[...], (((1,), (1,)), ((), ())), preferred_element_type=F32)
    row_max = jnp.max(scores, axis=1, keepdims=True)
    log_total = row_max + jnp.log(jnp.sum(jnp.exp(scores - row_max), axis=1, keepdims=True))
    is_positive = (columns_ref[...] == positive_ref[...]).astype(F32)
    loss_ref[...] = (log_total - jnp.sum(scores * is_positive, axis=1, keepdims=True))[:chains, :]
    weights = (jnp.exp(scores - log_total) - is_positive).astype(BF16)
    weights_ref[...] = weights[:chains, :]
    for grad_ref, block in zip(grad_refs, own_blocks[0]):
        grad_ref[...] = lax.dot_general(
            weights[:, block * block_rows : (block + 1) * block_rows],
            updated,
            (((0,), (0,)), ((), ())),
            preferred_element_type=F32,
        ).astype(BF16)


def weight_pieces(own, units, groups):
    arrays, plan = [], []

    def whole(place, shard):
        arrays.append(shard)
        plan.append((place, (len(arrays) - 1, 0), (len(arrays) - 1, units), units))

    def halves(place, in_half, out_half):
        arrays.extend((in_half, out_half))
        plan.append((place, (len(arrays) - 2, 0), (len(arrays) - 1, 0), units))

    levels = range(0, groups, 4)
    column = {0: own}
    for level in levels:
        if level:
            column[level] = flipped(own, "mp", level)
    diagonal = flipped(own, "mp", 3)
    for level in levels:
        shard = column[level]
        by_x, by_y = flipped(shard, "mp", 1), flipped(shard, "mp", 2)
        whole(level, shard)
        whole(level ^ 1, by_x)
        whole(level ^ 2, by_y)
        if level == 0:
            whole(level ^ 3, diagonal)
        elif level == 4:
            whole(level ^ 3, flipped(diagonal, "mp", 4))
        else:
            halves(level ^ 3, flipped(by_y[:units], "mp", 1), flipped(by_x[units:], "mp", 2))
    return arrays, tuple(plan)


def local(
    queries,
    first_owner,
    first_row,
    tool_table,
    norm_gain,
    weight_in,
    bias_in,
    weight_out,
    bias_out,
    tool_embeds,
    positive,
):
    chains, features = queries.shape
    groups, cycle = lax.axis_size("mp"), lax.axis_size("dp")
    me, core = lax.axis_index("mp"), lax.axis_index("dp")
    capacity = 2 * chains // groups
    slots = groups * capacity
    units = weight_in.shape[0] // 2
    block_rows = tool_embeds.shape[0]
    half = core % 2

    own = jnp.concatenate(
        [
            lax.dynamic_slice_in_dim(weight_in, half * units, units, 0),
            lax.dynamic_slice_in_dim(weight_out, half * units, units, 0),
        ],
        axis=0,
    )
    own_bias = lax.dynamic_slice_in_dim(bias_in, half * units, units, 0)
    arrays, plan = weight_pieces(own, units, groups)

    width = -(-(units + capacity) // 128) * 128
    message = kernel_call(
        functools.partial(request_body, groups, capacity),
        jax.ShapeDtypeStruct((groups, width), F32),
        first_owner,
        first_row[:, None],
        own_bias[None, :],
    )
    asked = lax.all_to_all(message, "mp", split_axis=0, concat_axis=0, tiled=True)
    served = kernel_call(
        functools.partial(serve_body, capacity, units),
        jax.ShapeDtypeStruct((slots, features), BF16),
        asked,
        tool_table,
    )
    fetched = lax.all_to_all(served, "mp", split_axis=0, concat_axis=0, tiled=True)
    first_rows = kernel_call(
        functools.partial(select_body, groups, capacity),
        jax.ShapeDtypeStruct((chains, features), BF16),
        first_owner,
        fetched,
    )
    combined, normed = kernel_call(
        norm_body,
        (
            jax.ShapeDtypeStruct((2 * chains, features), F32),
            jax.ShapeDtypeStruct((2 * chains, features), BF16),
        ),
        queries,
        flipped(queries, "dp", 1),
        first_rows,
        flipped(first_rows, "dp", 1),
        norm_gain[None, :],
    )
    partial = kernel_call(
        functools.partial(hidden_body, plan),
        jax.ShapeDtypeStruct((2 * chains, features), F32),
        me[None],
        normed,
        asked,
        *arrays,
        smem=(0,),
    )

    tools = jnp.concatenate([tool_embeds] + [flipped(tool_embeds, "dp", j) for j in range(1, cycle)], axis=0)
    columns = jnp.concatenate(
        [(core ^ j) * block_rows + jnp.arange(block_rows, dtype=jnp.int32) for j in range(cycle)]
    )
    positives = jnp.concatenate([positive, flipped(positive, "dp", 1)])
    own_blocks = tuple(range(0, cycle, 2))
    updated, loss, weights, *grads = kernel_call(
        functools.partial(score_body, (own_blocks, cycle)),
        (
            jax.ShapeDtypeStruct((chains, features), BF16),
            jax.ShapeDtypeStruct((chains, 1), F32),
            jax.ShapeDtypeStruct((chains, block_rows * cycle), BF16),
        )
        + tuple(jax.ShapeDtypeStruct((block_rows, features), BF16) for _ in own_blocks),
        combined,
        partial,
        flipped(partial, "dp", 1),
        bias_out[None, :],
        tools,
        columns[None, :],
        positives[:, None],
    )
    query_grad = jnp.dot(weights, tools, preferred_element_type=F32)

    grad = grads[0].astype(F32)
    for block, term in zip(own_blocks[1:], grads[1:]):
        grad = grad + flipped(term, "dp", block).astype(F32)
    mask = 1
    while mask < groups:
        rounded = grad.astype(BF16)
        grad = rounded.astype(F32) + flipped(rounded, "mp", mask).astype(F32)
        mask *= 2
    grad_scale = (block_rows * cycle / (chains * groups * cycle)) ** 0.5
    return updated, loss[:, 0], query_grad, grad * grad_scale


def solution(mesh):
    in_specs = (
        P(("dp", "mp"), None),
        P(("dp", "mp"), None),
        P(("dp", "mp")),
        P("mp", None),
        P(),
        P("mp", None),
        P("mp"),
        P("mp", None),
        P(),
        P("dp", None),
        P(("dp", "mp")),
    )
    out_specs = (P(("dp", "mp"), None), P(("dp", "mp")), P(("dp", "mp"), None), P("dp", None))
    return jax.shard_map(local, mesh=mesh, in_specs=in_specs, out_specs=out_specs, check_vma=False)
```

time: 302 us -> 124 us (0.41)
  waiting for transfers between devices: 206 us -> 63.3 us
  blocking collectives: 59.1 us -> 0 us
  starting transfers between devices: 3.94 us -> 35.4 us
  between operations: 14.7 us -> 0.91 us
  Pallas kernels: 0 us -> 12 us
  matrix products: 8.45 us -> 0.94 us
  local copies, waits for them, and re-layouts: 4.33 us -> 10 us
  other arithmetic: 6.05 us -> 1.51 us
    psum x1 -> x0, waiting for transfers between devices: 105 us -> none  [local(): tool_grad = lax.psum(partial_grad, 'mp') * grad_scale]
    all_gather x2 -> x0, waiting for transfers between devices: 98.2 us -> none  [the longest x1 82.1 us: local(): lax.all_gather(weight_out, 'mp', axis=0, tiled=True)]
    ppermute x2 -> x26, waiting for transfers between devices: 1.29 us -> 57.1 us  [flipped(): lax.ppermute(block, axis, [(i, i ^ mask) for i in range(lax.axis_size(axi...]
    unnamed x1 -> x0, blocking collectives: 43.7 us -> none
    ppermute x2 -> x26, starting transfers between devices: 0.14 us -> 23.5 us  [flipped(): lax.ppermute(block, axis, [(i, i ^ mask) for i in range(lax.axis_size(axi...]
    all_to_all x1 -> x0, blocking collectives: 15.4 us -> none  [local(): lax.all_to_all(request, 'mp', split_axis=0, concat_axis=0, tiled=True)]
    pallas_call x0 -> x6, Pallas kernels: none -> 12 us  [kernel_call(): pl.pallas_call(body, out_shape=out_shape, in_specs=[pl.BlockSpec(memory_s...]
    all_to_all x1 -> x2, starting transfers between devices: 3.68 us -> 11.9 us  [the longest x1 8.31 us: local(): lax.all_to_all(message, 'mp', split_axis=0, concat_axis=0, tiled=True)]
  transfers between devices with their start and end apart: 6 -> 28, of which waited for: 4 -> 14; matrix products, arithmetic and copies ran while one was open for 3% -> 4% of each run, Pallas kernels for 0% -> 1%
where the time goes in v1:
time: 124 us
  waiting for transfers between devices  63.3 us (51%)
  starting transfers between devices  35.4 us (29%)
  Pallas kernels  12 us (10%)
  local copies, waits for them, and re-layouts  10 us (8%)
  other arithmetic  1.51 us (1%)
    ppermute x26, waiting for transfers between devices, flipped(): lax.ppermute(block, axis, [(i, i ^ mask) for i in range(lax.axis_size(axi...  57.1 us
    ppermute x26, starting transfers between devices, flipped(): lax.ppermute(block, axis, [(i, i ^ mask) for i in range(lax.axis_size(axi...  23.5 us
    pallas_call x6, Pallas kernels, kernel_call(): pl.pallas_call(body, out_shape=out_shape, in_specs=[pl.BlockSpec(memory_s...  12 us
    all_to_all x1, starting transfers between devices, local(): lax.all_to_all(message, 'mp', split_axis=0, concat_axis=0, tiled=True)  8.31 us
    all_to_all x1, waiting for transfers between devices, local(): lax.all_to_all(message, 'mp', split_axis=0, concat_axis=0, tiled=True)  6.24 us
    unnamed x38, local copies, waits for them, and re-layouts  5.41 us
    all_to_all x1, starting transfers between devices, local(): lax.all_to_all(served, 'mp', split_axis=0, concat_axis=0, tiled=True)  3.55 us
  transfers between devices with their start and end apart: 28, of which 14 were waited for; matrix products, arithmetic and copies ran while one was open for 4% of the time, Pallas kernels for 1%

profile of v1, /device:TPU:0, one launch (start us, length us, event | category | flops | bytes accessed | tf_op | source)
XLA Modules:
  0.0 124.0 jit_solution(10198573599513587132)
XLA Ops:
  2.3 1.1 shard_map.138
  3.4 8.3 %all-to-all-start = ((f32[16,1,128]{2,1,0:T(1,128)}), f32[16,1,128]{2,1,0:T(1,128)S(1)}, u32[]{:S(2)}, u32[]{:S(2)}) async-start(f32[16,1,128]{2,1,0:T(1,128)} %bitcast.3), calls=%async_computation | async-start | bytes 16384 | tf_op jit(solution)/shard_map/all_to_all | solution.py:219
  12.7 6.2 %all-to-all-done = f32[16,1,128]{2,1,0:T(1,128)S(1)} async-done(((f32[16,1,128]{2,1,0:T(1,128)}), f32[16,1,128]{2,1,0:T(1,128)S(1)}, u32[]{:S(2)}, u32[]{:S(2)}) %all-to-all-start) | async-done | bytes 8224 | tf_op jit(solution)/shard_map/all_to_all | solution.py:219
  18.9 1.3 %shard_map.139 = bf16[256,768]{1,0:T(8,128)(2,1)} custom-call(f32[16,128]{1,0:T(8,128)S(1)} %bitcast.16, bf16[256,768]{1,0:T(8,128)(2,1)S(1)} %copy-done.1), custom_call_target="tpu_custom_call" | custom-call | tf_op jit(solution)/shard_map/pallas_call | solution.py:20
  20.2 3.6 %all-to-all-start.1 = ((bf16[16,16,768]{2,1,0:T(8,128)(2,1)}), bf16[16,16,768]{2,1,0:T(8,128)(2,1)S(1)}, u32[]{:S(2)}, u32[]{:S(2)}) async-start(bf16[16,16,768]{2,1,0:T(8,128)(2,1)} %bitcast.5), calls=%async_computation.1 | async-start | bytes 786432 | tf_op jit(solution)/shard_map/all_to_all | solution.py:226
  23.8 2.8 %collective-permute-start.9 = (bf16[192,768]{1,0:T(8,128)(2,1)S(1)}, bf16[192,768]{1,0:T(8,128)(2,1)S(1)}, u32[]{:S(2)}, u32[]{:S(2)}) collective-permute-start(bf16[192,768]{1,0:T(8,128)(2,1)S(1)} %pad_maximum_fusion.refs_0_), channel_id=1, source_target_pairs={{0,8},{1,9},{2,10},{3,11},{4,12},{5,13},{6,14},{7,15},{8,0},{9,1},... | collective-permute-start | bytes 884744 | tf_op jit(solution)/shard_map/ppermute | solution.py:16
  26.6 1.5 %collective-permute-start.2 = (bf16[192,768]{1,0:T(8,128)(2,1)S(1)}, bf16[192,768]{1,0:T(8,128)(2,1)S(1)}, u32[]{:S(2)}, u32[]{:S(2)}) collective-permute-start(bf16[192,768]{1,0:T(8,128)(2,1)S(1)} %pad_maximum_fusion.refs_0_), channel_id=1, source_target_pairs={{0,1},{1,0},{2,3},{3,2},{4,5},{5,4},{6,7},{7,6},{8,9},{9,8},{10,11... | collective-permute-start | bytes 884744 | tf_op jit(solution)/shard_map/ppermute | solution.py:16
  28.1 1.4 %collective-permute-start.14 = (bf16[192,768]{1,0:T(8,128)(2,1)S(1)}, bf16[192,768]{1,0:T(8,128)(2,1)S(1)}, u32[]{:S(2)}, u32[]{:S(2)}) collective-permute-start(bf16[192,768]{1,0:T(8,128)(2,1)S(1)} %pad_maximum_fusion.refs_0_), channel_id=1, source_target_pairs={{0,12},{1,13},{2,14},{3,15},{4,8},{5,9},{6,10},{7,11},{8,4},{9,5},... | collective-permute-start | bytes 884744 | tf_op jit(solution)/shard_map/ppermute | solution.py:16
  29.5 1.5 %collective-permute-start.4 = (bf16[192,768]{1,0:T(8,128)(2,1)S(1)}, bf16[192,768]{1,0:T(8,128)(2,1)}, u32[]{:S(2)}, u32[]{:S(2)}) collective-permute-start(bf16[192,768]{1,0:T(8,128)(2,1)S(1)} %pad_maximum_fusion.refs_0_), channel_id=1, source_target_pairs={{0,3},{1,2},{2,1},{3,0},{4,7},{5,6},{6,5},{7,4},{8,11},{9,10},{10,... | collective-permute-start | bytes 884744 | tf_op jit(solution)/shard_map/ppermute | solution.py:16
  31.8 22.9 %collective-permute-done.9.refs_8_ = bf16[192,768]{1,0:T(8,128)(2,1)S(1)} collective-permute-done((bf16[192,768]{1,0:T(8,128)(2,1)S(1)}, bf16[192,768]{1,0:T(8,128)(2,1)S(1)}, u32[]{:S(2)}, u32[]{:S(2)}) %collective-permute-start.9) | collective-permute-done | bytes 294944 | tf_op jit(solution)/shard_map/ppermute | solution.py:16
  54.7 1.5 %collective-permute-start.10 = (bf16[192,768]{1,0:T(8,128)(2,1)S(1)}, bf16[192,768]{1,0:T(8,128)(2,1)S(1)}, u32[]{:S(2)}, u32[]{:S(2)}) collective-permute-start(bf16[192,768]{1,0:T(8,128)(2,1)S(1)} %collective-permute-done.9.refs_8_), channel_id=1, source_target_pairs={{0,1},{1,0},{2,3},{3,2},{4,5},{5,4},{6,7},{7,6},{8,9},{9,8},{10,11... | collective-permute-start | bytes 884744 | tf_op jit(solution)/shard_map/ppermute | solution.py:16
  56.2 1.4 %collective-permute-start.11 = (bf16[192,768]{1,0:T(8,128)(2,1)S(1)}, bf16[192,768]{1,0:T(8,128)(2,1)S(1)}, u32[]{:S(2)}, u32[]{:S(2)}) collective-permute-start(bf16[192,768]{1,0:T(8,128)(2,1)S(1)} %collective-permute-done.9.refs_8_), channel_id=1, source_target_pairs={{0,2},{1,3},{2,0},{3,1},{4,6},{5,7},{6,4},{7,5},{8,10},{9,11},{10,... | collective-permute-start | bytes 884744 | tf_op jit(solution)/shard_map/ppermute | solution.py:16
  58.8 1.4 %collective-permute-start.3 = (bf16[192,768]{1,0:T(8,128)(2,1)S(1)}, bf16[192,768]{1,0:T(8,128)(2,1)}, u32[]{:S(2)}, u32[]{:S(2)}) collective-permute-start(bf16[192,768]{1,0:T(8,128)(2,1)S(1)} %pad_maximum_fusion.refs_0_), channel_id=1, source_target_pairs={{0,2},{1,3},{2,0},{3,1},{4,6},{5,7},{6,4},{7,5},{8,10},{9,11},{10,... | collective-permute-start | bytes 884744 | tf_op jit(solution)/shard_map/ppermute | solution.py:16
  60.2 4.5 %collective-permute-done.10.refs_9_ = bf16[192,768]{1,0:T(8,128)(2,1)S(1)} collective-permute-done((bf16[192,768]{1,0:T(8,128)(2,1)S(1)}, bf16[192,768]{1,0:T(8,128)(2,1)S(1)}, u32[]{:S(2)}, u32[]{:S(2)}) %collective-permute-start.10) | collective-permute-done | bytes 294944 | tf_op jit(solution)/shard_map/ppermute | solution.py:16
  64.7 1.5 %collective-permute-start.6 = (bf16[192,768]{1,0:T(8,128)(2,1)}, bf16[192,768]{1,0:T(8,128)(2,1)}, u32[]{:S(2)}, u32[]{:S(2)}) collective-permute-start(bf16[192,768]{1,0:T(8,128)(2,1)} %collective-permute-done.5.refs_4_), channel_id=1, source_target_pairs={{0,1},{1,0},{2,3},{3,2},{4,5},{5,4},{6,7},{7,6},{8,9},{9,8},{10,11... | collective-permute-start | bytes 884744 | tf_op jit(solution)/shard_map/ppermute | solution.py:16
  66.2 1.4 %collective-permute-start.7 = (bf16[192,768]{1,0:T(8,128)(2,1)}, bf16[192,768]{1,0:T(8,128)(2,1)}, u32[]{:S(2)}, u32[]{:S(2)}) collective-permute-start(bf16[192,768]{1,0:T(8,128)(2,1)} %collective-permute-done.5.refs_4_), channel_id=1, source_target_pairs={{0,2},{1,3},{2,0},{3,1},{4,6},{5,7},{6,4},{7,5},{8,10},{9,11},{10,... | collective-permute-start | bytes 884744 | tf_op jit(solution)/shard_map/ppermute | solution.py:16
  68.1 2.0 %collective-permute-done.15.refs_14_ = bf16[192,768]{1,0:T(8,128)(2,1)S(1)} collective-permute-done((bf16[192,768]{1,0:T(8,128)(2,1)S(1)}, bf16[192,768]{1,0:T(8,128)(2,1)S(1)}, u32[]{:S(2)}, u32[]{:S(2)}) %collective-permute-start.15) | collective-permute-done | bytes 294944 | tf_op jit(solution)/shard_map/ppermute | solution.py:16
  70.1 2.4 %collective-permute-done.16.refs_15_ = bf16[192,768]{1,0:T(8,128)(2,1)S(1)} collective-permute-done((bf16[192,768]{1,0:T(8,128)(2,1)S(1)}, bf16[192,768]{1,0:T(8,128)(2,1)S(1)}, u32[]{:S(2)}, u32[]{:S(2)}) %collective-permute-start.16) | collective-permute-done | bytes 294944 | tf_op jit(solution)/shard_map/ppermute | solution.py:16
  75.1 2.9 %collective-permute-done.3.refs_2_ = bf16[192,768]{1,0:T(8,128)(2,1)} collective-permute-done((bf16[192,768]{1,0:T(8,128)(2,1)S(1)}, bf16[192,768]{1,0:T(8,128)(2,1)}, u32[]{:S(2)}, u32[]{:S(2)}) %collective-permute-start.3) | collective-permute-done | bytes 294944 | tf_op jit(solution)/shard_map/ppermute | solution.py:16
  78.6 1.5 %collective-permute-start.13 = (bf16[96,768]{1,0:T(8,128)(2,1)}, bf16[96,768]{1,0:T(8,128)(2,1)}, u32[]{:S(2)}, u32[]{:S(2)}) collective-permute-start(bf16[96,768]{1,0:T(8,128)(2,1)} %slice.17), channel_id=1, source_target_pairs={{0,2},{1,3},{2,0},{3,1},{4,6},{5,7},{6,4},{7,5},{8,10},{9,11},{10,... | collective-permute-start | bytes 442376 | tf_op jit(solution)/shard_map/ppermute | solution.py:16
  80.1 4.0 %collective-permute-done.7.refs_6_ = bf16[192,768]{1,0:T(8,128)(2,1)} collective-permute-done((bf16[192,768]{1,0:T(8,128)(2,1)}, bf16[192,768]{1,0:T(8,128)(2,1)}, u32[]{:S(2)}, u32[]{:S(2)}) %collective-permute-start.7) | collective-permute-done | bytes 294944 | tf_op jit(solution)/shard_map/ppermute | solution.py:16
  84.7 1.5 %collective-permute-start.18 = (bf16[96,768]{1,0:T(8,128)(2,1)}, bf16[96,768]{1,0:T(8,128)(2,1)}, u32[]{:S(2)}, u32[]{:S(2)}) collective-permute-start(bf16[96,768]{1,0:T(8,128)(2,1)} %slice.19), channel_id=1, source_target_pairs={{0,2},{1,3},{2,0},{3,1},{4,6},{5,7},{6,4},{7,5},{8,10},{9,11},{10,... | collective-permute-start | bytes 442376 | tf_op jit(solution)/shard_map/ppermute | solution.py:16
  88.2 1.3 %collective-permute-done.17.refs_16_ = bf16[96,768]{1,0:T(8,128)(2,1)} collective-permute-done((bf16[96,768]{1,0:T(8,128)(2,1)}, bf16[96,768]{1,0:T(8,128)(2,1)}, u32[]{:S(2)}, u32[]{:S(2)}) %collective-permute-start.17) | collective-permute-done | bytes 147488 | tf_op jit(solution)/shard_map/ppermute | solution.py:16
  91.2 7.7 %shard_map.142.partial_ref = f32[256,768]{1,0:T(8,128)S(1)} custom-call(s32[1]{0:T(128)} %bitcast.7.me_ref, bf16[256,768]{1,0:T(8,128)(2,1)S(1)} %get-tuple-element.11.normed_ref, f32[16,128]{1,0:T(8,128)S(1)} %bitcast.17, bf16[192,768]{1,0:T(8,128)(2,1)S(1)} %pad_maximum_fusion.refs_0_, bf16[192,768]{1,0:T(8,128)(2,1)S(1)} %copy-done.3, ...), custom_call_target="tpu_custom_call" | custom-call | tf_op jit(solution)/shard_map/pallas_call | solution.py:20
  100.2 1.1 collective-permute-done.21
  101.5 1.1 shard_map.143
  102.7 2.0 %collective-permute-start.22 = (bf16[64,768]{1,0:T(8,128)(2,1)S(1)}, bf16[64,768]{1,0:T(8,128)(2,1)S(1)}, u32[]{:S(2)}, u32[]{:S(2)}) collective-permute-start(bf16[64,768]{1,0:T(8,128)(2,1)S(1)} %get-tuple-element.15), channel_id=1, source_target_pairs={{0,1},{1,0},{2,3},{3,2},{4,5},{5,4},{6,7},{7,6},{8,9},{9,8},{10,11... | collective-permute-start | bytes 294920 | tf_op jit(solution)/shard_map/ppermute | solution.py:16
  104.7 3.1 %collective-permute-done.22 = bf16[64,768]{1,0:T(8,128)(2,1)S(1)} collective-permute-done((bf16[64,768]{1,0:T(8,128)(2,1)S(1)}, bf16[64,768]{1,0:T(8,128)(2,1)S(1)}, u32[]{:S(2)}, u32[]{:S(2)}) %collective-permute-start.22) | collective-permute-done | bytes 98336 | tf_op jit(solution)/shard_map/ppermute | solution.py:16
  107.8 1.5 %collective-permute-start.23 = (bf16[64,768]{1,0:T(8,128)(2,1)S(1)}, bf16[64,768]{1,0:T(8,128)(2,1)S(1)}, u32[]{:S(2)}, u32[]{:S(2)}) collective-permute-start(bf16[64,768]{1,0:T(8,128)(2,1)S(1)} %add_convert_fusion.2), channel_id=1, source_target_pairs={{0,2},{1,3},{2,0},{3,1},{4,6},{5,7},{6,4},{7,5},{8,10},{9,11},{10,... | collective-permute-start | bytes 294920 | tf_op jit(solution)/shard_map/ppermute | solution.py:16
  109.4 3.1 %collective-permute-done.23 = bf16[64,768]{1,0:T(8,128)(2,1)S(1)} collective-permute-done((bf16[64,768]{1,0:T(8,128)(2,1)S(1)}, bf16[64,768]{1,0:T(8,128)(2,1)S(1)}, u32[]{:S(2)}, u32[]{:S(2)}) %collective-permute-start.23) | collective-permute-done | bytes 98336 | tf_op jit(solution)/shard_map/ppermute | solution.py:16
  112.6 4.6 %collective-permute-done.24 = bf16[64,768]{1,0:T(8,128)(2,1)S(1)} collective-permute-done((bf16[64,768]{1,0:T(8,128)(2,1)S(1)}, bf16[64,768]{1,0:T(8,128)(2,1)S(1)}, u32[]{:S(2)}, u32[]{:S(2)}) %collective-permute-start.24) | collective-permute-done | bytes 98336 | tf_op jit(solution)/shard_map/ppermute | solution.py:16
  118.9 4.4 %collective-permute-done.25 = bf16[64,768]{1,0:T(8,128)(2,1)S(1)} collective-permute-done((bf16[64,768]{1,0:T(8,128)(2,1)S(1)}, bf16[64,768]{1,0:T(8,128)(2,1)S(1)}, u32[]{:S(2)}, u32[]{:S(2)}) %collective-permute-start.25) | collective-permute-done | bytes 98336 | tf_op jit(solution)/shard_map/ppermute | solution.py:16
  (89 shorter events, 16.7 us)
Async XLA Ops:
  2.2 16.7 %copy-start.1 = (bf16[256,768]{1,0:T(8,128)(2,1)S(1)}, bf16[256,768]{1,0:T(8,128)(2,1)}, u32[]{:S(2)}) copy-start(bf16[256,768]{1,0:T(8,128)(2,1)} %table_ref.1) | copy-start | bytes 1179652
  3.4 15.5 %all-to-all-start = ((f32[16,1,128]{2,1,0:T(1,128)}), f32[16,1,128]{2,1,0:T(1,128)S(1)}, u32[]{:S(2)}, u32[]{:S(2)}) async-start(f32[16,1,128]{2,1,0:T(1,128)} %bitcast.3), calls=%async_computation | async-start | bytes 16384 | tf_op jit(solution)/shard_map/all_to_all | solution.py:219
  20.2 47.3 %all-to-all-start.1 = ((bf16[16,16,768]{2,1,0:T(8,128)(2,1)}), bf16[16,16,768]{2,1,0:T(8,128)(2,1)S(1)}, u32[]{:S(2)}, u32[]{:S(2)}) async-start(bf16[16,16,768]{2,1,0:T(8,128)(2,1)} %bitcast.5), calls=%async_computation.1 | async-start | bytes 786432 | tf_op jit(solution)/shard_map/all_to_all | solution.py:226
  23.8 30.9 %collective-permute-start.9 = (bf16[192,768]{1,0:T(8,128)(2,1)S(1)}, bf16[192,768]{1,0:T(8,128)(2,1)S(1)}, u32[]{:S(2)}, u32[]{:S(2)}) collective-permute-start(bf16[192,768]{1,0:T(8,128)(2,1)S(1)} %pad_maximum_fusion.refs_0_), channel_id=1, source_target_pairs={{0,8},{1,9},{2,10},{3,11},{4,12},{5,13},{6,14},{7,15},{8,0},{9,1},... | collective-permute-start | bytes 884744 | tf_op jit(solution)/shard_map/ppermute | solution.py:16
  26.6 29.6 %collective-permute-start.2 = (bf16[192,768]{1,0:T(8,128)(2,1)S(1)}, bf16[192,768]{1,0:T(8,128)(2,1)S(1)}, u32[]{:S(2)}, u32[]{:S(2)}) collective-permute-start(bf16[192,768]{1,0:T(8,128)(2,1)S(1)} %pad_maximum_fusion.refs_0_), channel_id=1, source_target_pairs={{0,1},{1,0},{2,3},{3,2},{4,5},{5,4},{6,7},{7,6},{8,9},{9,8},{10,11... | collective-permute-start | bytes 884744 | tf_op jit(solution)/shard_map/ppermute | solution.py:16
  28.1 2.9 %collective-permute-start = (bf16[128,768]{1,0:T(8,128)(2,1)S(1)}, bf16[128,768]{1,0:T(8,128)(2,1)S(1)}, u32[]{:S(2)}, u32[]{:S(2)}) collective-permute-start(bf16[128,768]{1,0:T(8,128)(2,1)S(1)} %copy-done.8), channel_id=1, source_target_pairs={{0,16},{16,0},{1,17},{17,1},{2,18},{18,2},{3,19},{19,3},{4,20},{20... | collective-permute-start | bytes 589832 | tf_op jit(solution)/shard_map/ppermute | solution.py:16
  28.1 29.5 %collective-permute-start.14 = (bf16[192,768]{1,0:T(8,128)(2,1)S(1)}, bf16[192,768]{1,0:T(8,128)(2,1)S(1)}, u32[]{:S(2)}, u32[]{:S(2)}) collective-permute-start(bf16[192,768]{1,0:T(8,128)(2,1)S(1)} %pad_maximum_fusion.refs_0_), channel_id=1, source_target_pairs={{0,12},{1,13},{2,14},{3,15},{4,8},{5,9},{6,10},{7,11},{8,4},{9,5},... | collective-permute-start | bytes 884744 | tf_op jit(solution)/shard_map/ppermute | solution.py:16
  29.5 28.6 %collective-permute-start.4 = (bf16[192,768]{1,0:T(8,128)(2,1)S(1)}, bf16[192,768]{1,0:T(8,128)(2,1)}, u32[]{:S(2)}, u32[]{:S(2)}) collective-permute-start(bf16[192,768]{1,0:T(8,128)(2,1)S(1)} %pad_maximum_fusion.refs_0_), channel_id=1, source_target_pairs={{0,3},{1,2},{2,1},{3,0},{4,7},{5,6},{6,5},{7,4},{8,11},{9,10},{10,... | collective-permute-start | bytes 884744 | tf_op jit(solution)/shard_map/ppermute | solution.py:16
  31.7 27.1 %collective-permute-start.5 = (bf16[192,768]{1,0:T(8,128)(2,1)S(1)}, bf16[192,768]{1,0:T(8,128)(2,1)}, u32[]{:S(2)}, u32[]{:S(2)}) collective-permute-start(bf16[192,768]{1,0:T(8,128)(2,1)S(1)} %pad_maximum_fusion.refs_0_), channel_id=1, source_target_pairs={{0,4},{1,5},{2,6},{3,7},{4,0},{5,1},{6,2},{7,3},{8,12},{9,13},{10,... | collective-permute-start | bytes 884744 | tf_op jit(solution)/shard_map/ppermute | solution.py:16
  54.7 9.9 %collective-permute-start.10 = (bf16[192,768]{1,0:T(8,128)(2,1)S(1)}, bf16[192,768]{1,0:T(8,128)(2,1)S(1)}, u32[]{:S(2)}, u32[]{:S(2)}) collective-permute-start(bf16[192,768]{1,0:T(8,128)(2,1)S(1)} %collective-permute-done.9.refs_8_), channel_id=1, source_target_pairs={{0,1},{1,0},{2,3},{3,2},{4,5},{5,4},{6,7},{7,6},{8,9},{9,8},{10,11... | collective-permute-start | bytes 884744 | tf_op jit(solution)/shard_map/ppermute | solution.py:16
  56.2 11.9 %copy-start.2 = (bf16[192,768]{1,0:T(8,128)(2,1)}, bf16[192,768]{1,0:T(8,128)(2,1)S(1)}, u32[]{:S(2)}) copy-start(bf16[192,768]{1,0:T(8,128)(2,1)S(1)} %collective-permute-done.2.refs_1_) | copy-start | bytes 884740
  56.2 9.9 %collective-permute-start.11 = (bf16[192,768]{1,0:T(8,128)(2,1)S(1)}, bf16[192,768]{1,0:T(8,128)(2,1)S(1)}, u32[]{:S(2)}, u32[]{:S(2)}) collective-permute-start(bf16[192,768]{1,0:T(8,128)(2,1)S(1)} %collective-permute-done.9.refs_8_), channel_id=1, source_target_pairs={{0,2},{1,3},{2,0},{3,1},{4,6},{5,7},{6,4},{7,5},{8,10},{9,11},{10,... | collective-permute-start | bytes 884744 | tf_op jit(solution)/shard_map/ppermute | solution.py:16
  57.6 12.5 %collective-permute-start.15 = (bf16[192,768]{1,0:T(8,128)(2,1)S(1)}, bf16[192,768]{1,0:T(8,128)(2,1)S(1)}, u32[]{:S(2)}, u32[]{:S(2)}) collective-permute-start(bf16[192,768]{1,0:T(8,128)(2,1)S(1)} %collective-permute-done.14.refs_13_), channel_id=1, source_target_pairs={{0,1},{1,0},{2,3},{3,2},{4,5},{5,4},{6,7},{7,6},{8,9},{9,8},{10,11... | collective-permute-start | bytes 884744 | tf_op jit(solution)/shard_map/ppermute | solution.py:16
  58.2 14.3 %collective-permute-start.16 = (bf16[192,768]{1,0:T(8,128)(2,1)S(1)}, bf16[192,768]{1,0:T(8,128)(2,1)S(1)}, u32[]{:S(2)}, u32[]{:S(2)}) collective-permute-start(bf16[192,768]{1,0:T(8,128)(2,1)S(1)} %collective-permute-done.14.refs_13_), channel_id=1, source_target_pairs={{0,2},{1,3},{2,0},{3,1},{4,6},{5,7},{6,4},{7,5},{8,10},{9,11},{10,... | collective-permute-start | bytes 884744 | tf_op jit(solution)/shard_map/ppermute | solution.py:16
  58.8 19.2 %collective-permute-start.3 = (bf16[192,768]{1,0:T(8,128)(2,1)S(1)}, bf16[192,768]{1,0:T(8,128)(2,1)}, u32[]{:S(2)}, u32[]{:S(2)}) collective-permute-start(bf16[192,768]{1,0:T(8,128)(2,1)S(1)} %pad_maximum_fusion.refs_0_), channel_id=1, source_target_pairs={{0,2},{1,3},{2,0},{3,1},{4,6},{5,7},{6,4},{7,5},{8,10},{9,11},{10,... | collective-permute-start | bytes 884744 | tf_op jit(solution)/shard_map/ppermute | solution.py:16
  64.7 13.9 %collective-permute-start.6 = (bf16[192,768]{1,0:T(8,128)(2,1)}, bf16[192,768]{1,0:T(8,128)(2,1)}, u32[]{:S(2)}, u32[]{:S(2)}) collective-permute-start(bf16[192,768]{1,0:T(8,128)(2,1)} %collective-permute-done.5.refs_4_), channel_id=1, source_target_pairs={{0,1},{1,0},{2,3},{3,2},{4,5},{5,4},{6,7},{7,6},{8,9},{9,8},{10,11... | collective-permute-start | bytes 884744 | tf_op jit(solution)/shard_map/ppermute | solution.py:16
  66.2 17.9 %collective-permute-start.7 = (bf16[192,768]{1,0:T(8,128)(2,1)}, bf16[192,768]{1,0:T(8,128)(2,1)}, u32[]{:S(2)}, u32[]{:S(2)}) collective-permute-start(bf16[192,768]{1,0:T(8,128)(2,1)} %collective-permute-done.5.refs_4_), channel_id=1, source_target_pairs={{0,2},{1,3},{2,0},{3,1},{4,6},{5,7},{6,4},{7,5},{8,10},{9,11},{10,... | collective-permute-start | bytes 884744 | tf_op jit(solution)/shard_map/ppermute | solution.py:16
  70.1 13.9 %collective-permute-start.1 = (bf16[128,768]{1,0:T(8,128)(2,1)S(1)}, bf16[128,768]{1,0:T(8,128)(2,1)S(1)}, u32[]{:S(2)}, u32[]{:S(2)}) collective-permute-start(bf16[128,768]{1,0:T(8,128)(2,1)S(1)} %shard_map.140.rows_ref), channel_id=1, source_target_pairs={{0,16},{16,0},{1,17},{17,1},{2,18},{18,2},{3,19},{19,3},{4,20},{20... | collective-permute-start | bytes 589832 | tf_op jit(solution)/shard_map/ppermute | solution.py:16
  72.5 15.0 %collective-permute-start.8 = (bf16[192,768]{1,0:T(8,128)(2,1)}, bf16[192,768]{1,0:T(8,128)(2,1)S(1)}, u32[]{:S(2)}, u32[]{:S(2)}) collective-permute-start(bf16[192,768]{1,0:T(8,128)(2,1)} %collective-permute-done.4.refs_3_), channel_id=1, source_target_pairs={{0,4},{1,5},{2,6},{3,7},{4,0},{5,1},{6,2},{7,3},{8,12},{9,13},{10,... | collective-permute-start | bytes 884744 | tf_op jit(solution)/shard_map/ppermute | solution.py:16
  74.5 11.8 %copy-start.15 = (bf16[768]{0:T(1024)(128)(2,1)S(1)}, bf16[768]{0:T(1024)(128)(2,1)}, u32[]{:S(2)}) copy-start(bf16[768]{0:T(1024)(128)(2,1)} %param.15) | copy-start | bytes 4612
  74.5 11.8 %copy-start.10 = (bf16[128,768]{1,0:T(8,128)(2,1)S(1)}, bf16[128,768]{1,0:T(8,128)(2,1)}, u32[]{:S(2)}) copy-start(bf16[128,768]{1,0:T(8,128)(2,1)} %copy-done.9) | copy-start | bytes 589828
  78.0 10.2 %collective-permute-start.12 = (bf16[96,768]{1,0:T(8,128)(2,1)}, bf16[96,768]{1,0:T(8,128)(2,1)}, u32[]{:S(2)}, u32[]{:S(2)}) collective-permute-start(bf16[96,768]{1,0:T(8,128)(2,1)} %slice.16), channel_id=1, source_target_pairs={{0,1},{1,0},{2,3},{3,2},{4,5},{5,4},{6,7},{7,6},{8,9},{9,8},{10,11... | collective-permute-start | bytes 442376 | tf_op jit(solution)/shard_map/ppermute | solution.py:16
  78.6 9.6 %collective-permute-start.13 = (bf16[96,768]{1,0:T(8,128)(2,1)}, bf16[96,768]{1,0:T(8,128)(2,1)}, u32[]{:S(2)}, u32[]{:S(2)}) collective-permute-start(bf16[96,768]{1,0:T(8,128)(2,1)} %slice.17), channel_id=1, source_target_pairs={{0,2},{1,3},{2,0},{3,1},{4,6},{5,7},{6,4},{7,5},{8,10},{9,11},{10,... | collective-permute-start | bytes 442376 | tf_op jit(solution)/shard_map/ppermute | solution.py:16
  84.1 5.5 %collective-permute-start.17 = (bf16[96,768]{1,0:T(8,128)(2,1)}, bf16[96,768]{1,0:T(8,128)(2,1)}, u32[]{:S(2)}, u32[]{:S(2)}) collective-permute-start(bf16[96,768]{1,0:T(8,128)(2,1)} %slice.18), channel_id=1, source_target_pairs={{0,1},{1,0},{2,3},{3,2},{4,5},{5,4},{6,7},{7,6},{8,9},{9,8},{10,11... | collective-permute-start | bytes 442376 | tf_op jit(solution)/shard_map/ppermute | solution.py:16
  84.7 5.5 %collective-permute-start.18 = (bf16[96,768]{1,0:T(8,128)(2,1)}, bf16[96,768]{1,0:T(8,128)(2,1)}, u32[]{:S(2)}, u32[]{:S(2)}) collective-permute-start(bf16[96,768]{1,0:T(8,128)(2,1)} %slice.19), channel_id=1, source_target_pairs={{0,2},{1,3},{2,0},{3,1},{4,6},{5,7},{6,4},{7,5},{8,10},{9,11},{10,... | collective-permute-start | bytes 442376 | tf_op jit(solution)/shard_map/ppermute | solution.py:16
  98.9 2.7 %collective-permute-start.19 = (f32[256,768]{1,0:T(8,128)S(1)}, f32[256,768]{1,0:T(8,128)S(1)}, u32[]{:S(2)}, u32[]{:S(2)}) collective-permute-start(f32[256,768]{1,0:T(8,128)S(1)} %shard_map.142.partial_ref), channel_id=1, source_target_pairs={{0,16},{16,0},{1,17},{17,1},{2,18},{18,2},{3,19},{19,3},{4,20},{20... | collective-permute-start | bytes 2359304 | tf_op jit(solution)/shard_map/ppermute | solution.py:16
  99.0 2.6 %collective-permute-start.20 = (bf16[64,768]{1,0:T(8,128)(2,1)S(1)}, bf16[64,768]{1,0:T(8,128)(2,1)S(1)}, u32[]{:S(2)}, u32[]{:S(2)}) collective-permute-start(bf16[64,768]{1,0:T(8,128)(2,1)S(1)} %copy-done.13), channel_id=1, source_target_pairs={{0,16},{16,0},{1,17},{17,1},{2,18},{18,2},{3,19},{19,3},{4,20},{20... | collective-permute-start | bytes 294920 | tf_op jit(solution)/shard_map/ppermute | solution.py:16
  99.4 1.9 %collective-permute-start.21 = (s32[128]{0:T(128)S(1)}, s32[128]{0:T(128)S(1)}, u32[]{:S(2)}, u32[]{:S(2)}) collective-permute-start(s32[128]{0:T(128)S(1)} %copy-done.17), channel_id=1, source_target_pairs={{0,16},{16,0},{1,17},{17,1},{2,18},{18,2},{3,19},{19,3},{4,20},{20... | collective-permute-start | bytes 1544 | tf_op jit(solution)/shard_map/ppermute | solution.py:16
  102.7 5.1 %collective-permute-start.22 = (bf16[64,768]{1,0:T(8,128)(2,1)S(1)}, bf16[64,768]{1,0:T(8,128)(2,1)S(1)}, u32[]{:S(2)}, u32[]{:S(2)}) collective-permute-start(bf16[64,768]{1,0:T(8,128)(2,1)S(1)} %get-tuple-element.15), channel_id=1, source_target_pairs={{0,1},{1,0},{2,3},{3,2},{4,5},{5,4},{6,7},{7,6},{8,9},{9,8},{10,11... | collective-permute-start | bytes 294920 | tf_op jit(solution)/shard_map/ppermute | solution.py:16
  107.8 4.7 %collective-permute-start.23 = (bf16[64,768]{1,0:T(8,128)(2,1)S(1)}, bf16[64,768]{1,0:T(8,128)(2,1)S(1)}, u32[]{:S(2)}, u32[]{:S(2)}) collective-permute-start(bf16[64,768]{1,0:T(8,128)(2,1)S(1)} %add_convert_fusion.2), channel_id=1, source_target_pairs={{0,2},{1,3},{2,0},{3,1},{4,6},{5,7},{6,4},{7,5},{8,10},{9,11},{10,... | collective-permute-start | bytes 294920 | tf_op jit(solution)/shard_map/ppermute | solution.py:16
  112.5 4.7 %collective-permute-start.24 = (bf16[64,768]{1,0:T(8,128)(2,1)S(1)}, bf16[64,768]{1,0:T(8,128)(2,1)S(1)}, u32[]{:S(2)}, u32[]{:S(2)}) collective-permute-start(bf16[64,768]{1,0:T(8,128)(2,1)S(1)} %add_convert_fusion.1), channel_id=1, source_target_pairs={{0,4},{1,5},{2,6},{3,7},{4,0},{5,1},{6,2},{7,3},{8,12},{9,13},{10,... | collective-permute-start | bytes 294920 | tf_op jit(solution)/shard_map/ppermute | solution.py:16
  117.3 6.1 %collective-permute-start.25 = (bf16[64,768]{1,0:T(8,128)(2,1)S(1)}, bf16[64,768]{1,0:T(8,128)(2,1)S(1)}, u32[]{:S(2)}, u32[]{:S(2)}) collective-permute-start(bf16[64,768]{1,0:T(8,128)(2,1)S(1)} %add_convert_fusion), channel_id=1, source_target_pairs={{0,8},{1,9},{2,10},{3,11},{4,12},{5,13},{6,14},{7,15},{8,0},{9,1},... | collective-permute-start | bytes 294920 | tf_op jit(solution)/shard_map/ppermute | solution.py:16
  (14 other events, 54.3 us)

commit v2 on v0

v2 whole, which is shorter than its diff:
```python
import functools

import jax
import jax.numpy as jnp
from jax import lax
from jax.experimental import pallas as pl
from jax.experimental.pallas import tpu as pltpu
from jax.sharding import PartitionSpec as P

F32 = jnp.float32
BF16 = jnp.bfloat16
DIGIT = 256
TILE_ROWS = 16
SMALL_VMEM = 6 * 1024 * 1024
LARGE_VMEM = 14 * 1024 * 1024


def flipped(block, axis, mask):
    return lax.ppermute(block, axis, [(i, i ^ mask) for i in range(lax.axis_size(axis))])


def moved(block, *moves):
    cycle, groups = lax.axis_size("dp"), lax.axis_size("mp")
    route = [
        ((d ^ to ^ source) * groups + (i ^ mask), d * groups + i)
        for to, source, mask in moves
        for d in range(to, cycle, 2)
        for i in range(groups)
    ]
    return lax.ppermute(block, ("dp", "mp"), route)


def after(value, *others):
    return lax.optimization_barrier((value, *others))[0]


def kernel_call(body, out_shape, *args, in_place=(), scratch=(), vmem=SMALL_VMEM):
    return pl.pallas_call(
        body,
        out_shape=out_shape,
        in_specs=[
            pl.BlockSpec(memory_space=pltpu.HBM if i in in_place else pltpu.VMEM) for i in range(len(args))
        ],
        out_specs=jax.tree.map(lambda _: pl.BlockSpec(memory_space=pltpu.VMEM), out_shape),
        scratch_shapes=scratch,
        compiler_params=pltpu.CompilerParams(vmem_limit_bytes=vmem),
    )(*args)


def iota(shape, dimension):
    return lax.broadcasted_iota(jnp.int32, shape, dimension)


def slots_of(owner, groups):
    chains = owner.shape[1]
    marks = (owner == iota((groups, chains), 0)).astype(F32)
    before = (iota((chains, chains), 0) < iota((chains, chains), 1)).astype(BF16)
    counts = jnp.dot(marks.astype(BF16), before, preferred_element_type=F32)
    return marks, jnp.sum(counts * marks, axis=0, keepdims=True)


def request_body(capacity, owner_ref, row_ref, bias_ref, message_ref):
    groups, _, width = message_ref.shape
    bias_count = bias_ref.shape[1]
    marks, rank = slots_of(owner_ref[...], groups)
    ranked = (rank.astype(jnp.int32) == iota((capacity, rank.shape[1]), 0)).astype(F32) * row_ref[...].astype(F32)
    request = lax.dot_general(
        marks.astype(BF16), ranked.astype(BF16), (((1,), (1,)), ((), ())), preferred_element_type=F32
    )
    bias = jnp.broadcast_to(bias_ref[...].astype(F32), (groups, bias_count))
    rest = jnp.zeros((groups, width - bias_count - capacity), F32)
    message_ref[...] = jnp.concatenate([bias, request, rest], axis=1).reshape(message_ref.shape)


def serve_body(capacity, bias_count, message_ref, table_ref, rows_ref):
    groups = message_ref.shape[0]
    slots, held = groups * capacity, table_ref.shape[0]
    message = message_ref[...].reshape(groups, message_ref.shape[2])
    wanted = message[:, bias_count : bias_count + capacity].astype(BF16)
    spread = (iota((slots, groups), 0) // capacity == iota((slots, groups), 1)).astype(BF16)
    by_rank = jnp.dot(spread, wanted, preferred_element_type=F32)
    mine = (iota((slots, capacity), 0) % capacity == iota((slots, capacity), 1)).astype(F32)
    row = jnp.sum(by_rank * mine, axis=1, keepdims=True).astype(jnp.int32)
    pick = (row == iota((slots, held), 1)).astype(BF16)
    rows_ref[...] = jnp.dot(pick, table_ref[...], preferred_element_type=F32).astype(BF16)


def pack_body(capacity, groups, owner_ref, positive_ref, gain_ref, bias_ref, queries_ref, packed_ref):
    chains, features = queries_ref.shape
    owner, positive = owner_ref[...], positive_ref[...]
    _, rank = slots_of(owner, groups)
    slot = owner * capacity + rank.astype(jnp.int32)
    small = jnp.concatenate([slot, positive // DIGIT, positive % DIGIT], axis=0).astype(F32)
    small = jnp.concatenate([small, jnp.zeros((3, features - chains), F32)], axis=1)
    wide = jnp.concatenate([gain_ref[...], bias_ref[...]], axis=0).astype(F32)
    rest = jnp.zeros((TILE_ROWS - 5, features), F32)
    packed_ref[:chains, :] = queries_ref[...]
    packed_ref[chains:, :] = jnp.concatenate([small, wide, rest], axis=0).astype(BF16)


def select_body(packed_ref, fetched_ref, shifted_ref, normed_ref, positive_ref):
    slots = fetched_ref.shape[0]
    chains = shifted_ref.shape[0]
    extra = packed_ref[chains:, :].astype(F32)
    digits = extra[:3, :chains].astype(jnp.int32)
    positive_ref[...] = digits[1:2, :] * DIGIT + digits[2:3, :]
    pick = (digits[0:1, :] == iota((slots, chains), 0)).astype(F32).T.astype(BF16)
    rows = jnp.dot(pick, fetched_ref[...], preferred_element_type=F32)
    combined = packed_ref[:chains, :].astype(F32) + rows
    centred = combined - jnp.mean(combined, axis=1, keepdims=True)
    spread = jnp.mean(centred * centred, axis=1, keepdims=True)
    normed_ref[...] = (centred * lax.rsqrt(spread + 1e-05) * extra[3:4, :]).astype(BF16)
    shifted_ref[...] = combined + extra[4:5, :]


def gelu(u):
    return 0.5 * u * (1.0 + jnp.tanh(0.7978845608028654 * (u + 0.044715 * (u * u * u))))


def hidden_body(plan, normed_ref, normed2_ref, message_ref, *refs):
    shards, (total_ref, total2_ref, held, sems) = refs[:-4], refs[-4:]
    chains, units = total_ref.shape[0], held.shape[1] // 2
    me, first_core = lax.axis_index("mp"), lax.axis_index("dp") % 2 == 0

    def copy(at, p):
        return pltpu.make_async_copy(shards[at], held.at[p], sems.at[p])

    for p, (_, at, _, other_at) in enumerate(plan):
        if at == other_at:
            copy(at, p).start()
        else:
            pl.when(first_core)(copy(at, p).start)
            pl.when(jnp.logical_not(first_core))(copy(other_at, p).start)
    normed = jnp.concatenate([normed_ref[...], normed2_ref[...]], axis=0)
    total = None
    for p, (mask, at, other_mask, _) in enumerate(plan):
        copy(at, p).wait()
        preact = lax.dot_general(
            normed, held[p, :units, :], (((1,), (1,)), ((), ())), preferred_element_type=F32
        )
        bias = message_ref[pl.ds(me ^ jnp.where(first_core, mask, other_mask), 1)]
        activated = gelu(preact + bias.reshape(1, bias.shape[2])[:, :units]).astype(BF16)
        term = jnp.dot(activated, held[p, units:, :], preferred_element_type=F32)
        total = term if total is None else total + term
    total_ref[...] = total[:chains, :]
    total2_ref[...] = total[chains:, :]


def add_body(total_ref, received_ref, sum_ref):
    sum_ref[...] = (total_ref[...] + received_ref[...]).astype(sum_ref.dtype)


def score_body(
    blocks,
    shifted_ref,
    total_ref,
    received_ref,
    other_ref,
    positive_ref,
    *refs,
):
    tools = [ref[...] for ref in refs[:blocks]]
    updated_ref, loss_ref, weights_ref, *grad_refs = refs[blocks:]
    block_rows = tools[0].shape[0]
    branch = total_ref[...] + received_ref[...] + other_ref[...].astype(F32)
    updated = (shifted_ref[...] + branch).astype(BF16)
    updated_ref[...] = updated
    scores = jnp.concatenate(
        [
            lax.dot_general(updated, t, (((1,), (1,)), ((), ())), preferred_element_type=F32)
            for t in tools
        ],
        axis=1,
    )
    tool = iota((scores.shape[1], scores.shape[0]), 0)
    column = ((tool // block_rows) ^ lax.axis_index("dp")) * block_rows + tool % block_rows
    is_positive = (column == positive_ref[...]).astype(F32).T
    row_max = jnp.max(scores, axis=1, keepdims=True)
    log_total = row_max + jnp.log(jnp.sum(jnp.exp(scores - row_max), axis=1, keepdims=True))
    loss_ref[...] = log_total - jnp.sum(scores * is_positive, axis=1, keepdims=True)
    weights = (jnp.exp(scores - log_total) - is_positive).astype(BF16)
    weights_ref[...] = weights
    for block, grad_ref in enumerate(grad_refs):
        grad_ref[...] = lax.dot_general(
            weights[:, block * block_rows : (block + 1) * block_rows],
            updated,
            (((0,), (0,)), ((), ())),
            preferred_element_type=F32,
        ).astype(BF16)


def query_grad_body(weights_ref, *refs):
    tool_refs, grad_ref = refs[:-1], refs[-1]
    block_rows = tool_refs[0].shape[0]
    grad_ref[...] = sum(
        jnp.dot(
            weights_ref[:, j * block_rows : (j + 1) * block_rows], ref[...], preferred_element_type=F32
        )
        for j, ref in enumerate(tool_refs)
    )


def weight_pieces(own, own_later, groups, hold):
    near = moved(own, (0, 0, 1), (1, 1, 8))
    near_y = moved(own_later, (0, 0, 2))
    near_both = moved(own_later, (0, 0, 3))
    near, near_y, near_both = hold(near, near_y, near_both)
    far_x, far_y, far_both = (moved(near, (1, 1, mask)) for mask in (1, 2, 3))
    pieces = [(0, own, 8, near), (1, near, 9, far_x), (2, near_y, 10, far_y), (3, near_both, 11, far_both)]
    for level in range(16, groups, 16):
        base = moved(own, (0, 0, level), (1, 1, level ^ 8))
        by_x, by_y = (moved(base, (0, 0, bit), (1, 1, bit)) for bit in (1, 2))
        both = moved(by_x, (0, 0, 2), (1, 1, 2))
        pieces += [(level ^ m, s, level ^ 8 ^ m, s) for m, s in enumerate((base, by_x, by_y, both))]
    return pieces


def local(
    queries,
    first_owner,
    first_row,
    tool_table,
    norm_gain,
    weight_in,
    bias_in,
    weight_out,
    bias_out,
    tool_embeds,
    positive,
):
    chains, features = queries.shape
    groups, cycle = lax.axis_size("mp"), lax.axis_size("dp")
    capacity = 2 * chains // groups
    slots = groups * capacity
    units = weight_in.shape[0]
    block_rows = tool_embeds.shape[0]
    tool_count = block_rows * cycle

    def whole(shape, dtype):
        return jax.ShapeDtypeStruct(shape, dtype)

    owner_row = first_owner.reshape(1, chains)
    width = -(-(units + capacity) // 128) * 128
    message = kernel_call(
        functools.partial(request_body, capacity),
        whole((groups, 1, width), F32),
        owner_row,
        first_row.reshape(1, chains),
        bias_in.reshape(1, units),
    )
    asked = lax.all_to_all(message, "mp", split_axis=0, concat_axis=0, tiled=True)
    packed = kernel_call(
        functools.partial(pack_body, capacity, groups),
        whole((chains + TILE_ROWS, features), BF16),
        after(owner_row, message),
        positive.reshape(1, chains),
        norm_gain.reshape(1, features),
        bias_out.reshape(1, features),
        queries,
    )
    served = kernel_call(
        functools.partial(serve_body, capacity, units),
        whole((slots, features), BF16),
        after(asked, packed),
        tool_table,
    )
    own = jnp.concatenate([weight_in, weight_out], axis=0)
    own_later = after(own, message)
    held = []

    def hold(*early):
        early_and_served = lax.optimization_barrier((*early, served))
        held.append(early_and_served[-1])
        return early_and_served[:-1]

    pieces = weight_pieces(own, own_later, groups, hold)
    fetched = lax.all_to_all(held[0], "mp", split_axis=0, concat_axis=0, tiled=True)
    shards = []
    for piece in pieces:
        for shard in (piece[1], piece[3]):
            if all(shard is not s for s in shards):
                shards.append(shard)
    index_of = {id(s): i for i, s in enumerate(shards)}
    plan = tuple((mask, index_of[id(s)], other, index_of[id(t)]) for mask, s, other, t in pieces)

    shifted, normed, positive_row = kernel_call(
        select_body,
        (whole((chains, features), F32), whole((chains, features), BF16), whole((1, chains), jnp.int32)),
        packed,
        fetched,
    )

    def hidden(own_rows):
        return kernel_call(
            functools.partial(hidden_body, plan),
            (whole((chains, features), F32),) * 2,
            own_rows,
            flipped(own_rows, "dp", 1),
            asked,
            *shards,
            in_place=range(3, 3 + len(shards)),
            scratch=(pltpu.VMEM((len(plan), 2 * units, features), BF16), pltpu.SemaphoreType.DMA((len(plan),))),
            vmem=LARGE_VMEM,
        )

    total, total_for = hidden(normed)
    neighbour, neighbour_for = hidden(after(flipped(normed, "mp", 4), total))
    neighbour_sum = kernel_call(
        add_body, whole((chains, features), BF16), neighbour, flipped(neighbour_for, "dp", 1)
    )
    late_tools = after(tool_embeds, total)
    tools = [tool_embeds] + [flipped(late_tools, "dp", j) for j in range(1, cycle)]
    updated, loss, weights, *grads = kernel_call(
        functools.partial(score_body, cycle),
        (
            whole((chains, features), BF16),
            whole((chains, 1), F32),
            whole((chains, tool_count), BF16),
            *(whole((block_rows, features), BF16) for _ in range(cycle)),
        ),
        shifted,
        total,
        flipped(total_for, "dp", 1),
        flipped(neighbour_sum, "mp", 4),
        positive_row,
        *tools,
    )
    query_grad = kernel_call(query_grad_body, whole((chains, features), F32), weights, *tools)

    grad = grads[0].astype(F32)
    for block in range(1, cycle):
        grad = grad + flipped(grads[block], "dp", block).astype(F32)
    bits = [1 << b for b in range((groups - 1).bit_length())]
    turned = bits[len(bits) // 2 :] + bits[: len(bits) // 2]
    for bit, other_bit in zip(bits, turned):
        rounded = grad.astype(BF16)
        grad = rounded.astype(F32) + moved(rounded, (0, 0, bit), (1, 1, other_bit)).astype(F32)
    grad_scale = (tool_count / (chains * groups * cycle)) ** 0.5
    return updated, loss[:, 0], query_grad, grad * grad_scale


def solution(mesh):
    in_specs = (
        P(("dp", "mp"), None),
        P(("dp", "mp"), None),
        P(("dp", "mp")),
        P("mp", None),
        P(),
        P("mp", None),
        P("mp"),
        P("mp", None),
        P(),
        P("dp", None),
        P(("dp", "mp")),
    )
    out_specs = (P(("dp", "mp"), None), P(("dp", "mp")), P(("dp", "mp"), None), P("dp", None))
    return jax.shard_map(local, mesh=mesh, in_specs=in_specs, out_specs=out_specs, check_vma=False)
```

time: 302 us -> 90.7 us (0.30)
  waiting for transfers between devices: 206 us -> 40.9 us
  blocking collectives: 59.1 us -> 0 us
  starting transfers between devices: 3.94 us -> 32.9 us
  between operations: 14.7 us -> 0.9 us
  Pallas kernels: 0 us -> 11.3 us
  matrix products: 8.45 us -> 0 us
  other arithmetic: 6.05 us -> 1.43 us
    psum x1 -> x0, waiting for transfers between devices: 105 us -> none  [local(): tool_grad = lax.psum(partial_grad, 'mp') * grad_scale]
    all_gather x2 -> x0, waiting for transfers between devices: 98.2 us -> none  [the longest x1 82.1 us: local(): lax.all_gather(weight_out, 'mp', axis=0, tiled=True)]
    unnamed x1 -> x0, blocking collectives: 43.7 us -> none
    ppermute x2 -> x18, waiting for transfers between devices: 1.29 us -> 27.6 us  [the longest x10 14.6 us: moved(): return lax.ppermute(block, ('dp', 'mp'), route)]
    ppermute x2 -> x18, starting transfers between devices: 0.14 us -> 21.7 us  [the longest x10 16 us: moved(): return lax.ppermute(block, ('dp', 'mp'), route)]
    all_to_all x1 -> x0, blocking collectives: 15.4 us -> none  [local(): lax.all_to_all(request, 'mp', split_axis=0, concat_axis=0, tiled=True)]
    all_to_all x1 -> x2, waiting for transfers between devices: 0.01 us -> 13.3 us  [the longest x1 6.87 us: local(): lax.all_to_all(held[0], 'mp', split_axis=0, concat_axis=0, tiled=True)]
    pallas_call x0 -> x9, Pallas kernels: none -> 11.3 us  [kernel_call(): pl.pallas_call(body, out_shape=out_shape, in_specs=[pl.BlockSpec(memory_s...]
  transfers between devices with their start and end apart: 6 -> 20, of which waited for: 4 -> 13; matrix products, arithmetic and copies ran while one was open for 3% -> 1% of each run, Pallas kernels for 0% -> 8%
where the time goes in v2:
time: 90.7 us; the launch traced here: 90.2 us
  waiting for transfers between devices  40.9 us (45%)
  starting transfers between devices  32.9 us (36%)
  Pallas kernels  11.3 us (12%)
  local copies, waits for them, and re-layouts  2.75 us (3%)
  other arithmetic  1.43 us (2%)
    ppermute x10, starting transfers between devices, moved(): return lax.ppermute(block, ('dp', 'mp'), route)  16 us
    ppermute x10, waiting for transfers between devices, moved(): return lax.ppermute(block, ('dp', 'mp'), route)  14.6 us
    ppermute x8, waiting for transfers between devices, flipped(): lax.ppermute(block, axis, [(i, i ^ mask) for i in range(lax.axis_size(axi...  13 us
    pallas_call x9, Pallas kernels, kernel_call(): pl.pallas_call(body, out_shape=out_shape, in_specs=[pl.BlockSpec(memory_s...  11.3 us
    all_to_all x1, starting transfers between devices, local(): lax.all_to_all(message, 'mp', split_axis=0, concat_axis=0, tiled=True)  6.94 us
    all_to_all x1, waiting for transfers between devices, local(): lax.all_to_all(held[0], 'mp', split_axis=0, concat_axis=0, tiled=True)  6.87 us
    all_to_all x1, waiting for transfers between devices, local(): lax.all_to_all(message, 'mp', split_axis=0, concat_axis=0, tiled=True)  6.42 us
    ppermute x8, starting transfers between devices, flipped(): lax.ppermute(block, axis, [(i, i ^ mask) for i in range(lax.axis_size(axi...  5.72 us
  transfers between devices with their start and end apart: 20, of which 13 were waited for; matrix products, arithmetic and copies ran while one was open for 1% of the time, Pallas kernels for 8%

profile of v2, /device:TPU:0, one launch (start us, length us, event | category | flops | bytes accessed | tf_op | source)
XLA Modules:
  0.0 90.2 jit_solution(2278531906106008204)
XLA Ops:
  0.6 1.0 %constant_dynamic-update-slice_fusion.1 = bf16[384,768]{1,0:T(8,128)(2,1)S(1)} fusion(bf16[192,768]{1,0:T(8,128)(2,1)} %param.16), kind=kLoop, calls=%fused_computation.6 | loop fusion | bytes 589824
  1.8 3.0 %collective-permute-start = (bf16[384,768]{1,0:T(8,128)(2,1)S(1)}, bf16[384,768]{1,0:T(8,128)(2,1)S(1)}, u32[]{:S(2)}, u32[]{:S(2)}) collective-permute-start(bf16[384,768]{1,0:T(8,128)(2,1)S(1)} %constant_dynamic-update-slice_fusion.refs_0_), channel_id=1, source_target_pairs={{1,0},{0,1},{3,2},{2,3},{5,4},{4,5},{7,6},{6,7},{9,8},{8,9},{11,10... | collective-permute-start | bytes 1769480 | tf_op jit(solution)/shard_map/ppermute | solution.py:30
  4.8 0.9 %shard_map.138 = f32[16,1,256]{2,1,0:T(1,128)} custom-call(s32[1,128]{1,0:T(1,128)S(1)} %bitcast.5, s32[1,128]{1,0:T(1,128)S(1)} %bitcast.8, bf16[1,192]{1,0:T(2,128)(2,1)S(1)} %reshape.30.bias_ref), custom_call_target="tpu_custom_call" | custom-call | tf_op jit(solution)/shard_map/pallas_call | solution.py:38
  5.8 3.4 %collective-permute-start.1 = (bf16[384,768]{1,0:T(8,128)(2,1)S(1)}, bf16[384,768]{1,0:T(8,128)(2,1)S(1)}, u32[]{:S(2)}, u32[]{:S(2)}) collective-permute-start(bf16[384,768]{1,0:T(8,128)(2,1)S(1)} %constant_dynamic-update-slice_fusion.refs_0_), channel_id=1, source_target_pairs={{2,0},{3,1},{0,2},{1,3},{6,4},{7,5},{4,6},{5,7},{10,8},{11,9},{8,1... | collective-permute-start | bytes 1769480 | tf_op jit(solution)/shard_map/ppermute | solution.py:30
  9.2 2.3 %collective-permute-start.2 = (bf16[384,768]{1,0:T(8,128)(2,1)S(1)}, bf16[384,768]{1,0:T(8,128)(2,1)S(1)}, u32[]{:S(2)}, u32[]{:S(2)}) collective-permute-start(bf16[384,768]{1,0:T(8,128)(2,1)S(1)} %constant_dynamic-update-slice_fusion.refs_0_), channel_id=1, source_target_pairs={{3,0},{2,1},{1,2},{0,3},{7,4},{6,5},{5,6},{4,7},{11,8},{10,9},{9,1... | collective-permute-start | bytes 1769480 | tf_op jit(solution)/shard_map/ppermute | solution.py:30
  11.5 6.9 %all-to-all-start = ((f32[16,1,256]{2,1,0:T(1,128)}), f32[16,1,256]{2,1,0:T(1,128)S(1)}, u32[]{:S(2)}, u32[]{:S(2)}) async-start(f32[16,1,256]{2,1,0:T(1,128)} %shard_map.138), calls=%async_computation | async-start | bytes 32768 | tf_op jit(solution)/shard_map/all_to_all | solution.py:251
  19.4 6.4 %all-to-all-done.message_ref = f32[16,1,256]{2,1,0:T(1,128)S(1)} async-done(((f32[16,1,256]{2,1,0:T(1,128)}), f32[16,1,256]{2,1,0:T(1,128)S(1)}, u32[]{:S(2)}, u32[]{:S(2)}) %all-to-all-start) | async-done | bytes 16416 | tf_op jit(solution)/shard_map/all_to_all | solution.py:251
  25.8 1.3 %shard_map.140 = bf16[256,768]{1,0:T(8,128)(2,1)} custom-call(f32[16,1,256]{2,1,0:T(1,128)S(1)} %all-to-all-done.message_ref, bf16[256,768]{1,0:T(8,128)(2,1)S(1)} %copy-done.3), custom_call_target="tpu_custom_call" | custom-call | tf_op jit(solution)/shard_map/pallas_call | solution.py:38
  27.1 4.3 %all-to-all-start.1 = ((bf16[16,16,768]{2,1,0:T(8,128)(2,1)}), bf16[16,16,768]{2,1,0:T(8,128)(2,1)}, u32[]{:S(2)}, u32[]{:S(2)}) async-start(bf16[16,16,768]{2,1,0:T(8,128)(2,1)} %bitcast.3), calls=%async_computation.1 | async-start | bytes 786432 | tf_op jit(solution)/shard_map/all_to_all | solution.py:277
  32.8 1.5 %collective-permute-start.6 = (bf16[384,768]{1,0:T(8,128)(2,1)S(1)}, bf16[384,768]{1,0:T(8,128)(2,1)}, u32[]{:S(2)}, u32[]{:S(2)}) collective-permute-start(bf16[384,768]{1,0:T(8,128)(2,1)S(1)} %collective-permute-done.refs_1_), channel_id=1, source_target_pairs={{19,16},{18,17},{17,18},{16,19},{23,20},{22,21},{21,22},{20,23},{2... | collective-permute-start | bytes 1769480 | tf_op jit(solution)/shard_map/ppermute | solution.py:30
  34.3 6.9 %all-to-all-done.1 = bf16[16,16,768]{2,1,0:T(8,128)(2,1)} async-done(((bf16[16,16,768]{2,1,0:T(8,128)(2,1)}), bf16[16,16,768]{2,1,0:T(8,128)(2,1)}, u32[]{:S(2)}, u32[]{:S(2)}) %all-to-all-start.1) | async-done | bytes 393248 | tf_op jit(solution)/shard_map/all_to_all | solution.py:277
  41.1 0.9 %copy-done.1 = bf16[144,768]{1,0:T(8,128)(2,1)S(1)} copy-done((bf16[144,768]{1,0:T(8,128)(2,1)S(1)}, bf16[144,768]{1,0:T(8,128)(2,1)}, u32[]{:S(2)}) %copy-start.1) | copy-done | bytes 221208
  42.1 1.4 %shard_map.141 = (f32[128,768]{1,0:T(8,128)S(1)}, bf16[128,768]{1,0:T(8,128)(2,1)S(1)}, s32[1,128]{1,0:T(1,128)S(1)}) custom-call(bf16[144,768]{1,0:T(8,128)(2,1)S(1)} %copy-done.1, bf16[256,768]{1,0:T(8,128)(2,1)} %bitcast.4.fetched_ref), custom_call_target="tpu_custom_call" | custom-call | tf_op jit(solution)/shard_map/pallas_call | solution.py:38
  43.6 1.2 %collective-permute-start.8 = (bf16[128,768]{1,0:T(8,128)(2,1)S(1)}, bf16[128,768]{1,0:T(8,128)(2,1)S(1)}, u32[]{:S(2)}, u32[]{:S(2)}) collective-permute-start(bf16[128,768]{1,0:T(8,128)(2,1)S(1)} %get-tuple-element.30.normed_ref), channel_id=1, source_target_pairs={{0,4},{1,5},{2,6},{3,7},{4,0},{5,1},{6,2},{7,3},{8,12},{9,13},{10,... | collective-permute-start | bytes 589832 | tf_op jit(solution)/shard_map/ppermute | solution.py:19
  45.0 2.6 %shard_map.142 = (f32[128,768]{1,0:T(8,128)S(1)}, f32[128,768]{1,0:T(8,128)S(1)}) custom-call(bf16[128,768]{1,0:T(8,128)(2,1)S(1)} %get-tuple-element.30.normed_ref, bf16[128,768]{1,0:T(8,128)(2,1)S(1)} %collective-permute-done.3.normed2_ref, f32[16,1,256]{2,1,0:T(1,128)S(1)} %all-to-all-done.message_ref, ...), custom_call_target="tpu_custom_call" | custom-call | tf_op jit(solution)/shard_map/pallas_call | solution.py:38
  47.7 3.2 %collective-permute-done.8.normed_ref = bf16[128,768]{1,0:T(8,128)(2,1)S(1)} collective-permute-done((bf16[128,768]{1,0:T(8,128)(2,1)S(1)}, bf16[128,768]{1,0:T(8,128)(2,1)S(1)}, u32[]{:S(2)}, u32[]{:S(2)}) %collective-permute-start.8) | collective-permute-done | bytes 196640 | tf_op jit(solution)/shard_map/ppermute | solution.py:19
  50.9 2.7 %collective-permute-start.9 = (bf16[128,768]{1,0:T(8,128)(2,1)S(1)}, bf16[128,768]{1,0:T(8,128)(2,1)S(1)}, u32[]{:S(2)}, u32[]{:S(2)}) collective-permute-start(bf16[128,768]{1,0:T(8,128)(2,1)S(1)} %collective-permute-done.8.normed_ref), channel_id=1, source_target_pairs={{0,16},{16,0},{1,17},{17,1},{2,18},{18,2},{3,19},{19,3},{4,20},{20... | collective-permute-start | bytes 589832 | tf_op jit(solution)/shard_map/ppermute | solution.py:19
  53.6 1.1 %collective-permute-done.9.normed2_ref = bf16[128,768]{1,0:T(8,128)(2,1)S(1)} collective-permute-done((bf16[128,768]{1,0:T(8,128)(2,1)S(1)}, bf16[128,768]{1,0:T(8,128)(2,1)S(1)}, u32[]{:S(2)}, u32[]{:S(2)}) %collective-permute-start.9) | collective-permute-done | bytes 196640 | tf_op jit(solution)/shard_map/ppermute | solution.py:19
  54.7 2.6 %shard_map.143 = (f32[128,768]{1,0:T(8,128)S(1)}, f32[128,768]{1,0:T(8,128)S(1)}) custom-call(bf16[128,768]{1,0:T(8,128)(2,1)S(1)} %collective-permute-done.8.normed_ref, bf16[128,768]{1,0:T(8,128)(2,1)S(1)} %collective-permute-done.9.normed2_ref, f32[16,1,256]{2,1,0:T(1,128)S(1)} %all-to-all-done.message_ref, ...), custom_call_target="tpu_custom_call" | custom-call | tf_op jit(solution)/shard_map/pallas_call | solution.py:38
  57.9 1.2 %collective-permute-done.10.received_ref = f32[128,768]{1,0:T(8,128)S(1)} collective-permute-done((f32[128,768]{1,0:T(8,128)S(1)}, f32[128,768]{1,0:T(8,128)S(1)}, u32[]{:S(2)}, u32[]{:S(2)}) %collective-permute-start.10) | collective-permute-done | bytes 393248 | tf_op jit(solution)/shard_map/ppermute | solution.py:19
  59.2 1.2 %collective-permute-start.11 = (bf16[128,768]{1,0:T(8,128)(2,1)S(1)}, bf16[128,768]{1,0:T(8,128)(2,1)S(1)}, u32[]{:S(2)}, u32[]{:S(2)}) collective-permute-start(bf16[128,768]{1,0:T(8,128)(2,1)S(1)} %shard_map.144), channel_id=1, source_target_pairs={{0,4},{1,5},{2,6},{3,7},{4,0},{5,1},{6,2},{7,3},{8,12},{9,13},{10,... | collective-permute-start | bytes 589832 | tf_op jit(solution)/shard_map/ppermute | solution.py:19
  60.4 1.3 %collective-permute-done.12.refs_1_ = bf16[64,768]{1,0:T(8,128)(2,1)S(1)} collective-permute-done((bf16[64,768]{1,0:T(8,128)(2,1)S(1)}, bf16[64,768]{1,0:T(8,128)(2,1)S(1)}, u32[]{:S(2)}, u32[]{:S(2)}) %collective-permute-start.12) | collective-permute-done | bytes 98336 | tf_op jit(solution)/shard_map/ppermute | solution.py:19
  61.7 4.6 %collective-permute-done.11.other_ref = bf16[128,768]{1,0:T(8,128)(2,1)S(1)} collective-permute-done((bf16[128,768]{1,0:T(8,128)(2,1)S(1)}, bf16[128,768]{1,0:T(8,128)(2,1)S(1)}, u32[]{:S(2)}, u32[]{:S(2)}) %collective-permute-start.11) | collective-permute-done | bytes 196640 | tf_op jit(solution)/shard_map/ppermute | solution.py:19
  66.3 1.1 %shard_map.145 = (bf16[128,768]{1,0:T(8,128)(2,1)}, f32[128,1]{1,0:T(8,128)S(1)}, bf16[128,128]{1,0:T(8,128)(2,1)S(1)}, bf16[64,768]{1,0:T(8,128)(2,1)S(1)}, bf16[64,768]{1,0:T(8,128)(2,1)S(1)}) custom-call(f32[128,768]{1,0:T(8,128)S(1)} %get-tuple-element.29.shifted_ref, f32[128,768]{1,0:T(8,128)S(1)} %get-tuple-element.34.total_ref, ...), custom_call_target="tpu_custom_call" | custom-call | tf_op jit(solution)/shard_map/pallas_call | solution.py:38
  67.4 1.3 %collective-permute-done.13 = bf16[64,768]{1,0:T(8,128)(2,1)S(1)} collective-permute-done((bf16[64,768]{1,0:T(8,128)(2,1)S(1)}, bf16[64,768]{1,0:T(8,128)(2,1)S(1)}, u32[]{:S(2)}, u32[]{:S(2)}) %collective-permute-start.13) | collective-permute-done | bytes 98336 | tf_op jit(solution)/shard_map/ppermute | solution.py:19
  69.6 3.8 %collective-permute-done.14 = bf16[64,768]{1,0:T(8,128)(2,1)S(1)} collective-permute-done((bf16[64,768]{1,0:T(8,128)(2,1)S(1)}, bf16[64,768]{1,0:T(8,128)(2,1)S(1)}, u32[]{:S(2)}, u32[]{:S(2)}) %collective-permute-start.14) | collective-permute-done | bytes 98336 | tf_op jit(solution)/shard_map/ppermute | solution.py:30
  74.3 3.8 %collective-permute-done.15 = bf16[64,768]{1,0:T(8,128)(2,1)S(1)} collective-permute-done((bf16[64,768]{1,0:T(8,128)(2,1)S(1)}, bf16[64,768]{1,0:T(8,128)(2,1)S(1)}, u32[]{:S(2)}, u32[]{:S(2)}) %collective-permute-start.15) | collective-permute-done | bytes 98336 | tf_op jit(solution)/shard_map/ppermute | solution.py:30
  78.2 1.2 %collective-permute-start.16 = (bf16[64,768]{1,0:T(8,128)(2,1)S(1)}, bf16[64,768]{1,0:T(8,128)(2,1)S(1)}, u32[]{:S(2)}, u32[]{:S(2)}) collective-permute-start(bf16[64,768]{1,0:T(8,128)(2,1)S(1)} %add_convert_fusion.1), channel_id=1, source_target_pairs={{4,0},{5,1},{6,2},{7,3},{0,4},{1,5},{2,6},{3,7},{12,8},{13,9},{14,... | collective-permute-start | bytes 294920 | tf_op jit(solution)/shard_map/ppermute | solution.py:30
  79.4 3.5 %collective-permute-done.16 = bf16[64,768]{1,0:T(8,128)(2,1)S(1)} collective-permute-done((bf16[64,768]{1,0:T(8,128)(2,1)S(1)}, bf16[64,768]{1,0:T(8,128)(2,1)S(1)}, u32[]{:S(2)}, u32[]{:S(2)}) %collective-permute-start.16) | collective-permute-done | bytes 98336 | tf_op jit(solution)/shard_map/ppermute | solution.py:30
  82.9 1.5 %collective-permute-start.17 = (bf16[64,768]{1,0:T(8,128)(2,1)S(1)}, bf16[64,768]{1,0:T(8,128)(2,1)S(1)}, u32[]{:S(2)}, u32[]{:S(2)}) collective-permute-start(bf16[64,768]{1,0:T(8,128)(2,1)S(1)} %add_convert_fusion), channel_id=1, source_target_pairs={{8,0},{9,1},{10,2},{11,3},{12,4},{13,5},{14,6},{15,7},{0,8},{1,9},... | collective-permute-start | bytes 294920 | tf_op jit(solution)/shard_map/ppermute | solution.py:30
  85.0 1.0 %shard_map.146 = f32[128,768]{1,0:T(8,128)} custom-call(bf16[128,128]{1,0:T(8,128)(2,1)S(1)} %get-tuple-element.43.weights_ref, bf16[64,768]{1,0:T(8,128)(2,1)S(1)} %copy-done.2, bf16[64,768]{1,0:T(8,128)(2,1)S(1)} %collective-permute-done.12.refs_1_), custom_call_target="tpu_custom_call" | custom-call | tf_op jit(solution)/shard_map/pallas_call | solution.py:38
  86.1 3.5 %collective-permute-done.17 = bf16[64,768]{1,0:T(8,128)(2,1)S(1)} collective-permute-done((bf16[64,768]{1,0:T(8,128)(2,1)S(1)}, bf16[64,768]{1,0:T(8,128)(2,1)S(1)}, u32[]{:S(2)}, u32[]{:S(2)}) %collective-permute-start.17) | collective-permute-done | bytes 98336 | tf_op jit(solution)/shard_map/ppermute | solution.py:30
  (52 shorter events, 6.4 us)
Async XLA Ops:
  0.6 1.1 %copy-start.8 = (bf16[192,768]{1,0:T(8,128)(2,1)S(1)}, bf16[192,768]{1,0:T(8,128)(2,1)}, u32[]{:S(2)}) copy-start(bf16[192,768]{1,0:T(8,128)(2,1)} %param.18) | copy-start | bytes 884740
  1.7 3.1 %copy-start.11 = (bf16[192]{0:T(256)(128)(2,1)S(1)}, bf16[192]{0:T(256)(128)(2,1)}, u32[]{:S(2)}) copy-start(bf16[192]{0:T(256)(128)(2,1)} %param.17) | copy-start | bytes 1156
  1.7 3.1 %copy-start.5 = (s32[128,1]{0,1:T(1,128)S(1)}, s32[128,1]{0,1:T(1,128)}, u32[]{:S(2)}) copy-start(s32[128,1]{0,1:T(1,128)} %param.12) | copy-start | bytes 1540
  1.7 3.1 %copy-start.7 = (s32[128]{0:T(128)S(1)}, s32[128]{0:T(128)}, u32[]{:S(2)}) copy-start(s32[128]{0:T(128)} %param.13) | copy-start | bytes 1540
  1.7 16.8 %copy-start.9 = (bf16[768]{0:T(1024)(128)(2,1)S(1)}, bf16[768]{0:T(1024)(128)(2,1)}, u32[]{:S(2)}) copy-start(bf16[768]{0:T(1024)(128)(2,1)} %param.15) | copy-start | bytes 4612
  1.7 16.8 %copy-start.10 = (bf16[768]{0:T(1024)(128)(2,1)S(1)}, bf16[768]{0:T(1024)(128)(2,1)}, u32[]{:S(2)}) copy-start(bf16[768]{0:T(1024)(128)(2,1)} %param.19) | copy-start | bytes 4612
  1.7 16.8 %copy-start.4 = (bf16[128,768]{1,0:T(8,128)(2,1)S(1)}, bf16[128,768]{1,0:T(8,128)(2,1)}, u32[]{:S(2)}) copy-start(bf16[128,768]{1,0:T(8,128)(2,1)} %queries_ref.1) | copy-start | bytes 589828
  1.8 16.8 %copy-start.6 = (s32[128]{0:T(128)S(1)}, s32[128]{0:T(128)}, u32[]{:S(2)}) copy-start(s32[128]{0:T(128)} %param.21) | copy-start | bytes 1540
  1.8 24.0 %copy-start.3 = (bf16[256,768]{1,0:T(8,128)(2,1)S(1)}, bf16[256,768]{1,0:T(8,128)(2,1)}, u32[]{:S(2)}) copy-start(bf16[256,768]{1,0:T(8,128)(2,1)} %table_ref.1) | copy-start | bytes 1179652
  1.8 25.3 %collective-permute-start = (bf16[384,768]{1,0:T(8,128)(2,1)S(1)}, bf16[384,768]{1,0:T(8,128)(2,1)S(1)}, u32[]{:S(2)}, u32[]{:S(2)}) collective-permute-start(bf16[384,768]{1,0:T(8,128)(2,1)S(1)} %constant_dynamic-update-slice_fusion.refs_0_), channel_id=1, source_target_pairs={{1,0},{0,1},{3,2},{2,3},{5,4},{4,5},{7,6},{6,7},{9,8},{8,9},{11,10... | collective-permute-start | bytes 1769480 | tf_op jit(solution)/shard_map/ppermute | solution.py:30
  5.8 21.3 %collective-permute-start.1 = (bf16[384,768]{1,0:T(8,128)(2,1)S(1)}, bf16[384,768]{1,0:T(8,128)(2,1)S(1)}, u32[]{:S(2)}, u32[]{:S(2)}) collective-permute-start(bf16[384,768]{1,0:T(8,128)(2,1)S(1)} %constant_dynamic-update-slice_fusion.refs_0_), channel_id=1, source_target_pairs={{2,0},{3,1},{0,2},{1,3},{6,4},{7,5},{4,6},{5,7},{10,8},{11,9},{8,1... | collective-permute-start | bytes 1769480 | tf_op jit(solution)/shard_map/ppermute | solution.py:30
  9.2 17.9 %collective-permute-start.2 = (bf16[384,768]{1,0:T(8,128)(2,1)S(1)}, bf16[384,768]{1,0:T(8,128)(2,1)S(1)}, u32[]{:S(2)}, u32[]{:S(2)}) collective-permute-start(bf16[384,768]{1,0:T(8,128)(2,1)S(1)} %constant_dynamic-update-slice_fusion.refs_0_), channel_id=1, source_target_pairs={{3,0},{2,1},{1,2},{0,3},{7,4},{6,5},{5,6},{4,7},{11,8},{10,9},{9,1... | collective-permute-start | bytes 1769480 | tf_op jit(solution)/shard_map/ppermute | solution.py:30
  11.5 14.3 %all-to-all-start = ((f32[16,1,256]{2,1,0:T(1,128)}), f32[16,1,256]{2,1,0:T(1,128)S(1)}, u32[]{:S(2)}, u32[]{:S(2)}) async-start(f32[16,1,256]{2,1,0:T(1,128)} %shard_map.138), calls=%async_computation | async-start | bytes 32768 | tf_op jit(solution)/shard_map/all_to_all | solution.py:251
  18.7 0.7 copy-start
  27.1 14.0 %all-to-all-start.1 = ((bf16[16,16,768]{2,1,0:T(8,128)(2,1)}), bf16[16,16,768]{2,1,0:T(8,128)(2,1)}, u32[]{:S(2)}, u32[]{:S(2)}) async-start(bf16[16,16,768]{2,1,0:T(8,128)(2,1)} %bitcast.3), calls=%async_computation.1 | async-start | bytes 786432 | tf_op jit(solution)/shard_map/all_to_all | solution.py:277
  31.4 13.4 %collective-permute-start.4 = (bf16[384,768]{1,0:T(8,128)(2,1)S(1)}, bf16[384,768]{1,0:T(8,128)(2,1)S(1)}, u32[]{:S(2)}, u32[]{:S(2)}) collective-permute-start(bf16[384,768]{1,0:T(8,128)(2,1)S(1)} %collective-permute-done.refs_1_), channel_id=1, source_target_pairs={{17,16},{16,17},{19,18},{18,19},{21,20},{20,21},{23,22},{22,23},{2... | collective-permute-start | bytes 1769480 | tf_op jit(solution)/shard_map/ppermute | solution.py:30
  32.1 12.7 %collective-permute-start.5 = (bf16[384,768]{1,0:T(8,128)(2,1)S(1)}, bf16[384,768]{1,0:T(8,128)(2,1)S(1)}, u32[]{:S(2)}, u32[]{:S(2)}) collective-permute-start(bf16[384,768]{1,0:T(8,128)(2,1)S(1)} %collective-permute-done.refs_1_), channel_id=1, source_target_pairs={{18,16},{19,17},{16,18},{17,19},{22,20},{23,21},{20,22},{21,23},{2... | collective-permute-start | bytes 1769480 | tf_op jit(solution)/shard_map/ppermute | solution.py:30
  32.8 12.0 %collective-permute-start.6 = (bf16[384,768]{1,0:T(8,128)(2,1)S(1)}, bf16[384,768]{1,0:T(8,128)(2,1)}, u32[]{:S(2)}, u32[]{:S(2)}) collective-permute-start(bf16[384,768]{1,0:T(8,128)(2,1)S(1)} %collective-permute-done.refs_1_), channel_id=1, source_target_pairs={{19,16},{18,17},{17,18},{16,19},{23,20},{22,21},{21,22},{20,23},{2... | collective-permute-start | bytes 1769480 | tf_op jit(solution)/shard_map/ppermute | solution.py:30
  41.1 0.9 %copy-start.1 = (bf16[144,768]{1,0:T(8,128)(2,1)S(1)}, bf16[144,768]{1,0:T(8,128)(2,1)}, u32[]{:S(2)}) copy-start(bf16[144,768]{1,0:T(8,128)(2,1)} %copy-done) | copy-start | bytes 663556
  43.5 1.5 %collective-permute-start.3 = (bf16[128,768]{1,0:T(8,128)(2,1)S(1)}, bf16[128,768]{1,0:T(8,128)(2,1)S(1)}, u32[]{:S(2)}, u32[]{:S(2)}) collective-permute-start(bf16[128,768]{1,0:T(8,128)(2,1)S(1)} %get-tuple-element.30.normed_ref), channel_id=1, source_target_pairs={{0,16},{16,0},{1,17},{17,1},{2,18},{18,2},{3,19},{19,3},{4,20},{20... | collective-permute-start | bytes 589832 | tf_op jit(solution)/shard_map/ppermute | solution.py:19
  43.6 7.3 %collective-permute-start.8 = (bf16[128,768]{1,0:T(8,128)(2,1)S(1)}, bf16[128,768]{1,0:T(8,128)(2,1)S(1)}, u32[]{:S(2)}, u32[]{:S(2)}) collective-permute-start(bf16[128,768]{1,0:T(8,128)(2,1)S(1)} %get-tuple-element.30.normed_ref), channel_id=1, source_target_pairs={{0,4},{1,5},{2,6},{3,7},{4,0},{5,1},{6,2},{7,3},{8,12},{9,13},{10,... | collective-permute-start | bytes 589832 | tf_op jit(solution)/shard_map/ppermute | solution.py:19
  50.9 3.8 %collective-permute-start.9 = (bf16[128,768]{1,0:T(8,128)(2,1)S(1)}, bf16[128,768]{1,0:T(8,128)(2,1)S(1)}, u32[]{:S(2)}, u32[]{:S(2)}) collective-permute-start(bf16[128,768]{1,0:T(8,128)(2,1)S(1)} %collective-permute-done.8.normed_ref), channel_id=1, source_target_pairs={{0,16},{16,0},{1,17},{17,1},{2,18},{18,2},{3,19},{19,3},{4,20},{20... | collective-permute-start | bytes 589832 | tf_op jit(solution)/shard_map/ppermute | solution.py:19
  57.4 1.8 %collective-permute-start.10 = (f32[128,768]{1,0:T(8,128)S(1)}, f32[128,768]{1,0:T(8,128)S(1)}, u32[]{:S(2)}, u32[]{:S(2)}) collective-permute-start(f32[128,768]{1,0:T(8,128)S(1)} %get-tuple-element.38), channel_id=1, source_target_pairs={{0,16},{16,0},{1,17},{17,1},{2,18},{18,2},{3,19},{19,3},{4,20},{20... | collective-permute-start | bytes 1179656 | tf_op jit(solution)/shard_map/ppermute | solution.py:19
  57.7 4.0 %collective-permute-start.7 = (f32[128,768]{1,0:T(8,128)S(1)}, f32[128,768]{1,0:T(8,128)S(1)}, u32[]{:S(2)}, u32[]{:S(2)}) collective-permute-start(f32[128,768]{1,0:T(8,128)S(1)} %get-tuple-element.35), channel_id=1, source_target_pairs={{0,16},{16,0},{1,17},{17,1},{2,18},{18,2},{3,19},{19,3},{4,20},{20... | collective-permute-start | bytes 1179656 | tf_op jit(solution)/shard_map/ppermute | solution.py:19
  59.1 1.2 %copy-start.2 = (bf16[64,768]{1,0:T(8,128)(2,1)S(1)}, bf16[64,768]{1,0:T(8,128)(2,1)}, u32[]{:S(2)}) copy-start(bf16[64,768]{1,0:T(8,128)(2,1)} %refs_0_.3) | copy-start | bytes 294916
  59.2 7.1 %collective-permute-start.11 = (bf16[128,768]{1,0:T(8,128)(2,1)S(1)}, bf16[128,768]{1,0:T(8,128)(2,1)S(1)}, u32[]{:S(2)}, u32[]{:S(2)}) collective-permute-start(bf16[128,768]{1,0:T(8,128)(2,1)S(1)} %shard_map.144), channel_id=1, source_target_pairs={{0,4},{1,5},{2,6},{3,7},{4,0},{5,1},{6,2},{7,3},{8,12},{9,13},{10,... | collective-permute-start | bytes 589832 | tf_op jit(solution)/shard_map/ppermute | solution.py:19
  60.4 1.3 %collective-permute-start.12 = (bf16[64,768]{1,0:T(8,128)(2,1)S(1)}, bf16[64,768]{1,0:T(8,128)(2,1)S(1)}, u32[]{:S(2)}, u32[]{:S(2)}) collective-permute-start(bf16[64,768]{1,0:T(8,128)(2,1)S(1)} %copy-done.2), channel_id=1, source_target_pairs={{0,16},{16,0},{1,17},{17,1},{2,18},{18,2},{3,19},{19,3},{4,20},{20... | collective-permute-start | bytes 294920 | tf_op jit(solution)/shard_map/ppermute | solution.py:19
  67.4 1.3 %collective-permute-start.13 = (bf16[64,768]{1,0:T(8,128)(2,1)S(1)}, bf16[64,768]{1,0:T(8,128)(2,1)S(1)}, u32[]{:S(2)}, u32[]{:S(2)}) collective-permute-start(bf16[64,768]{1,0:T(8,128)(2,1)S(1)} %get-tuple-element.45), channel_id=1, source_target_pairs={{0,16},{16,0},{1,17},{17,1},{2,18},{18,2},{3,19},{19,3},{4,20},{20... | collective-permute-start | bytes 294920 | tf_op jit(solution)/shard_map/ppermute | solution.py:19
  68.8 4.7 %collective-permute-start.14 = (bf16[64,768]{1,0:T(8,128)(2,1)S(1)}, bf16[64,768]{1,0:T(8,128)(2,1)S(1)}, u32[]{:S(2)}, u32[]{:S(2)}) collective-permute-start(bf16[64,768]{1,0:T(8,128)(2,1)S(1)} %add_convert_fusion.3), channel_id=1, source_target_pairs={{1,0},{0,1},{3,2},{2,3},{5,4},{4,5},{7,6},{6,7},{9,8},{8,9},{11,10... | collective-permute-start | bytes 294920 | tf_op jit(solution)/shard_map/ppermute | solution.py:30
  73.5 4.7 %collective-permute-start.15 = (bf16[64,768]{1,0:T(8,128)(2,1)S(1)}, bf16[64,768]{1,0:T(8,128)(2,1)S(1)}, u32[]{:S(2)}, u32[]{:S(2)}) collective-permute-start(bf16[64,768]{1,0:T(8,128)(2,1)S(1)} %add_convert_fusion.2), channel_id=1, source_target_pairs={{2,0},{3,1},{0,2},{1,3},{6,4},{7,5},{4,6},{5,7},{10,8},{11,9},{8,1... | collective-permute-start | bytes 294920 | tf_op jit(solution)/shard_map/ppermute | solution.py:30
  78.2 4.7 %collective-permute-start.16 = (bf16[64,768]{1,0:T(8,128)(2,1)S(1)}, bf16[64,768]{1,0:T(8,128)(2,1)S(1)}, u32[]{:S(2)}, u32[]{:S(2)}) collective-permute-start(bf16[64,768]{1,0:T(8,128)(2,1)S(1)} %add_convert_fusion.1), channel_id=1, source_target_pairs={{4,0},{5,1},{6,2},{7,3},{0,4},{1,5},{2,6},{3,7},{12,8},{13,9},{14,... | collective-permute-start | bytes 294920 | tf_op jit(solution)/shard_map/ppermute | solution.py:30
  82.9 6.6 %collective-permute-start.17 = (bf16[64,768]{1,0:T(8,128)(2,1)S(1)}, bf16[64,768]{1,0:T(8,128)(2,1)S(1)}, u32[]{:S(2)}, u32[]{:S(2)}) collective-permute-start(bf16[64,768]{1,0:T(8,128)(2,1)S(1)} %add_convert_fusion), channel_id=1, source_target_pairs={{8,0},{9,1},{10,2},{11,3},{12,4},{13,5},{14,6},{15,7},{0,8},{1,9},... | collective-permute-start | bytes 294920 | tf_op jit(solution)/shard_map/ppermute | solution.py:30

commit v3 on v2

--- a/solution.py
+++ b/solution.py
@@ -118,30 +118,42 @@
 
 
 def hidden_body(plan, normed_ref, normed2_ref, message_ref, *refs):
-    shards, (total_ref, total2_ref, held, sems) = refs[:-4], refs[-4:]
-    chains, units = total_ref.shape[0], held.shape[1] // 2
+    shards, (total_ref, total2_ref, held_in, held_out, sems) = refs[:-5], refs[-5:]
+    chains, units = total_ref.shape[0], held_in.shape[0] // len(plan)
     me, first_core = lax.axis_index("mp"), lax.axis_index("dp") % 2 == 0
-
-    def copy(at, p):
-        return pltpu.make_async_copy(shards[at], held.at[p], sems.at[p])
-
-    for p, (_, at, _, other_at) in enumerate(plan):
-        if at == other_at:
-            copy(at, p).start()
-        else:
-            pl.when(first_core)(copy(at, p).start)
-            pl.when(jnp.logical_not(first_core))(copy(other_at, p).start)
+    held = (held_in, held_out)
+
+    def copy(at, p, side):
+        return pltpu.make_async_copy(
+            shards[at].at[pl.ds(side * units, units)], held[side].at[pl.ds(p * units, units)], sems.at[side, p]
+        )
+
+    for side in (0, 1):
+        for p, (_, at, _, other_at) in enumerate(plan):
+            if at == other_at:
+                copy(at, p, side).start()
+            else:
+
+                @pl.when(first_core)
+                def _():
+                    copy(at, p, side).start()
+
+                @pl.when(jnp.logical_not(first_core))
+                def _():
+                    copy(other_at, p, side).start()
+
     normed = jnp.concatenate([normed_ref[...], normed2_ref[...]], axis=0)
-    total = None
-    for p, (mask, at, other_mask, _) in enumerate(plan):
-        copy(at, p).wait()
-        preact = lax.dot_general(
-            normed, held[p, :units, :], (((1,), (1,)), ((), ())), preferred_element_type=F32
-        )
-        bias = message_ref[pl.ds(me ^ jnp.where(first_core, mask, other_mask), 1)]
-        activated = gelu(preact + bias.reshape(1, bias.shape[2])[:, :units]).astype(BF16)
-        term = jnp.dot(activated, held[p, units:, :], preferred_element_type=F32)
-        total = term if total is None else total + term
+    places = [me ^ jnp.where(first_core, mask, other_mask) for mask, _, other_mask, _ in plan]
+    bias = jnp.concatenate(
+        [message_ref[pl.ds(place, 1)].reshape(1, message_ref.shape[2])[:, :units] for place in places], axis=1
+    )
+    for p, (_, at, _, _) in enumerate(plan):
+        copy(at, p, 0).wait()
+    preact = lax.dot_general(normed, held_in[...], (((1,), (1,)), ((), ())), preferred_element_type=F32)
+    activated = gelu(preact + bias).astype(BF16)
+    for p, (_, at, _, _) in enumerate(plan):
+        copy(at, p, 1).wait()
+    total = jnp.dot(activated, held_out[...], preferred_element_type=F32)
     total_ref[...] = total[:chains, :]
     total2_ref[...] = total[chains:, :]
 
@@ -200,13 +212,15 @@
     )
 
 
-def weight_pieces(own, own_later, groups, hold):
+def weight_pieces(own, own_later, groups, hold, asked):
     near = moved(own, (0, 0, 1), (1, 1, 8))
     near_y = moved(own_later, (0, 0, 2))
-    near_both = moved(own_later, (0, 0, 3))
-    near, near_y, near_both = hold(near, near_y, near_both)
-    far_x, far_y, far_both = (moved(near, (1, 1, mask)) for mask in (1, 2, 3))
-    pieces = [(0, own, 8, near), (1, near, 9, far_x), (2, near_y, 10, far_y), (3, near_both, 11, far_both)]
+    first = after(near, asked)
+    near, near_y = hold(near, near_y)
+    turned = moved(first, (0, 0, 2), (1, 1, 2))
+    far_x = moved(first, (1, 1, 1))
+    far_both = moved(turned, (1, 1, 1))
+    pieces = [(0, own, 8, near), (1, near, 9, far_x), (2, near_y, 10, turned), (3, turned, 11, far_both)]
     for level in range(16, groups, 16):
         base = moved(own, (0, 0, level), (1, 1, level ^ 8))
         by_x, by_y = (moved(base, (0, 0, bit), (1, 1, bit)) for bit in (1, 2))
@@ -273,7 +287,7 @@
         held.append(early_and_served[-1])
         return early_and_served[:-1]
 
-    pieces = weight_pieces(own, own_later, groups, hold)
+    pieces = weight_pieces(own, own_later, groups, hold, asked)
     fetched = lax.all_to_all(held[0], "mp", split_axis=0, concat_axis=0, tiled=True)
     shards = []
     for piece in pieces:
@@ -299,7 +313,11 @@
             asked,
             *shards,
             in_place=range(3, 3 + len(shards)),
-            scratch=(pltpu.VMEM((len(plan), 2 * units, features), BF16), pltpu.SemaphoreType.DMA((len(plan),))),
+            scratch=(
+                pltpu.VMEM((len(plan) * units, features), BF16),
+                pltpu.VMEM((len(plan) * units, features), BF16),
+                pltpu.SemaphoreType.DMA((2, len(plan))),
+            ),
             vmem=LARGE_VMEM,
         )
 

time: 90.7 us -> 88.5 us (0.976)
  blocking collectives: 0 us -> 12.2 us
  starting transfers between devices: 32.9 us -> 23.1 us
  waiting for transfers between devices: 40.9 us -> 38.5 us
  Pallas kernels: 11.3 us -> 9.19 us
    all_to_all x0 -> x1, blocking collectives: none -> 12.2 us  [local(): lax.all_to_all(message, 'mp', split_axis=0, concat_axis=0, tiled=True)]
    ppermute x10 -> x9, waiting for transfers between devices: 14.6 us -> 25.4 us  [moved(): return lax.ppermute(block, ('dp', 'mp'), route)]
    all_to_all x1 -> x0, starting transfers between devices: 6.94 us -> none  [local(): lax.all_to_all(message, 'mp', split_axis=0, concat_axis=0, tiled=True)]
    all_to_all x1, waiting for transfers between devices: 6.87 us -> 0.01 us  [local(): lax.all_to_all(held[0], 'mp', split_axis=0, concat_axis=0, tiled=True)]
    all_to_all x1 -> x0, waiting for transfers between devices: 6.42 us -> none  [local(): lax.all_to_all(message, 'mp', split_axis=0, concat_axis=0, tiled=True)]
    ppermute x10 -> x9, starting transfers between devices: 16 us -> 13.5 us  [moved(): return lax.ppermute(block, ('dp', 'mp'), route)]
    pallas_call x9, Pallas kernels: 11.3 us -> 9.19 us  [kernel_call(): pl.pallas_call(body, out_shape=out_shape, in_specs=[pl.BlockSpec(memory_s...]
  transfers between devices with their start and end apart: 20 -> 18, of which waited for: 13 -> 11; matrix products, arithmetic and copies ran while one was open for 1% -> 1% of each run, Pallas kernels for 8% -> 7%
where the time goes in v3:
time: 88.5 us; the launch traced here: 88.1 us
  waiting for transfers between devices  38.5 us (44%)
  starting transfers between devices  23.1 us (26%)
  blocking collectives  12.2 us (14%)
  Pallas kernels  9.19 us (10%)
  local copies, waits for them, and re-layouts  2.74 us (3%)
  other arithmetic  1.43 us (2%)
    ppermute x9, waiting for transfers between devices, moved(): return lax.ppermute(block, ('dp', 'mp'), route)  25.4 us
    ppermute x9, starting transfers between devices, moved(): return lax.ppermute(block, ('dp', 'mp'), route)  13.5 us
    ppermute x8, waiting for transfers between devices, flipped(): lax.ppermute(block, axis, [(i, i ^ mask) for i in range(lax.axis_size(axi...  13.1 us
    all_to_all x1, blocking collectives, local(): lax.all_to_all(message, 'mp', split_axis=0, concat_axis=0, tiled=True)  12.2 us
    pallas_call x9, Pallas kernels, kernel_call(): pl.pallas_call(body, out_shape=out_shape, in_specs=[pl.BlockSpec(memory_s...  9.19 us
    ppermute x8, starting transfers between devices, flipped(): lax.ppermute(block, axis, [(i, i ^ mask) for i in range(lax.axis_size(axi...  5.43 us
    all_to_all x1, starting transfers between devices, local(): lax.all_to_all(held[0], 'mp', split_axis=0, concat_axis=0, tiled=True)  4.22 us
    unnamed x25, local copies, waits for them, and re-layouts  2.71 us
  transfers between devices with their start and end apart: 18, of which 11 were waited for; matrix products, arithmetic and copies ran while one was open for 1% of the time, Pallas kernels for 7%

profile of v3, /device:TPU:0, one launch (start us, length us, event | category | flops | bytes accessed | tf_op | source)
XLA Modules:
  0.0 88.1 jit_solution(7840791258257963194)
XLA Ops:
  0.6 1.0 %constant_dynamic-update-slice_fusion.1 = bf16[384,768]{1,0:T(8,128)(2,1)S(1)} fusion(bf16[192,768]{1,0:T(8,128)(2,1)} %param.16), kind=kLoop, calls=%fused_computation.6 | loop fusion | bytes 589824
  1.8 3.0 %collective-permute-start = (bf16[384,768]{1,0:T(8,128)(2,1)S(1)}, bf16[384,768]{1,0:T(8,128)(2,1)S(1)}, u32[]{:S(2)}, u32[]{:S(2)}) collective-permute-start(bf16[384,768]{1,0:T(8,128)(2,1)S(1)} %constant_dynamic-update-slice_fusion.refs_0_), channel_id=1, source_target_pairs={{1,0},{0,1},{3,2},{2,3},{5,4},{4,5},{7,6},{6,7},{9,8},{8,9},{11,10... | collective-permute-start | bytes 1769480 | tf_op jit(solution)/shard_map/ppermute | solution.py:30
  5.2 3.4 %collective-permute-start.1 = (bf16[384,768]{1,0:T(8,128)(2,1)S(1)}, bf16[384,768]{1,0:T(8,128)(2,1)S(1)}, u32[]{:S(2)}, u32[]{:S(2)}) collective-permute-start(bf16[384,768]{1,0:T(8,128)(2,1)S(1)} %constant_dynamic-update-slice_fusion.refs_0_), channel_id=1, source_target_pairs={{2,0},{3,1},{0,2},{1,3},{6,4},{7,5},{4,6},{5,7},{10,8},{11,9},{8,1... | collective-permute-start | bytes 1769480 | tf_op jit(solution)/shard_map/ppermute | solution.py:30
  8.6 12.2 %all_to_all.16.message_ref = f32[16,1,256]{2,1,0:T(1,128)S(1)} all-to-all(f32[16,1,256]{2,1,0:T(1,128)S(1)} %shard_map.138), channel_id=1, replica_groups=mesh['dp'=2,'mp'=16] {'mp'}, dimensions={0} | all-to-all | bytes 32768 | tf_op jit(solution)/shard_map/all_to_all | solution.py:265
  22.3 1.3 %shard_map.140 = bf16[256,768]{1,0:T(8,128)(2,1)} custom-call(f32[16,1,256]{2,1,0:T(1,128)S(1)} %all_to_all.16.message_ref, bf16[256,768]{1,0:T(8,128)(2,1)S(1)} %copy-done.3), custom_call_target="tpu_custom_call" | custom-call | tf_op jit(solution)/shard_map/pallas_call | solution.py:38
  23.6 4.2 %all-to-all-start.1 = ((bf16[16,16,768]{2,1,0:T(8,128)(2,1)}), bf16[16,16,768]{2,1,0:T(8,128)(2,1)}, u32[]{:S(2)}, u32[]{:S(2)}) async-start(bf16[16,16,768]{2,1,0:T(8,128)(2,1)} %bitcast.3), calls=%async_computation.1 | async-start | bytes 786432 | tf_op jit(solution)/shard_map/all_to_all | solution.py:291
  28.5 11.5 %collective-permute-done.4.refs_4_ = bf16[384,768]{1,0:T(8,128)(2,1)S(1)} collective-permute-done((bf16[384,768]{1,0:T(8,128)(2,1)S(1)}, bf16[384,768]{1,0:T(8,128)(2,1)S(1)}, u32[]{:S(2)}, u32[]{:S(2)}) %collective-permute-start.4) | collective-permute-done | bytes 589856 | tf_op jit(solution)/shard_map/ppermute | solution.py:30
  40.7 0.9 %copy-done.1 = bf16[144,768]{1,0:T(8,128)(2,1)S(1)} copy-done((bf16[144,768]{1,0:T(8,128)(2,1)S(1)}, bf16[144,768]{1,0:T(8,128)(2,1)}, u32[]{:S(2)}) %copy-start.1) | copy-done | bytes 221208
  41.6 1.4 %shard_map.141 = (f32[128,768]{1,0:T(8,128)S(1)}, bf16[128,768]{1,0:T(8,128)(2,1)S(1)}, s32[1,128]{1,0:T(1,128)S(1)}) custom-call(bf16[144,768]{1,0:T(8,128)(2,1)S(1)} %copy-done.1, bf16[256,768]{1,0:T(8,128)(2,1)} %bitcast.4.fetched_ref), custom_call_target="tpu_custom_call" | custom-call | tf_op jit(solution)/shard_map/pallas_call | solution.py:38
  43.1 0.8 collective-permute-start.2
  43.9 1.4 %collective-permute-start.7 = (bf16[128,768]{1,0:T(8,128)(2,1)S(1)}, bf16[128,768]{1,0:T(8,128)(2,1)S(1)}, u32[]{:S(2)}, u32[]{:S(2)}) collective-permute-start(bf16[128,768]{1,0:T(8,128)(2,1)S(1)} %get-tuple-element.30.normed_ref), channel_id=1, source_target_pairs={{0,4},{1,5},{2,6},{3,7},{4,0},{5,1},{6,2},{7,3},{8,12},{9,13},{10,... | collective-permute-start | bytes 589832 | tf_op jit(solution)/shard_map/ppermute | solution.py:19
  45.3 1.9 %shard_map.142 = (f32[128,768]{1,0:T(8,128)S(1)}, f32[128,768]{1,0:T(8,128)S(1)}) custom-call(bf16[128,768]{1,0:T(8,128)(2,1)S(1)} %get-tuple-element.30.normed_ref, bf16[128,768]{1,0:T(8,128)(2,1)S(1)} %collective-permute-done.2.normed2_ref, f32[16,1,256]{2,1,0:T(1,128)S(1)} %all_to_all.16.message_ref, ...), custom_call_target="tpu_custom_call" | custom-call | tf_op jit(solution)/shard_map/pallas_call | solution.py:38
  47.2 3.5 %collective-permute-done.7.normed_ref = bf16[128,768]{1,0:T(8,128)(2,1)S(1)} collective-permute-done((bf16[128,768]{1,0:T(8,128)(2,1)S(1)}, bf16[128,768]{1,0:T(8,128)(2,1)S(1)}, u32[]{:S(2)}, u32[]{:S(2)}) %collective-permute-start.7) | collective-permute-done | bytes 196640 | tf_op jit(solution)/shard_map/ppermute | solution.py:19
  50.7 1.4 %collective-permute-start.8 = (bf16[128,768]{1,0:T(8,128)(2,1)S(1)}, bf16[128,768]{1,0:T(8,128)(2,1)S(1)}, u32[]{:S(2)}, u32[]{:S(2)}) collective-permute-start(bf16[128,768]{1,0:T(8,128)(2,1)S(1)} %collective-permute-done.7.normed_ref), channel_id=1, source_target_pairs={{0,16},{16,0},{1,17},{17,1},{2,18},{18,2},{3,19},{19,3},{4,20},{20... | collective-permute-start | bytes 589832 | tf_op jit(solution)/shard_map/ppermute | solution.py:19
  52.1 1.1 %collective-permute-done.8.normed2_ref = bf16[128,768]{1,0:T(8,128)(2,1)S(1)} collective-permute-done((bf16[128,768]{1,0:T(8,128)(2,1)S(1)}, bf16[128,768]{1,0:T(8,128)(2,1)S(1)}, u32[]{:S(2)}, u32[]{:S(2)}) %collective-permute-start.8) | collective-permute-done | bytes 196640 | tf_op jit(solution)/shard_map/ppermute | solution.py:19
  53.2 1.9 %shard_map.143 = (f32[128,768]{1,0:T(8,128)S(1)}, f32[128,768]{1,0:T(8,128)S(1)}) custom-call(bf16[128,768]{1,0:T(8,128)(2,1)S(1)} %collective-permute-done.7.normed_ref, bf16[128,768]{1,0:T(8,128)(2,1)S(1)} %collective-permute-done.8.normed2_ref, f32[16,1,256]{2,1,0:T(1,128)S(1)} %all_to_all.16.message_ref, ...), custom_call_target="tpu_custom_call" | custom-call | tf_op jit(solution)/shard_map/pallas_call | solution.py:38
  55.6 1.2 %collective-permute-done.9.received_ref = f32[128,768]{1,0:T(8,128)S(1)} collective-permute-done((f32[128,768]{1,0:T(8,128)S(1)}, f32[128,768]{1,0:T(8,128)S(1)}, u32[]{:S(2)}, u32[]{:S(2)}) %collective-permute-start.9) | collective-permute-done | bytes 393248 | tf_op jit(solution)/shard_map/ppermute | solution.py:19
  56.9 1.2 %collective-permute-start.10 = (bf16[128,768]{1,0:T(8,128)(2,1)S(1)}, bf16[128,768]{1,0:T(8,128)(2,1)S(1)}, u32[]{:S(2)}, u32[]{:S(2)}) collective-permute-start(bf16[128,768]{1,0:T(8,128)(2,1)S(1)} %shard_map.144), channel_id=1, source_target_pairs={{0,4},{1,5},{2,6},{3,7},{4,0},{5,1},{6,2},{7,3},{8,12},{9,13},{10,... | collective-permute-start | bytes 589832 | tf_op jit(solution)/shard_map/ppermute | solution.py:19
  58.2 1.2 %collective-permute-done.11.refs_1_ = bf16[64,768]{1,0:T(8,128)(2,1)S(1)} collective-permute-done((bf16[64,768]{1,0:T(8,128)(2,1)S(1)}, bf16[64,768]{1,0:T(8,128)(2,1)S(1)}, u32[]{:S(2)}, u32[]{:S(2)}) %collective-permute-start.11) | collective-permute-done | bytes 98336 | tf_op jit(solution)/shard_map/ppermute | solution.py:19
  59.4 4.7 %collective-permute-done.10.other_ref = bf16[128,768]{1,0:T(8,128)(2,1)S(1)} collective-permute-done((bf16[128,768]{1,0:T(8,128)(2,1)S(1)}, bf16[128,768]{1,0:T(8,128)(2,1)S(1)}, u32[]{:S(2)}, u32[]{:S(2)}) %collective-permute-start.10) | collective-permute-done | bytes 196640 | tf_op jit(solution)/shard_map/ppermute | solution.py:19
  64.1 1.1 %shard_map.145 = (bf16[128,768]{1,0:T(8,128)(2,1)}, f32[128,1]{1,0:T(8,128)S(1)}, bf16[128,128]{1,0:T(8,128)(2,1)S(1)}, bf16[64,768]{1,0:T(8,128)(2,1)S(1)}, bf16[64,768]{1,0:T(8,128)(2,1)S(1)}) custom-call(f32[128,768]{1,0:T(8,128)S(1)} %get-tuple-element.29.shifted_ref, f32[128,768]{1,0:T(8,128)S(1)} %get-tuple-element.34.total_ref, ...), custom_call_target="tpu_custom_call" | custom-call | tf_op jit(solution)/shard_map/pallas_call | solution.py:38
  65.3 1.3 %collective-permute-done.12 = bf16[64,768]{1,0:T(8,128)(2,1)S(1)} collective-permute-done((bf16[64,768]{1,0:T(8,128)(2,1)S(1)}, bf16[64,768]{1,0:T(8,128)(2,1)S(1)}, u32[]{:S(2)}, u32[]{:S(2)}) %collective-permute-start.12) | collective-permute-done | bytes 98336 | tf_op jit(solution)/shard_map/ppermute | solution.py:19
  66.6 0.8 collective-permute-start.13
  67.4 3.9 %collective-permute-done.13 = bf16[64,768]{1,0:T(8,128)(2,1)S(1)} collective-permute-done((bf16[64,768]{1,0:T(8,128)(2,1)S(1)}, bf16[64,768]{1,0:T(8,128)(2,1)S(1)}, u32[]{:S(2)}, u32[]{:S(2)}) %collective-permute-start.13) | collective-permute-done | bytes 98336 | tf_op jit(solution)/shard_map/ppermute | solution.py:30
  71.3 0.9 %collective-permute-start.14 = (bf16[64,768]{1,0:T(8,128)(2,1)S(1)}, bf16[64,768]{1,0:T(8,128)(2,1)S(1)}, u32[]{:S(2)}, u32[]{:S(2)}) collective-permute-start(bf16[64,768]{1,0:T(8,128)(2,1)S(1)} %add_convert_fusion.2), channel_id=1, source_target_pairs={{2,0},{3,1},{0,2},{1,3},{6,4},{7,5},{4,6},{5,7},{10,8},{11,9},{8,1... | collective-permute-start | bytes 294920 | tf_op jit(solution)/shard_map/ppermute | solution.py:30
  72.2 3.7 %collective-permute-done.14 = bf16[64,768]{1,0:T(8,128)(2,1)S(1)} collective-permute-done((bf16[64,768]{1,0:T(8,128)(2,1)S(1)}, bf16[64,768]{1,0:T(8,128)(2,1)S(1)}, u32[]{:S(2)}, u32[]{:S(2)}) %collective-permute-start.14) | collective-permute-done | bytes 98336 | tf_op jit(solution)/shard_map/ppermute | solution.py:30
  76.0 1.2 %collective-permute-start.15 = (bf16[64,768]{1,0:T(8,128)(2,1)S(1)}, bf16[64,768]{1,0:T(8,128)(2,1)S(1)}, u32[]{:S(2)}, u32[]{:S(2)}) collective-permute-start(bf16[64,768]{1,0:T(8,128)(2,1)S(1)} %add_convert_fusion.1), channel_id=1, source_target_pairs={{4,0},{5,1},{6,2},{7,3},{0,4},{1,5},{2,6},{3,7},{12,8},{13,9},{14,... | collective-permute-start | bytes 294920 | tf_op jit(solution)/shard_map/ppermute | solution.py:30
  77.2 3.5 %collective-permute-done.15 = bf16[64,768]{1,0:T(8,128)(2,1)S(1)} collective-permute-done((bf16[64,768]{1,0:T(8,128)(2,1)S(1)}, bf16[64,768]{1,0:T(8,128)(2,1)S(1)}, u32[]{:S(2)}, u32[]{:S(2)}) %collective-permute-start.15) | collective-permute-done | bytes 98336 | tf_op jit(solution)/shard_map/ppermute | solution.py:30
  80.7 2.1 %collective-permute-start.16 = (bf16[64,768]{1,0:T(8,128)(2,1)S(1)}, bf16[64,768]{1,0:T(8,128)(2,1)S(1)}, u32[]{:S(2)}, u32[]{:S(2)}) collective-permute-start(bf16[64,768]{1,0:T(8,128)(2,1)S(1)} %add_convert_fusion), channel_id=1, source_target_pairs={{8,0},{9,1},{10,2},{11,3},{12,4},{13,5},{14,6},{15,7},{0,8},{1,9},... | collective-permute-start | bytes 294920 | tf_op jit(solution)/shard_map/ppermute | solution.py:30
  83.5 1.0 %shard_map.146 = f32[128,768]{1,0:T(8,128)} custom-call(bf16[128,128]{1,0:T(8,128)(2,1)S(1)} %get-tuple-element.43.weights_ref, bf16[64,768]{1,0:T(8,128)(2,1)S(1)} %copy-done.2, bf16[64,768]{1,0:T(8,128)(2,1)S(1)} %collective-permute-done.11.refs_1_), custom_call_target="tpu_custom_call" | custom-call | tf_op jit(solution)/shard_map/pallas_call | solution.py:38
  84.5 2.8 %collective-permute-done.16 = bf16[64,768]{1,0:T(8,128)(2,1)S(1)} collective-permute-done((bf16[64,768]{1,0:T(8,128)(2,1)S(1)}, bf16[64,768]{1,0:T(8,128)(2,1)S(1)}, u32[]{:S(2)}, u32[]{:S(2)}) %collective-permute-start.16) | collective-permute-done | bytes 98336 | tf_op jit(solution)/shard_map/ppermute | solution.py:30
  87.4 0.7 add_multiply_fusion
  (49 shorter events, 4.7 us)
Async XLA Ops:
  0.6 1.1 %copy-start.8 = (bf16[192,768]{1,0:T(8,128)(2,1)S(1)}, bf16[192,768]{1,0:T(8,128)(2,1)}, u32[]{:S(2)}) copy-start(bf16[192,768]{1,0:T(8,128)(2,1)} %param.18) | copy-start | bytes 884740
  1.7 3.1 %copy-start.11 = (bf16[192]{0:T(256)(128)(2,1)S(1)}, bf16[192]{0:T(256)(128)(2,1)}, u32[]{:S(2)}) copy-start(bf16[192]{0:T(256)(128)(2,1)} %param.17) | copy-start | bytes 1156
  1.7 3.1 %copy-start.5 = (s32[128,1]{0,1:T(1,128)S(1)}, s32[128,1]{0,1:T(1,128)}, u32[]{:S(2)}) copy-start(s32[128,1]{0,1:T(1,128)} %param.12) | copy-start | bytes 1540
  1.7 3.1 %copy-start.7 = (s32[128]{0:T(128)S(1)}, s32[128]{0:T(128)}, u32[]{:S(2)}) copy-start(s32[128]{0:T(128)} %param.13) | copy-start | bytes 1540
  1.7 19.7 %copy-start.9 = (bf16[768]{0:T(1024)(128)(2,1)S(1)}, bf16[768]{0:T(1024)(128)(2,1)}, u32[]{:S(2)}) copy-start(bf16[768]{0:T(1024)(128)(2,1)} %param.15) | copy-start | bytes 4612
  1.7 19.7 %copy-start.10 = (bf16[768]{0:T(1024)(128)(2,1)S(1)}, bf16[768]{0:T(1024)(128)(2,1)}, u32[]{:S(2)}) copy-start(bf16[768]{0:T(1024)(128)(2,1)} %param.19) | copy-start | bytes 4612
  1.7 19.7 %copy-start.4 = (bf16[128,768]{1,0:T(8,128)(2,1)S(1)}, bf16[128,768]{1,0:T(8,128)(2,1)}, u32[]{:S(2)}) copy-start(bf16[128,768]{1,0:T(8,128)(2,1)} %queries_ref.1) | copy-start | bytes 589828
  1.8 19.7 %copy-start.6 = (s32[128]{0:T(128)S(1)}, s32[128]{0:T(128)}, u32[]{:S(2)}) copy-start(s32[128]{0:T(128)} %param.21) | copy-start | bytes 1540
  1.8 20.5 %copy-start.3 = (bf16[256,768]{1,0:T(8,128)(2,1)S(1)}, bf16[256,768]{1,0:T(8,128)(2,1)}, u32[]{:S(2)}) copy-start(bf16[256,768]{1,0:T(8,128)(2,1)} %table_ref.1) | copy-start | bytes 1179652
  1.8 19.0 %collective-permute-start = (bf16[384,768]{1,0:T(8,128)(2,1)S(1)}, bf16[384,768]{1,0:T(8,128)(2,1)S(1)}, u32[]{:S(2)}, u32[]{:S(2)}) collective-permute-start(bf16[384,768]{1,0:T(8,128)(2,1)S(1)} %constant_dynamic-update-slice_fusion.refs_0_), channel_id=1, source_target_pairs={{1,0},{0,1},{3,2},{2,3},{5,4},{4,5},{7,6},{6,7},{9,8},{8,9},{11,10... | collective-permute-start | bytes 1769480 | tf_op jit(solution)/shard_map/ppermute | solution.py:30
  5.2 18.4 %collective-permute-start.1 = (bf16[384,768]{1,0:T(8,128)(2,1)S(1)}, bf16[384,768]{1,0:T(8,128)(2,1)S(1)}, u32[]{:S(2)}, u32[]{:S(2)}) collective-permute-start(bf16[384,768]{1,0:T(8,128)(2,1)S(1)} %constant_dynamic-update-slice_fusion.refs_0_), channel_id=1, source_target_pairs={{2,0},{3,1},{0,2},{1,3},{6,4},{7,5},{4,6},{5,7},{10,8},{11,9},{8,1... | collective-permute-start | bytes 1769480 | tf_op jit(solution)/shard_map/ppermute | solution.py:30
  20.8 19.2 %collective-permute-start.4 = (bf16[384,768]{1,0:T(8,128)(2,1)S(1)}, bf16[384,768]{1,0:T(8,128)(2,1)S(1)}, u32[]{:S(2)}, u32[]{:S(2)}) collective-permute-start(bf16[384,768]{1,0:T(8,128)(2,1)S(1)} %collective-permute-done.refs_1_), channel_id=1, source_target_pairs={{2,0},{3,1},{0,2},{1,3},{6,4},{7,5},{4,6},{5,7},{10,8},{11,9},{8,1... | collective-permute-start | bytes 1769480 | tf_op jit(solution)/shard_map/ppermute | solution.py:30
  21.6 0.7 copy-start
  23.6 17.1 %all-to-all-start.1 = ((bf16[16,16,768]{2,1,0:T(8,128)(2,1)}), bf16[16,16,768]{2,1,0:T(8,128)(2,1)}, u32[]{:S(2)}, u32[]{:S(2)}) async-start(bf16[16,16,768]{2,1,0:T(8,128)(2,1)} %bitcast.3), calls=%async_computation.1 | async-start | bytes 786432 | tf_op jit(solution)/shard_map/all_to_all | solution.py:291
  27.8 17.5 %collective-permute-start.3 = (bf16[384,768]{1,0:T(8,128)(2,1)S(1)}, bf16[384,768]{1,0:T(8,128)(2,1)S(1)}, u32[]{:S(2)}, u32[]{:S(2)}) collective-permute-start(bf16[384,768]{1,0:T(8,128)(2,1)S(1)} %collective-permute-done.refs_1_), channel_id=1, source_target_pairs={{17,16},{16,17},{19,18},{18,19},{21,20},{20,21},{23,22},{22,23},{2... | collective-permute-start | bytes 1769480 | tf_op jit(solution)/shard_map/ppermute | solution.py:30
  40.0 5.3 %collective-permute-start.5 = (bf16[384,768]{1,0:T(8,128)(2,1)S(1)}, bf16[384,768]{1,0:T(8,128)(2,1)S(1)}, u32[]{:S(2)}, u32[]{:S(2)}) collective-permute-start(bf16[384,768]{1,0:T(8,128)(2,1)S(1)} %collective-permute-done.4.refs_4_), channel_id=1, source_target_pairs={{17,16},{16,17},{19,18},{18,19},{21,20},{20,21},{23,22},{22,23},{2... | collective-permute-start | bytes 1769480 | tf_op jit(solution)/shard_map/ppermute | solution.py:30
  40.7 0.9 %copy-start.1 = (bf16[144,768]{1,0:T(8,128)(2,1)S(1)}, bf16[144,768]{1,0:T(8,128)(2,1)}, u32[]{:S(2)}) copy-start(bf16[144,768]{1,0:T(8,128)(2,1)} %copy-done) | copy-start | bytes 663556
  43.1 2.2 %collective-permute-start.2 = (bf16[128,768]{1,0:T(8,128)(2,1)S(1)}, bf16[128,768]{1,0:T(8,128)(2,1)S(1)}, u32[]{:S(2)}, u32[]{:S(2)}) collective-permute-start(bf16[128,768]{1,0:T(8,128)(2,1)S(1)} %get-tuple-element.30.normed_ref), channel_id=1, source_target_pairs={{0,16},{16,0},{1,17},{17,1},{2,18},{18,2},{3,19},{19,3},{4,20},{20... | collective-permute-start | bytes 589832 | tf_op jit(solution)/shard_map/ppermute | solution.py:19
  43.9 6.9 %collective-permute-start.7 = (bf16[128,768]{1,0:T(8,128)(2,1)S(1)}, bf16[128,768]{1,0:T(8,128)(2,1)S(1)}, u32[]{:S(2)}, u32[]{:S(2)}) collective-permute-start(bf16[128,768]{1,0:T(8,128)(2,1)S(1)} %get-tuple-element.30.normed_ref), channel_id=1, source_target_pairs={{0,4},{1,5},{2,6},{3,7},{4,0},{5,1},{6,2},{7,3},{8,12},{9,13},{10,... | collective-permute-start | bytes 589832 | tf_op jit(solution)/shard_map/ppermute | solution.py:19
  50.7 2.4 %collective-permute-start.8 = (bf16[128,768]{1,0:T(8,128)(2,1)S(1)}, bf16[128,768]{1,0:T(8,128)(2,1)S(1)}, u32[]{:S(2)}, u32[]{:S(2)}) collective-permute-start(bf16[128,768]{1,0:T(8,128)(2,1)S(1)} %collective-permute-done.7.normed_ref), channel_id=1, source_target_pairs={{0,16},{16,0},{1,17},{17,1},{2,18},{18,2},{3,19},{19,3},{4,20},{20... | collective-permute-start | bytes 589832 | tf_op jit(solution)/shard_map/ppermute | solution.py:19
  55.1 1.8 %collective-permute-start.9 = (f32[128,768]{1,0:T(8,128)S(1)}, f32[128,768]{1,0:T(8,128)S(1)}, u32[]{:S(2)}, u32[]{:S(2)}) collective-permute-start(f32[128,768]{1,0:T(8,128)S(1)} %get-tuple-element.38), channel_id=1, source_target_pairs={{0,16},{16,0},{1,17},{17,1},{2,18},{18,2},{3,19},{19,3},{4,20},{20... | collective-permute-start | bytes 1179656 | tf_op jit(solution)/shard_map/ppermute | solution.py:19
  55.5 3.9 %collective-permute-start.6 = (f32[128,768]{1,0:T(8,128)S(1)}, f32[128,768]{1,0:T(8,128)S(1)}, u32[]{:S(2)}, u32[]{:S(2)}) collective-permute-start(f32[128,768]{1,0:T(8,128)S(1)} %get-tuple-element.35), channel_id=1, source_target_pairs={{0,16},{16,0},{1,17},{17,1},{2,18},{18,2},{3,19},{19,3},{4,20},{20... | collective-permute-start | bytes 1179656 | tf_op jit(solution)/shard_map/ppermute | solution.py:19
  56.9 1.2 %copy-start.2 = (bf16[64,768]{1,0:T(8,128)(2,1)S(1)}, bf16[64,768]{1,0:T(8,128)(2,1)}, u32[]{:S(2)}) copy-start(bf16[64,768]{1,0:T(8,128)(2,1)} %refs_0_.3) | copy-start | bytes 294916
  56.9 7.2 %collective-permute-start.10 = (bf16[128,768]{1,0:T(8,128)(2,1)S(1)}, bf16[128,768]{1,0:T(8,128)(2,1)S(1)}, u32[]{:S(2)}, u32[]{:S(2)}) collective-permute-start(bf16[128,768]{1,0:T(8,128)(2,1)S(1)} %shard_map.144), channel_id=1, source_target_pairs={{0,4},{1,5},{2,6},{3,7},{4,0},{5,1},{6,2},{7,3},{8,12},{9,13},{10,... | collective-permute-start | bytes 589832 | tf_op jit(solution)/shard_map/ppermute | solution.py:19
  58.1 1.3 %collective-permute-start.11 = (bf16[64,768]{1,0:T(8,128)(2,1)S(1)}, bf16[64,768]{1,0:T(8,128)(2,1)S(1)}, u32[]{:S(2)}, u32[]{:S(2)}) collective-permute-start(bf16[64,768]{1,0:T(8,128)(2,1)S(1)} %copy-done.2), channel_id=1, source_target_pairs={{0,16},{16,0},{1,17},{17,1},{2,18},{18,2},{3,19},{19,3},{4,20},{20... | collective-permute-start | bytes 294920 | tf_op jit(solution)/shard_map/ppermute | solution.py:19
  65.2 1.3 %collective-permute-start.12 = (bf16[64,768]{1,0:T(8,128)(2,1)S(1)}, bf16[64,768]{1,0:T(8,128)(2,1)S(1)}, u32[]{:S(2)}, u32[]{:S(2)}) collective-permute-start(bf16[64,768]{1,0:T(8,128)(2,1)S(1)} %get-tuple-element.45), channel_id=1, source_target_pairs={{0,16},{16,0},{1,17},{17,1},{2,18},{18,2},{3,19},{19,3},{4,20},{20... | collective-permute-start | bytes 294920 | tf_op jit(solution)/shard_map/ppermute | solution.py:19
  66.6 4.7 %collective-permute-start.13 = (bf16[64,768]{1,0:T(8,128)(2,1)S(1)}, bf16[64,768]{1,0:T(8,128)(2,1)S(1)}, u32[]{:S(2)}, u32[]{:S(2)}) collective-permute-start(bf16[64,768]{1,0:T(8,128)(2,1)S(1)} %add_convert_fusion.3), channel_id=1, source_target_pairs={{1,0},{0,1},{3,2},{2,3},{5,4},{4,5},{7,6},{6,7},{9,8},{8,9},{11,10... | collective-permute-start | bytes 294920 | tf_op jit(solution)/shard_map/ppermute | solution.py:30
  71.3 4.7 %collective-permute-start.14 = (bf16[64,768]{1,0:T(8,128)(2,1)S(1)}, bf16[64,768]{1,0:T(8,128)(2,1)S(1)}, u32[]{:S(2)}, u32[]{:S(2)}) collective-permute-start(bf16[64,768]{1,0:T(8,128)(2,1)S(1)} %add_convert_fusion.2), channel_id=1, source_target_pairs={{2,0},{3,1},{0,2},{1,3},{6,4},{7,5},{4,6},{5,7},{10,8},{11,9},{8,1... | collective-permute-start | bytes 294920 | tf_op jit(solution)/shard_map/ppermute | solution.py:30
  76.0 4.7 %collective-permute-start.15 = (bf16[64,768]{1,0:T(8,128)(2,1)S(1)}, bf16[64,768]{1,0:T(8,128)(2,1)S(1)}, u32[]{:S(2)}, u32[]{:S(2)}) collective-permute-start(bf16[64,768]{1,0:T(8,128)(2,1)S(1)} %add_convert_fusion.1), channel_id=1, source_target_pairs={{4,0},{5,1},{6,2},{7,3},{0,4},{1,5},{2,6},{3,7},{12,8},{13,9},{14,... | collective-permute-start | bytes 294920 | tf_op jit(solution)/shard_map/ppermute | solution.py:30
  80.7 6.6 %collective-permute-start.16 = (bf16[64,768]{1,0:T(8,128)(2,1)S(1)}, bf16[64,768]{1,0:T(8,128)(2,1)S(1)}, u32[]{:S(2)}, u32[]{:S(2)}) collective-permute-start(bf16[64,768]{1,0:T(8,128)(2,1)S(1)} %add_convert_fusion), channel_id=1, source_target_pairs={{8,0},{9,1},{10,2},{11,3},{12,4},{13,5},{14,6},{15,7},{0,8},{1,9},... | collective-permute-start | bytes 294920 | tf_op jit(solution)/shard_map/ppermute | solution.py:30

commit v4 on v3

--- a/solution.py
+++ b/solution.py
@@ -217,10 +217,10 @@
     near_y = moved(own_later, (0, 0, 2))
     first = after(near, asked)
     near, near_y = hold(near, near_y)
-    turned = moved(first, (0, 0, 2), (1, 1, 2))
-    far_x = moved(first, (1, 1, 1))
-    far_both = moved(turned, (1, 1, 1))
-    pieces = [(0, own, 8, near), (1, near, 9, far_x), (2, near_y, 10, turned), (3, turned, 11, far_both)]
+    turned = moved(first, (0, 0, 2), (1, 1, 1))
+    far_y = moved(first, (1, 1, 2))
+    far_both = moved(turned, (1, 1, 2))
+    pieces = [(0, own, 8, near), (1, near, 9, turned), (2, near_y, 10, far_y), (3, turned, 11, far_both)]
     for level in range(16, groups, 16):
         base = moved(own, (0, 0, level), (1, 1, level ^ 8))
         by_x, by_y = (moved(base, (0, 0, bit), (1, 1, bit)) for bit in (1, 2))

time: 88.5 us -> 86.3 us (0.975)
  waiting for transfers between devices: 38.5 us -> 34.6 us
  starting transfers between devices: 23.1 us -> 24.9 us
    ppermute x9, waiting for transfers between devices: 25.4 us -> 13.2 us  [moved(): return lax.ppermute(block, ('dp', 'mp'), route)]
    all_to_all x1, waiting for transfers between devices: 0.01 us -> 8.61 us  [local(): lax.all_to_all(held[0], 'mp', split_axis=0, concat_axis=0, tiled=True)]
    ppermute x9, starting transfers between devices: 13.5 us -> 15.3 us  [moved(): return lax.ppermute(block, ('dp', 'mp'), route)]
  transfers between devices with their start and end apart: 18 -> 18, of which waited for: 11 -> 12; matrix products, arithmetic and copies ran while one was open for 1% -> 1% of each run, Pallas kernels for 7% -> 7%
where the time goes in v4:
time: 86.3 us; the launch traced here: 85.9 us
  waiting for transfers between devices  34.6 us (40%)
  starting transfers between devices  24.9 us (29%)
  blocking collectives  12.2 us (14%)
  Pallas kernels  9.19 us (11%)
  local copies, waits for them, and re-layouts  2.75 us (3%)
  other arithmetic  1.43 us (2%)
    ppermute x9, starting transfers between devices, moved(): return lax.ppermute(block, ('dp', 'mp'), route)  15.3 us
    ppermute x9, waiting for transfers between devices, moved(): return lax.ppermute(block, ('dp', 'mp'), route)  13.2 us
    ppermute x8, waiting for transfers between devices, flipped(): lax.ppermute(block, axis, [(i, i ^ mask) for i in range(lax.axis_size(axi...  12.8 us
    all_to_all x1, blocking collectives, local(): lax.all_to_all(message, 'mp', split_axis=0, concat_axis=0, tiled=True)  12.2 us
    pallas_call x9, Pallas kernels, kernel_call(): pl.pallas_call(body, out_shape=out_shape, in_specs=[pl.BlockSpec(memory_s...  9.19 us
    all_to_all x1, waiting for transfers between devices, local(): lax.all_to_all(held[0], 'mp', split_axis=0, concat_axis=0, tiled=True)  8.61 us
    ppermute x8, starting transfers between devices, flipped(): lax.ppermute(block, axis, [(i, i ^ mask) for i in range(lax.axis_size(axi...  5.32 us
    all_to_all x1, starting transfers between devices, local(): lax.all_to_all(held[0], 'mp', split_axis=0, concat_axis=0, tiled=True)  4.22 us
  transfers between devices with their start and end apart: 18, of which 12 were waited for; matrix products, arithmetic and copies ran while one was open for 1% of the time, Pallas kernels for 7%

profile of v4, /device:TPU:0, one launch (start us, length us, event | category | flops | bytes accessed | tf_op | source)
XLA Modules:
  0.0 85.9 jit_solution(7281054541409357899)
XLA Ops:
  0.6 1.0 %constant_dynamic-update-slice_fusion.1 = bf16[384,768]{1,0:T(8,128)(2,1)S(1)} fusion(bf16[192,768]{1,0:T(8,128)(2,1)} %param.16), kind=kLoop, calls=%fused_computation.6 | loop fusion | bytes 589824
  1.8 3.0 %collective-permute-start = (bf16[384,768]{1,0:T(8,128)(2,1)S(1)}, bf16[384,768]{1,0:T(8,128)(2,1)S(1)}, u32[]{:S(2)}, u32[]{:S(2)}) collective-permute-start(bf16[384,768]{1,0:T(8,128)(2,1)S(1)} %constant_dynamic-update-slice_fusion.refs_0_), channel_id=1, source_target_pairs={{1,0},{0,1},{3,2},{2,3},{5,4},{4,5},{7,6},{6,7},{9,8},{8,9},{11,10... | collective-permute-start | bytes 1769480 | tf_op jit(solution)/shard_map/ppermute | solution.py:30
  5.2 3.4 %collective-permute-start.1 = (bf16[384,768]{1,0:T(8,128)(2,1)S(1)}, bf16[384,768]{1,0:T(8,128)(2,1)S(1)}, u32[]{:S(2)}, u32[]{:S(2)}) collective-permute-start(bf16[384,768]{1,0:T(8,128)(2,1)S(1)} %constant_dynamic-update-slice_fusion.refs_0_), channel_id=1, source_target_pairs={{2,0},{3,1},{0,2},{1,3},{6,4},{7,5},{4,6},{5,7},{10,8},{11,9},{8,1... | collective-permute-start | bytes 1769480 | tf_op jit(solution)/shard_map/ppermute | solution.py:30
  8.6 12.2 %all_to_all.16.message_ref = f32[16,1,256]{2,1,0:T(1,128)S(1)} all-to-all(f32[16,1,256]{2,1,0:T(1,128)S(1)} %shard_map.138), channel_id=1, replica_groups=mesh['dp'=2,'mp'=16] {'mp'}, dimensions={0} | all-to-all | bytes 32768 | tf_op jit(solution)/shard_map/all_to_all | solution.py:265
  22.3 1.3 %shard_map.140 = bf16[256,768]{1,0:T(8,128)(2,1)} custom-call(f32[16,1,256]{2,1,0:T(1,128)S(1)} %all_to_all.16.message_ref, bf16[256,768]{1,0:T(8,128)(2,1)S(1)} %copy-done.3), custom_call_target="tpu_custom_call" | custom-call | tf_op jit(solution)/shard_map/pallas_call | solution.py:38
  23.6 4.2 %all-to-all-start.1 = ((bf16[16,16,768]{2,1,0:T(8,128)(2,1)}), bf16[16,16,768]{2,1,0:T(8,128)(2,1)}, u32[]{:S(2)}, u32[]{:S(2)}) async-start(bf16[16,16,768]{2,1,0:T(8,128)(2,1)} %bitcast.3), calls=%async_computation.1 | async-start | bytes 786432 | tf_op jit(solution)/shard_map/all_to_all | solution.py:291
  28.5 2.2 %collective-permute-done.3.refs_2_ = bf16[384,768]{1,0:T(8,128)(2,1)S(1)} collective-permute-done((bf16[384,768]{1,0:T(8,128)(2,1)S(1)}, bf16[384,768]{1,0:T(8,128)(2,1)S(1)}, u32[]{:S(2)}, u32[]{:S(2)}) %collective-permute-start.3) | collective-permute-done | bytes 589856 | tf_op jit(solution)/shard_map/ppermute | solution.py:30
  31.4 8.6 %all-to-all-done.1 = bf16[16,16,768]{2,1,0:T(8,128)(2,1)} async-done(((bf16[16,16,768]{2,1,0:T(8,128)(2,1)}), bf16[16,16,768]{2,1,0:T(8,128)(2,1)}, u32[]{:S(2)}, u32[]{:S(2)}) %all-to-all-start.1) | async-done | bytes 393248 | tf_op jit(solution)/shard_map/all_to_all | solution.py:291
  40.0 0.9 %copy-done.1 = bf16[144,768]{1,0:T(8,128)(2,1)S(1)} copy-done((bf16[144,768]{1,0:T(8,128)(2,1)S(1)}, bf16[144,768]{1,0:T(8,128)(2,1)}, u32[]{:S(2)}) %copy-start.1) | copy-done | bytes 221208
  40.9 1.4 %shard_map.141 = (f32[128,768]{1,0:T(8,128)S(1)}, bf16[128,768]{1,0:T(8,128)(2,1)S(1)}, s32[1,128]{1,0:T(1,128)S(1)}) custom-call(bf16[144,768]{1,0:T(8,128)(2,1)S(1)} %copy-done.1, bf16[256,768]{1,0:T(8,128)(2,1)} %bitcast.4.fetched_ref), custom_call_target="tpu_custom_call" | custom-call | tf_op jit(solution)/shard_map/pallas_call | solution.py:38
  42.4 1.5 %collective-permute-start.2 = (bf16[128,768]{1,0:T(8,128)(2,1)S(1)}, bf16[128,768]{1,0:T(8,128)(2,1)S(1)}, u32[]{:S(2)}, u32[]{:S(2)}) collective-permute-start(bf16[128,768]{1,0:T(8,128)(2,1)S(1)} %get-tuple-element.30.normed_ref), channel_id=1, source_target_pairs={{0,16},{16,0},{1,17},{17,1},{2,18},{18,2},{3,19},{19,3},{4,20},{20... | collective-permute-start | bytes 589832 | tf_op jit(solution)/shard_map/ppermute | solution.py:19
  43.9 1.4 %collective-permute-start.7 = (bf16[128,768]{1,0:T(8,128)(2,1)S(1)}, bf16[128,768]{1,0:T(8,128)(2,1)S(1)}, u32[]{:S(2)}, u32[]{:S(2)}) collective-permute-start(bf16[128,768]{1,0:T(8,128)(2,1)S(1)} %get-tuple-element.30.normed_ref), channel_id=1, source_target_pairs={{0,4},{1,5},{2,6},{3,7},{4,0},{5,1},{6,2},{7,3},{8,12},{9,13},{10,... | collective-permute-start | bytes 589832 | tf_op jit(solution)/shard_map/ppermute | solution.py:19
  45.3 1.9 %shard_map.142 = (f32[128,768]{1,0:T(8,128)S(1)}, f32[128,768]{1,0:T(8,128)S(1)}) custom-call(bf16[128,768]{1,0:T(8,128)(2,1)S(1)} %get-tuple-element.30.normed_ref, bf16[128,768]{1,0:T(8,128)(2,1)S(1)} %collective-permute-done.2.normed2_ref, f32[16,1,256]{2,1,0:T(1,128)S(1)} %all_to_all.16.message_ref, ...), custom_call_target="tpu_custom_call" | custom-call | tf_op jit(solution)/shard_map/pallas_call | solution.py:38
  47.2 3.5 %collective-permute-done.7.normed_ref = bf16[128,768]{1,0:T(8,128)(2,1)S(1)} collective-permute-done((bf16[128,768]{1,0:T(8,128)(2,1)S(1)}, bf16[128,768]{1,0:T(8,128)(2,1)S(1)}, u32[]{:S(2)}, u32[]{:S(2)}) %collective-permute-start.7) | collective-permute-done | bytes 196640 | tf_op jit(solution)/shard_map/ppermute | solution.py:19
  50.8 1.4 %collective-permute-done.8.normed2_ref = bf16[128,768]{1,0:T(8,128)(2,1)S(1)} collective-permute-done((bf16[128,768]{1,0:T(8,128)(2,1)S(1)}, bf16[128,768]{1,0:T(8,128)(2,1)S(1)}, u32[]{:S(2)}, u32[]{:S(2)}) %collective-permute-start.8) | collective-permute-done | bytes 196640 | tf_op jit(solution)/shard_map/ppermute | solution.py:19
  52.2 1.9 %shard_map.143 = (f32[128,768]{1,0:T(8,128)S(1)}, f32[128,768]{1,0:T(8,128)S(1)}) custom-call(bf16[128,768]{1,0:T(8,128)(2,1)S(1)} %collective-permute-done.7.normed_ref, bf16[128,768]{1,0:T(8,128)(2,1)S(1)} %collective-permute-done.8.normed2_ref, f32[16,1,256]{2,1,0:T(1,128)S(1)} %all_to_all.16.message_ref, ...), custom_call_target="tpu_custom_call" | custom-call | tf_op jit(solution)/shard_map/pallas_call | solution.py:38
  54.7 1.2 %collective-permute-done.9.received_ref = f32[128,768]{1,0:T(8,128)S(1)} collective-permute-done((f32[128,768]{1,0:T(8,128)S(1)}, f32[128,768]{1,0:T(8,128)S(1)}, u32[]{:S(2)}, u32[]{:S(2)}) %collective-permute-start.9) | collective-permute-done | bytes 393248 | tf_op jit(solution)/shard_map/ppermute | solution.py:19
  55.9 1.7 %collective-permute-start.10 = (bf16[128,768]{1,0:T(8,128)(2,1)S(1)}, bf16[128,768]{1,0:T(8,128)(2,1)S(1)}, u32[]{:S(2)}, u32[]{:S(2)}) collective-permute-start(bf16[128,768]{1,0:T(8,128)(2,1)S(1)} %shard_map.144), channel_id=1, source_target_pairs={{0,4},{1,5},{2,6},{3,7},{4,0},{5,1},{6,2},{7,3},{8,12},{9,13},{10,... | collective-permute-start | bytes 589832 | tf_op jit(solution)/shard_map/ppermute | solution.py:19
  57.7 1.2 %collective-permute-done.11.refs_1_ = bf16[64,768]{1,0:T(8,128)(2,1)S(1)} collective-permute-done((bf16[64,768]{1,0:T(8,128)(2,1)S(1)}, bf16[64,768]{1,0:T(8,128)(2,1)S(1)}, u32[]{:S(2)}, u32[]{:S(2)}) %collective-permute-start.11) | collective-permute-done | bytes 98336 | tf_op jit(solution)/shard_map/ppermute | solution.py:19
  58.9 4.1 %collective-permute-done.10.other_ref = bf16[128,768]{1,0:T(8,128)(2,1)S(1)} collective-permute-done((bf16[128,768]{1,0:T(8,128)(2,1)S(1)}, bf16[128,768]{1,0:T(8,128)(2,1)S(1)}, u32[]{:S(2)}, u32[]{:S(2)}) %collective-permute-start.10) | collective-permute-done | bytes 196640 | tf_op jit(solution)/shard_map/ppermute | solution.py:19
  63.1 1.1 %shard_map.145 = (bf16[128,768]{1,0:T(8,128)(2,1)}, f32[128,1]{1,0:T(8,128)S(1)}, bf16[128,128]{1,0:T(8,128)(2,1)S(1)}, bf16[64,768]{1,0:T(8,128)(2,1)S(1)}, bf16[64,768]{1,0:T(8,128)(2,1)S(1)}) custom-call(f32[128,768]{1,0:T(8,128)S(1)} %get-tuple-element.29.shifted_ref, f32[128,768]{1,0:T(8,128)S(1)} %get-tuple-element.34.total_ref, ...), custom_call_target="tpu_custom_call" | custom-call | tf_op jit(solution)/shard_map/pallas_call | solution.py:38
  64.2 1.3 %collective-permute-done.12 = bf16[64,768]{1,0:T(8,128)(2,1)S(1)} collective-permute-done((bf16[64,768]{1,0:T(8,128)(2,1)S(1)}, bf16[64,768]{1,0:T(8,128)(2,1)S(1)}, u32[]{:S(2)}, u32[]{:S(2)}) %collective-permute-start.12) | collective-permute-done | bytes 98336 | tf_op jit(solution)/shard_map/ppermute | solution.py:19
  65.5 1.3 %collective-permute-start.13 = (bf16[64,768]{1,0:T(8,128)(2,1)S(1)}, bf16[64,768]{1,0:T(8,128)(2,1)S(1)}, u32[]{:S(2)}, u32[]{:S(2)}) collective-permute-start(bf16[64,768]{1,0:T(8,128)(2,1)S(1)} %add_convert_fusion.3), channel_id=1, source_target_pairs={{1,0},{0,1},{3,2},{2,3},{5,4},{4,5},{7,6},{6,7},{9,8},{8,9},{11,10... | collective-permute-start | bytes 294920 | tf_op jit(solution)/shard_map/ppermute | solution.py:30
  66.8 3.4 %collective-permute-done.13 = bf16[64,768]{1,0:T(8,128)(2,1)S(1)} collective-permute-done((bf16[64,768]{1,0:T(8,128)(2,1)S(1)}, bf16[64,768]{1,0:T(8,128)(2,1)S(1)}, u32[]{:S(2)}, u32[]{:S(2)}) %collective-permute-start.13) | collective-permute-done | bytes 98336 | tf_op jit(solution)/shard_map/ppermute | solution.py:30
  70.2 1.4 %collective-permute-start.14 = (bf16[64,768]{1,0:T(8,128)(2,1)S(1)}, bf16[64,768]{1,0:T(8,128)(2,1)S(1)}, u32[]{:S(2)}, u32[]{:S(2)}) collective-permute-start(bf16[64,768]{1,0:T(8,128)(2,1)S(1)} %add_convert_fusion.2), channel_id=1, source_target_pairs={{2,0},{3,1},{0,2},{1,3},{6,4},{7,5},{4,6},{5,7},{10,8},{11,9},{8,1... | collective-permute-start | bytes 294920 | tf_op jit(solution)/shard_map/ppermute | solution.py:30
  71.6 3.3 %collective-permute-done.14 = bf16[64,768]{1,0:T(8,128)(2,1)S(1)} collective-permute-done((bf16[64,768]{1,0:T(8,128)(2,1)S(1)}, bf16[64,768]{1,0:T(8,128)(2,1)S(1)}, u32[]{:S(2)}, u32[]{:S(2)}) %collective-permute-start.14) | collective-permute-done | bytes 98336 | tf_op jit(solution)/shard_map/ppermute | solution.py:30
  74.9 1.8 %collective-permute-start.15 = (bf16[64,768]{1,0:T(8,128)(2,1)S(1)}, bf16[64,768]{1,0:T(8,128)(2,1)S(1)}, u32[]{:S(2)}, u32[]{:S(2)}) collective-permute-start(bf16[64,768]{1,0:T(8,128)(2,1)S(1)} %add_convert_fusion.1), channel_id=1, source_target_pairs={{4,0},{5,1},{6,2},{7,3},{0,4},{1,5},{2,6},{3,7},{12,8},{13,9},{14,... | collective-permute-start | bytes 294920 | tf_op jit(solution)/shard_map/ppermute | solution.py:30
  76.7 2.9 %collective-permute-done.15 = bf16[64,768]{1,0:T(8,128)(2,1)S(1)} collective-permute-done((bf16[64,768]{1,0:T(8,128)(2,1)S(1)}, bf16[64,768]{1,0:T(8,128)(2,1)S(1)}, u32[]{:S(2)}, u32[]{:S(2)}) %collective-permute-start.15) | collective-permute-done | bytes 98336 | tf_op jit(solution)/shard_map/ppermute | solution.py:30
  79.6 2.4 %collective-permute-start.16 = (bf16[64,768]{1,0:T(8,128)(2,1)S(1)}, bf16[64,768]{1,0:T(8,128)(2,1)S(1)}, u32[]{:S(2)}, u32[]{:S(2)}) collective-permute-start(bf16[64,768]{1,0:T(8,128)(2,1)S(1)} %add_convert_fusion), channel_id=1, source_target_pairs={{8,0},{9,1},{10,2},{11,3},{12,4},{13,5},{14,6},{15,7},{0,8},{1,9},... | collective-permute-start | bytes 294920 | tf_op jit(solution)/shard_map/ppermute | solution.py:30
  82.7 1.0 %shard_map.146 = f32[128,768]{1,0:T(8,128)} custom-call(bf16[128,128]{1,0:T(8,128)(2,1)S(1)} %get-tuple-element.43.weights_ref, bf16[64,768]{1,0:T(8,128)(2,1)S(1)} %copy-done.2, bf16[64,768]{1,0:T(8,128)(2,1)S(1)} %collective-permute-done.11.refs_1_), custom_call_target="tpu_custom_call" | custom-call | tf_op jit(solution)/shard_map/pallas_call | solution.py:38
  83.7 1.5 %collective-permute-done.16 = bf16[64,768]{1,0:T(8,128)(2,1)S(1)} collective-permute-done((bf16[64,768]{1,0:T(8,128)(2,1)S(1)}, bf16[64,768]{1,0:T(8,128)(2,1)S(1)}, u32[]{:S(2)}, u32[]{:S(2)}) %collective-permute-start.16) | collective-permute-done | bytes 98336 | tf_op jit(solution)/shard_map/ppermute | solution.py:30
  85.2 0.7 add_multiply_fusion
  (49 shorter events, 4.7 us)
Async XLA Ops:
  0.6 1.1 %copy-start.8 = (bf16[192,768]{1,0:T(8,128)(2,1)S(1)}, bf16[192,768]{1,0:T(8,128)(2,1)}, u32[]{:S(2)}) copy-start(bf16[192,768]{1,0:T(8,128)(2,1)} %param.18) | copy-start | bytes 884740
  1.7 3.1 %copy-start.11 = (bf16[192]{0:T(256)(128)(2,1)S(1)}, bf16[192]{0:T(256)(128)(2,1)}, u32[]{:S(2)}) copy-start(bf16[192]{0:T(256)(128)(2,1)} %param.17) | copy-start | bytes 1156
  1.7 3.1 %copy-start.5 = (s32[128,1]{0,1:T(1,128)S(1)}, s32[128,1]{0,1:T(1,128)}, u32[]{:S(2)}) copy-start(s32[128,1]{0,1:T(1,128)} %param.12) | copy-start | bytes 1540
  1.7 3.1 %copy-start.7 = (s32[128]{0:T(128)S(1)}, s32[128]{0:T(128)}, u32[]{:S(2)}) copy-start(s32[128]{0:T(128)} %param.13) | copy-start | bytes 1540
  1.7 19.7 %copy-start.9 = (bf16[768]{0:T(1024)(128)(2,1)S(1)}, bf16[768]{0:T(1024)(128)(2,1)}, u32[]{:S(2)}) copy-start(bf16[768]{0:T(1024)(128)(2,1)} %param.15) | copy-start | bytes 4612
  1.7 19.7 %copy-start.10 = (bf16[768]{0:T(1024)(128)(2,1)S(1)}, bf16[768]{0:T(1024)(128)(2,1)}, u32[]{:S(2)}) copy-start(bf16[768]{0:T(1024)(128)(2,1)} %param.19) | copy-start | bytes 4612
  1.7 19.7 %copy-start.4 = (bf16[128,768]{1,0:T(8,128)(2,1)S(1)}, bf16[128,768]{1,0:T(8,128)(2,1)}, u32[]{:S(2)}) copy-start(bf16[128,768]{1,0:T(8,128)(2,1)} %queries_ref.1) | copy-start | bytes 589828
  1.8 19.7 %copy-start.6 = (s32[128]{0:T(128)S(1)}, s32[128]{0:T(128)}, u32[]{:S(2)}) copy-start(s32[128]{0:T(128)} %param.21) | copy-start | bytes 1540
  1.8 20.5 %copy-start.3 = (bf16[256,768]{1,0:T(8,128)(2,1)S(1)}, bf16[256,768]{1,0:T(8,128)(2,1)}, u32[]{:S(2)}) copy-start(bf16[256,768]{1,0:T(8,128)(2,1)} %table_ref.1) | copy-start | bytes 1179652
  1.8 19.0 %collective-permute-start = (bf16[384,768]{1,0:T(8,128)(2,1)S(1)}, bf16[384,768]{1,0:T(8,128)(2,1)S(1)}, u32[]{:S(2)}, u32[]{:S(2)}) collective-permute-start(bf16[384,768]{1,0:T(8,128)(2,1)S(1)} %constant_dynamic-update-slice_fusion.refs_0_), channel_id=1, source_target_pairs={{1,0},{0,1},{3,2},{2,3},{5,4},{4,5},{7,6},{6,7},{9,8},{8,9},{11,10... | collective-permute-start | bytes 1769480 | tf_op jit(solution)/shard_map/ppermute | solution.py:30
  5.2 18.4 %collective-permute-start.1 = (bf16[384,768]{1,0:T(8,128)(2,1)S(1)}, bf16[384,768]{1,0:T(8,128)(2,1)S(1)}, u32[]{:S(2)}, u32[]{:S(2)}) collective-permute-start(bf16[384,768]{1,0:T(8,128)(2,1)S(1)} %constant_dynamic-update-slice_fusion.refs_0_), channel_id=1, source_target_pairs={{2,0},{3,1},{0,2},{1,3},{6,4},{7,5},{4,6},{5,7},{10,8},{11,9},{8,1... | collective-permute-start | bytes 1769480 | tf_op jit(solution)/shard_map/ppermute | solution.py:30
  20.8 9.9 %collective-permute-start.3 = (bf16[384,768]{1,0:T(8,128)(2,1)S(1)}, bf16[384,768]{1,0:T(8,128)(2,1)S(1)}, u32[]{:S(2)}, u32[]{:S(2)}) collective-permute-start(bf16[384,768]{1,0:T(8,128)(2,1)S(1)} %collective-permute-done.refs_1_), channel_id=1, source_target_pairs={{2,0},{3,1},{0,2},{1,3},{6,4},{7,5},{4,6},{5,7},{10,8},{11,9},{8,1... | collective-permute-start | bytes 1769480 | tf_op jit(solution)/shard_map/ppermute | solution.py:30
  21.6 0.7 copy-start
  23.6 16.4 %all-to-all-start.1 = ((bf16[16,16,768]{2,1,0:T(8,128)(2,1)}), bf16[16,16,768]{2,1,0:T(8,128)(2,1)}, u32[]{:S(2)}, u32[]{:S(2)}) async-start(bf16[16,16,768]{2,1,0:T(8,128)(2,1)} %bitcast.3), calls=%async_computation.1 | async-start | bytes 786432 | tf_op jit(solution)/shard_map/all_to_all | solution.py:291
  27.8 17.5 %collective-permute-start.4 = (bf16[384,768]{1,0:T(8,128)(2,1)S(1)}, bf16[384,768]{1,0:T(8,128)(2,1)S(1)}, u32[]{:S(2)}, u32[]{:S(2)}) collective-permute-start(bf16[384,768]{1,0:T(8,128)(2,1)S(1)} %collective-permute-done.refs_1_), channel_id=1, source_target_pairs={{18,16},{19,17},{16,18},{17,19},{22,20},{23,21},{20,22},{21,23},{2... | collective-permute-start | bytes 1769480 | tf_op jit(solution)/shard_map/ppermute | solution.py:30
  30.7 14.6 %collective-permute-start.5 = (bf16[384,768]{1,0:T(8,128)(2,1)S(1)}, bf16[384,768]{1,0:T(8,128)(2,1)S(1)}, u32[]{:S(2)}, u32[]{:S(2)}) collective-permute-start(bf16[384,768]{1,0:T(8,128)(2,1)S(1)} %collective-permute-done.3.refs_2_), channel_id=1, source_target_pairs={{18,16},{19,17},{16,18},{17,19},{22,20},{23,21},{20,22},{21,23},{2... | collective-permute-start | bytes 1769480 | tf_op jit(solution)/shard_map/ppermute | solution.py:30
  40.0 0.9 %copy-start.1 = (bf16[144,768]{1,0:T(8,128)(2,1)S(1)}, bf16[144,768]{1,0:T(8,128)(2,1)}, u32[]{:S(2)}) copy-start(bf16[144,768]{1,0:T(8,128)(2,1)} %copy-done) | copy-start | bytes 663556
  42.4 2.9 %collective-permute-start.2 = (bf16[128,768]{1,0:T(8,128)(2,1)S(1)}, bf16[128,768]{1,0:T(8,128)(2,1)S(1)}, u32[]{:S(2)}, u32[]{:S(2)}) collective-permute-start(bf16[128,768]{1,0:T(8,128)(2,1)S(1)} %get-tuple-element.30.normed_ref), channel_id=1, source_target_pairs={{0,16},{16,0},{1,17},{17,1},{2,18},{18,2},{3,19},{19,3},{4,20},{20... | collective-permute-start | bytes 589832 | tf_op jit(solution)/shard_map/ppermute | solution.py:19
  43.9 6.9 %collective-permute-start.7 = (bf16[128,768]{1,0:T(8,128)(2,1)S(1)}, bf16[128,768]{1,0:T(8,128)(2,1)S(1)}, u32[]{:S(2)}, u32[]{:S(2)}) collective-permute-start(bf16[128,768]{1,0:T(8,128)(2,1)S(1)} %get-tuple-element.30.normed_ref), channel_id=1, source_target_pairs={{0,4},{1,5},{2,6},{3,7},{4,0},{5,1},{6,2},{7,3},{8,12},{9,13},{10,... | collective-permute-start | bytes 589832 | tf_op jit(solution)/shard_map/ppermute | solution.py:19
  50.7 1.4 %collective-permute-start.8 = (bf16[128,768]{1,0:T(8,128)(2,1)S(1)}, bf16[128,768]{1,0:T(8,128)(2,1)S(1)}, u32[]{:S(2)}, u32[]{:S(2)}) collective-permute-start(bf16[128,768]{1,0:T(8,128)(2,1)S(1)} %collective-permute-done.7.normed_ref), channel_id=1, source_target_pairs={{0,16},{16,0},{1,17},{17,1},{2,18},{18,2},{3,19},{19,3},{4,20},{20... | collective-permute-start | bytes 589832 | tf_op jit(solution)/shard_map/ppermute | solution.py:19
  54.1 1.8 %collective-permute-start.9 = (f32[128,768]{1,0:T(8,128)S(1)}, f32[128,768]{1,0:T(8,128)S(1)}, u32[]{:S(2)}, u32[]{:S(2)}) collective-permute-start(f32[128,768]{1,0:T(8,128)S(1)} %get-tuple-element.38), channel_id=1, source_target_pairs={{0,16},{16,0},{1,17},{17,1},{2,18},{18,2},{3,19},{19,3},{4,20},{20... | collective-permute-start | bytes 1179656 | tf_op jit(solution)/shard_map/ppermute | solution.py:19
  54.3 4.7 %collective-permute-start.6 = (f32[128,768]{1,0:T(8,128)S(1)}, f32[128,768]{1,0:T(8,128)S(1)}, u32[]{:S(2)}, u32[]{:S(2)}) collective-permute-start(f32[128,768]{1,0:T(8,128)S(1)} %get-tuple-element.35), channel_id=1, source_target_pairs={{0,16},{16,0},{1,17},{17,1},{2,18},{18,2},{3,19},{19,3},{4,20},{20... | collective-permute-start | bytes 1179656 | tf_op jit(solution)/shard_map/ppermute | solution.py:19
  55.9 1.8 %copy-start.2 = (bf16[64,768]{1,0:T(8,128)(2,1)S(1)}, bf16[64,768]{1,0:T(8,128)(2,1)}, u32[]{:S(2)}) copy-start(bf16[64,768]{1,0:T(8,128)(2,1)} %refs_0_.3) | copy-start | bytes 294916
  55.9 7.1 %collective-permute-start.10 = (bf16[128,768]{1,0:T(8,128)(2,1)S(1)}, bf16[128,768]{1,0:T(8,128)(2,1)S(1)}, u32[]{:S(2)}, u32[]{:S(2)}) collective-permute-start(bf16[128,768]{1,0:T(8,128)(2,1)S(1)} %shard_map.144), channel_id=1, source_target_pairs={{0,4},{1,5},{2,6},{3,7},{4,0},{5,1},{6,2},{7,3},{8,12},{9,13},{10,... | collective-permute-start | bytes 589832 | tf_op jit(solution)/shard_map/ppermute | solution.py:19
  57.6 1.3 %collective-permute-start.11 = (bf16[64,768]{1,0:T(8,128)(2,1)S(1)}, bf16[64,768]{1,0:T(8,128)(2,1)S(1)}, u32[]{:S(2)}, u32[]{:S(2)}) collective-permute-start(bf16[64,768]{1,0:T(8,128)(2,1)S(1)} %copy-done.2), channel_id=1, source_target_pairs={{0,16},{16,0},{1,17},{17,1},{2,18},{18,2},{3,19},{19,3},{4,20},{20... | collective-permute-start | bytes 294920 | tf_op jit(solution)/shard_map/ppermute | solution.py:19
  64.2 1.3 %collective-permute-start.12 = (bf16[64,768]{1,0:T(8,128)(2,1)S(1)}, bf16[64,768]{1,0:T(8,128)(2,1)S(1)}, u32[]{:S(2)}, u32[]{:S(2)}) collective-permute-start(bf16[64,768]{1,0:T(8,128)(2,1)S(1)} %get-tuple-element.45), channel_id=1, source_target_pairs={{0,16},{16,0},{1,17},{17,1},{2,18},{18,2},{3,19},{19,3},{4,20},{20... | collective-permute-start | bytes 294920 | tf_op jit(solution)/shard_map/ppermute | solution.py:19
  65.5 4.7 %collective-permute-start.13 = (bf16[64,768]{1,0:T(8,128)(2,1)S(1)}, bf16[64,768]{1,0:T(8,128)(2,1)S(1)}, u32[]{:S(2)}, u32[]{:S(2)}) collective-permute-start(bf16[64,768]{1,0:T(8,128)(2,1)S(1)} %add_convert_fusion.3), channel_id=1, source_target_pairs={{1,0},{0,1},{3,2},{2,3},{5,4},{4,5},{7,6},{6,7},{9,8},{8,9},{11,10... | collective-permute-start | bytes 294920 | tf_op jit(solution)/shard_map/ppermute | solution.py:30
  70.2 4.7 %collective-permute-start.14 = (bf16[64,768]{1,0:T(8,128)(2,1)S(1)}, bf16[64,768]{1,0:T(8,128)(2,1)S(1)}, u32[]{:S(2)}, u32[]{:S(2)}) collective-permute-start(bf16[64,768]{1,0:T(8,128)(2,1)S(1)} %add_convert_fusion.2), channel_id=1, source_target_pairs={{2,0},{3,1},{0,2},{1,3},{6,4},{7,5},{4,6},{5,7},{10,8},{11,9},{8,1... | collective-permute-start | bytes 294920 | tf_op jit(solution)/shard_map/ppermute | solution.py:30
  74.9 4.7 %collective-permute-start.15 = (bf16[64,768]{1,0:T(8,128)(2,1)S(1)}, bf16[64,768]{1,0:T(8,128)(2,1)S(1)}, u32[]{:S(2)}, u32[]{:S(2)}) collective-permute-start(bf16[64,768]{1,0:T(8,128)(2,1)S(1)} %add_convert_fusion.1), channel_id=1, source_target_pairs={{4,0},{5,1},{6,2},{7,3},{0,4},{1,5},{2,6},{3,7},{12,8},{13,9},{14,... | collective-permute-start | bytes 294920 | tf_op jit(solution)/shard_map/ppermute | solution.py:30
  79.6 5.6 %collective-permute-start.16 = (bf16[64,768]{1,0:T(8,128)(2,1)S(1)}, bf16[64,768]{1,0:T(8,128)(2,1)S(1)}, u32[]{:S(2)}, u32[]{:S(2)}) collective-permute-start(bf16[64,768]{1,0:T(8,128)(2,1)S(1)} %add_convert_fusion), channel_id=1, source_target_pairs={{8,0},{9,1},{10,2},{11,3},{12,4},{13,5},{14,6},{15,7},{0,8},{1,9},... | collective-permute-start | bytes 294920 | tf_op jit(solution)/shard_map/ppermute | solution.py:30

commit v5 on v4

--- a/solution.py
+++ b/solution.py
@@ -155,11 +155,11 @@
         copy(at, p, 1).wait()
     total = jnp.dot(activated, held_out[...], preferred_element_type=F32)
     total_ref[...] = total[:chains, :]
-    total2_ref[...] = total[chains:, :]
+    total2_ref[...] = total[chains:, :].astype(total2_ref.dtype)
 
 
 def add_body(total_ref, received_ref, sum_ref):
-    sum_ref[...] = (total_ref[...] + received_ref[...]).astype(sum_ref.dtype)
+    sum_ref[...] = (total_ref[...] + received_ref[...].astype(F32)).astype(sum_ref.dtype)
 
 
 def score_body(
@@ -201,8 +201,10 @@
         ).astype(BF16)
 
 
-def query_grad_body(weights_ref, *refs):
-    tool_refs, grad_ref = refs[:-1], refs[-1]
+def finish_body(weights_ref, updated_ref, loss_ref, *refs):
+    tool_refs, (grad_ref, result_ref, chain_loss_ref) = refs[:-3], refs[-3:]
+    result_ref[...] = updated_ref[...]
+    chain_loss_ref[...] = loss_ref[...]
     block_rows = tool_refs[0].shape[0]
     grad_ref[...] = sum(
         jnp.dot(
@@ -263,20 +265,20 @@
         bias_in.reshape(1, units),
     )
     asked = lax.all_to_all(message, "mp", split_axis=0, concat_axis=0, tiled=True)
+    served = kernel_call(
+        functools.partial(serve_body, capacity, units),
+        whole((slots, features), BF16),
+        asked,
+        tool_table,
+    )
     packed = kernel_call(
         functools.partial(pack_body, capacity, groups),
         whole((chains + TILE_ROWS, features), BF16),
-        after(owner_row, message),
+        after(owner_row, served),
         positive.reshape(1, chains),
         norm_gain.reshape(1, features),
         bias_out.reshape(1, features),
         queries,
-    )
-    served = kernel_call(
-        functools.partial(serve_body, capacity, units),
-        whole((slots, features), BF16),
-        after(asked, packed),
-        tool_table,
     )
     own = jnp.concatenate([weight_in, weight_out], axis=0)
     own_later = after(own, message)
@@ -304,12 +306,12 @@
         fetched,
     )
 
-    def hidden(own_rows):
+    def hidden(own_rows, to_share, given):
         return kernel_call(
             functools.partial(hidden_body, plan),
-            (whole((chains, features), F32),) * 2,
+            (whole((chains, features), F32), whole((chains, features), given)),
             own_rows,
-            flipped(own_rows, "dp", 1),
+            flipped(to_share, "dp", 1),
             asked,
             *shards,
             in_place=range(3, 3 + len(shards)),
@@ -321,8 +323,9 @@
             vmem=LARGE_VMEM,
         )
 
-    total, total_for = hidden(normed)
-    neighbour, neighbour_for = hidden(after(flipped(normed, "mp", 4), total))
+    total, total_for = hidden(normed, after(normed, pieces[2][1]), F32)
+    neighbour_normed = after(flipped(normed, "mp", 4), total)
+    neighbour, neighbour_for = hidden(neighbour_normed, neighbour_normed, BF16)
     neighbour_sum = kernel_call(
         add_body, whole((chains, features), BF16), neighbour, flipped(neighbour_for, "dp", 1)
     )
@@ -343,7 +346,14 @@
         positive_row,
         *tools,
     )
-    query_grad = kernel_call(query_grad_body, whole((chains, features), F32), weights, *tools)
+    query_grad, updated, loss = kernel_call(
+        finish_body,
+        (whole((chains, features), F32), whole((chains, features), BF16), whole((chains, 1), F32)),
+        weights,
+        updated,
+        loss,
+        *tools,
+    )
 
     grad = grads[0].astype(F32)
     for block in range(1, cycle):

time: 86.3 us -> 85.6 us (level)
  local copies, waits for them, and re-layouts: 2.75 us -> 5.64 us
  starting transfers between devices: 24.9 us -> 22.8 us
  waiting for transfers between devices: 34.6 us -> 33.4 us
    all_to_all x1, waiting for transfers between devices: 8.61 us -> 5.52 us  [local(): lax.all_to_all(held[0], 'mp', split_axis=0, concat_axis=0, tiled=True)]
    unnamed x25, local copies, waits for them, and re-layouts: 2.72 us -> 4.92 us
    ppermute x9, waiting for transfers between devices: 13.2 us -> 15 us  [moved(): return lax.ppermute(block, ('dp', 'mp'), route)]
    ppermute x8, starting transfers between devices: 5.32 us -> 3.98 us  [flipped(): lax.ppermute(block, axis, [(i, i ^ mask) for i in range(lax.axis_size(axi...]
  transfers between devices with their start and end apart: 18 -> 18, of which waited for: 12 -> 12; matrix products, arithmetic and copies ran while one was open for 1% -> 2% of each run, Pallas kernels for 7% -> 7%
where the time goes in v5:
time: 85.6 us; the launch traced here: 85.2 us
  waiting for transfers between devices  33.4 us (39%)
  starting transfers between devices  22.8 us (27%)
  blocking collectives  12.2 us (14%)
  Pallas kernels  8.9 us (10%)
  local copies, waits for them, and re-layouts  5.64 us (7%)
  other arithmetic  1.43 us (2%)
    ppermute x9, waiting for transfers between devices, moved(): return lax.ppermute(block, ('dp', 'mp'), route)  15 us
    ppermute x9, starting transfers between devices, moved(): return lax.ppermute(block, ('dp', 'mp'), route)  14.6 us
    ppermute x8, waiting for transfers between devices, flipped(): lax.ppermute(block, axis, [(i, i ^ mask) for i in range(lax.axis_size(axi...  12.8 us
    all_to_all x1, blocking collectives, local(): lax.all_to_all(message, 'mp', split_axis=0, concat_axis=0, tiled=True)  12.2 us
    pallas_call x9, Pallas kernels, kernel_call(): pl.pallas_call(body, out_shape=out_shape, in_specs=[pl.BlockSpec(memory_s...  8.9 us
    all_to_all x1, waiting for transfers between devices, local(): lax.all_to_all(held[0], 'mp', split_axis=0, concat_axis=0, tiled=True)  5.52 us
    unnamed x25, local copies, waits for them, and re-layouts  4.92 us
    all_to_all x1, starting transfers between devices, local(): lax.all_to_all(held[0], 'mp', split_axis=0, concat_axis=0, tiled=True)  4.22 us
  transfers between devices with their start and end apart: 18, of which 12 were waited for; matrix products, arithmetic and copies ran while one was open for 2% of the time, Pallas kernels for 7%

profile of v5, /device:TPU:0, one launch (start us, length us, event | category | flops | bytes accessed | tf_op | source)
XLA Modules:
  0.0 85.2 jit_solution(3532475236195779199)
XLA Ops:
  0.6 1.0 %constant_dynamic-update-slice_fusion.1 = bf16[384,768]{1,0:T(8,128)(2,1)S(1)} fusion(bf16[192,768]{1,0:T(8,128)(2,1)} %param.16), kind=kLoop, calls=%fused_computation.6 | loop fusion | bytes 589824
  1.7 3.0 %collective-permute-start = (bf16[384,768]{1,0:T(8,128)(2,1)S(1)}, bf16[384,768]{1,0:T(8,128)(2,1)S(1)}, u32[]{:S(2)}, u32[]{:S(2)}) collective-permute-start(bf16[384,768]{1,0:T(8,128)(2,1)S(1)} %constant_dynamic-update-slice_fusion.refs_0_), channel_id=1, source_target_pairs={{1,0},{0,1},{3,2},{2,3},{5,4},{4,5},{7,6},{6,7},{9,8},{8,9},{11,10... | collective-permute-start | bytes 1769480 | tf_op jit(solution)/shard_map/ppermute | solution.py:30
  5.8 3.4 %collective-permute-start.1 = (bf16[384,768]{1,0:T(8,128)(2,1)S(1)}, bf16[384,768]{1,0:T(8,128)(2,1)S(1)}, u32[]{:S(2)}, u32[]{:S(2)}) collective-permute-start(bf16[384,768]{1,0:T(8,128)(2,1)S(1)} %constant_dynamic-update-slice_fusion.refs_0_), channel_id=1, source_target_pairs={{2,0},{3,1},{0,2},{1,3},{6,4},{7,5},{4,6},{5,7},{10,8},{11,9},{8,1... | collective-permute-start | bytes 1769480 | tf_op jit(solution)/shard_map/ppermute | solution.py:30
  9.2 12.2 %all_to_all.16.message_ref = f32[16,1,256]{2,1,0:T(1,128)S(1)} all-to-all(f32[16,1,256]{2,1,0:T(1,128)S(1)} %shard_map.138), channel_id=1, replica_groups=mesh['dp'=2,'mp'=16] {'mp'}, dimensions={0} | all-to-all | bytes 32768 | tf_op jit(solution)/shard_map/all_to_all | solution.py:267
  22.0 1.3 %shard_map.139 = bf16[256,768]{1,0:T(8,128)(2,1)} custom-call(f32[16,1,256]{2,1,0:T(1,128)S(1)} %all_to_all.16.message_ref, bf16[256,768]{1,0:T(8,128)(2,1)S(1)} %copy-done.2), custom_call_target="tpu_custom_call" | custom-call | tf_op jit(solution)/shard_map/pallas_call | solution.py:38
  23.3 4.2 %all-to-all-start.1 = ((bf16[16,16,768]{2,1,0:T(8,128)(2,1)}), bf16[16,16,768]{2,1,0:T(8,128)(2,1)}, u32[]{:S(2)}, u32[]{:S(2)}) async-start(bf16[16,16,768]{2,1,0:T(8,128)(2,1)} %bitcast.3), calls=%async_computation.1 | async-start | bytes 786432 | tf_op jit(solution)/shard_map/all_to_all | solution.py:293
  28.2 3.3 %collective-permute-done.3.refs_2_ = bf16[384,768]{1,0:T(8,128)(2,1)S(1)} collective-permute-done((bf16[384,768]{1,0:T(8,128)(2,1)S(1)}, bf16[384,768]{1,0:T(8,128)(2,1)S(1)}, u32[]{:S(2)}, u32[]{:S(2)}) %collective-permute-start.3) | collective-permute-done | bytes 589856 | tf_op jit(solution)/shard_map/ppermute | solution.py:30
  33.5 0.9 %copy-done.4 = bf16[128,768]{1,0:T(8,128)(2,1)S(1)} copy-done((bf16[128,768]{1,0:T(8,128)(2,1)S(1)}, bf16[128,768]{1,0:T(8,128)(2,1)}, u32[]{:S(2)}) %copy-start.4) | copy-done | bytes 196632
  35.3 5.5 %all-to-all-done.1 = bf16[16,16,768]{2,1,0:T(8,128)(2,1)} async-done(((bf16[16,16,768]{2,1,0:T(8,128)(2,1)}), bf16[16,16,768]{2,1,0:T(8,128)(2,1)}, u32[]{:S(2)}, u32[]{:S(2)}) %all-to-all-start.1) | async-done | bytes 393248 | tf_op jit(solution)/shard_map/all_to_all | solution.py:293
  40.8 0.9 %copy-done.1 = bf16[144,768]{1,0:T(8,128)(2,1)S(1)} copy-done((bf16[144,768]{1,0:T(8,128)(2,1)S(1)}, bf16[144,768]{1,0:T(8,128)(2,1)}, u32[]{:S(2)}) %copy-start.1) | copy-done | bytes 221208
  41.8 1.4 %shard_map.141 = (f32[128,768]{1,0:T(8,128)S(1)}, bf16[128,768]{1,0:T(8,128)(2,1)S(1)}, s32[1,128]{1,0:T(1,128)S(1)}) custom-call(bf16[144,768]{1,0:T(8,128)(2,1)S(1)} %copy-done.1, bf16[256,768]{1,0:T(8,128)(2,1)} %bitcast.4.fetched_ref), custom_call_target="tpu_custom_call" | custom-call | tf_op jit(solution)/shard_map/pallas_call | solution.py:38
  43.3 1.6 %collective-permute-start.7 = (bf16[128,768]{1,0:T(8,128)(2,1)S(1)}, bf16[128,768]{1,0:T(8,128)(2,1)S(1)}, u32[]{:S(2)}, u32[]{:S(2)}) collective-permute-start(bf16[128,768]{1,0:T(8,128)(2,1)S(1)} %get-tuple-element.34.normed_ref), channel_id=1, source_target_pairs={{0,4},{1,5},{2,6},{3,7},{4,0},{5,1},{6,2},{7,3},{8,12},{9,13},{10,... | collective-permute-start | bytes 589832 | tf_op jit(solution)/shard_map/ppermute | solution.py:19
  44.9 1.9 %shard_map.142 = (f32[128,768]{1,0:T(8,128)S(1)}, f32[128,768]{1,0:T(8,128)S(1)}) custom-call(bf16[128,768]{1,0:T(8,128)(2,1)S(1)} %get-tuple-element.34.normed_ref, bf16[128,768]{1,0:T(8,128)(2,1)S(1)} %collective-permute-done.2.normed2_ref, f32[16,1,256]{2,1,0:T(1,128)S(1)} %all_to_all.16.message_ref, ...), custom_call_target="tpu_custom_call" | custom-call | tf_op jit(solution)/shard_map/pallas_call | solution.py:38
  46.9 3.8 %collective-permute-done.7.normed_ref = bf16[128,768]{1,0:T(8,128)(2,1)S(1)} collective-permute-done((bf16[128,768]{1,0:T(8,128)(2,1)S(1)}, bf16[128,768]{1,0:T(8,128)(2,1)S(1)}, u32[]{:S(2)}, u32[]{:S(2)}) %collective-permute-start.7) | collective-permute-done | bytes 196640 | tf_op jit(solution)/shard_map/ppermute | solution.py:19
  50.6 1.4 %collective-permute-done.8.normed2_ref = bf16[128,768]{1,0:T(8,128)(2,1)S(1)} collective-permute-done((bf16[128,768]{1,0:T(8,128)(2,1)S(1)}, bf16[128,768]{1,0:T(8,128)(2,1)S(1)}, u32[]{:S(2)}, u32[]{:S(2)}) %collective-permute-start.8) | collective-permute-done | bytes 196640 | tf_op jit(solution)/shard_map/ppermute | solution.py:19
  52.1 1.9 %shard_map.143 = (f32[128,768]{1,0:T(8,128)S(1)}, bf16[128,768]{1,0:T(8,128)(2,1)S(1)}) custom-call(bf16[128,768]{1,0:T(8,128)(2,1)S(1)} %collective-permute-done.7.normed_ref, bf16[128,768]{1,0:T(8,128)(2,1)S(1)} %collective-permute-done.8.normed2_ref, f32[16,1,256]{2,1,0:T(1,128)S(1)} %all_to_all.16.message_ref, ...), custom_call_target="tpu_custom_call" | custom-call | tf_op jit(solution)/shard_map/pallas_call | solution.py:38
  54.5 0.9 %collective-permute-done.9.received_ref = bf16[128,768]{1,0:T(8,128)(2,1)S(1)} collective-permute-done((bf16[128,768]{1,0:T(8,128)(2,1)S(1)}, bf16[128,768]{1,0:T(8,128)(2,1)S(1)}, u32[]{:S(2)}, u32[]{:S(2)}) %collective-permute-start.9) | collective-permute-done | bytes 196640 | tf_op jit(solution)/shard_map/ppermute | solution.py:19
  55.5 1.6 %collective-permute-start.10 = (bf16[128,768]{1,0:T(8,128)(2,1)S(1)}, bf16[128,768]{1,0:T(8,128)(2,1)S(1)}, u32[]{:S(2)}, u32[]{:S(2)}) collective-permute-start(bf16[128,768]{1,0:T(8,128)(2,1)S(1)} %shard_map.144), channel_id=1, source_target_pairs={{0,4},{1,5},{2,6},{3,7},{4,0},{5,1},{6,2},{7,3},{8,12},{9,13},{10,... | collective-permute-start | bytes 589832 | tf_op jit(solution)/shard_map/ppermute | solution.py:19
  57.1 1.3 %collective-permute-done.11.refs_1_ = bf16[64,768]{1,0:T(8,128)(2,1)S(1)} collective-permute-done((bf16[64,768]{1,0:T(8,128)(2,1)S(1)}, bf16[64,768]{1,0:T(8,128)(2,1)S(1)}, u32[]{:S(2)}, u32[]{:S(2)}) %collective-permute-start.11) | collective-permute-done | bytes 98336 | tf_op jit(solution)/shard_map/ppermute | solution.py:19
  58.4 4.1 %collective-permute-done.10.other_ref = bf16[128,768]{1,0:T(8,128)(2,1)S(1)} collective-permute-done((bf16[128,768]{1,0:T(8,128)(2,1)S(1)}, bf16[128,768]{1,0:T(8,128)(2,1)S(1)}, u32[]{:S(2)}, u32[]{:S(2)}) %collective-permute-start.10) | collective-permute-done | bytes 196640 | tf_op jit(solution)/shard_map/ppermute | solution.py:19
  62.5 0.8 shard_map.145
  63.4 1.3 %collective-permute-done.12 = bf16[64,768]{1,0:T(8,128)(2,1)S(1)} collective-permute-done((bf16[64,768]{1,0:T(8,128)(2,1)S(1)}, bf16[64,768]{1,0:T(8,128)(2,1)S(1)}, u32[]{:S(2)}, u32[]{:S(2)}) %collective-permute-start.12) | collective-permute-done | bytes 98336 | tf_op jit(solution)/shard_map/ppermute | solution.py:19
  64.7 1.4 %collective-permute-start.13 = (bf16[64,768]{1,0:T(8,128)(2,1)S(1)}, bf16[64,768]{1,0:T(8,128)(2,1)S(1)}, u32[]{:S(2)}, u32[]{:S(2)}) collective-permute-start(bf16[64,768]{1,0:T(8,128)(2,1)S(1)} %add_convert_fusion.3), channel_id=1, source_target_pairs={{1,0},{0,1},{3,2},{2,3},{5,4},{4,5},{7,6},{6,7},{9,8},{8,9},{11,10... | collective-permute-start | bytes 294920 | tf_op jit(solution)/shard_map/ppermute | solution.py:30
  66.1 3.3 %collective-permute-done.13 = bf16[64,768]{1,0:T(8,128)(2,1)S(1)} collective-permute-done((bf16[64,768]{1,0:T(8,128)(2,1)S(1)}, bf16[64,768]{1,0:T(8,128)(2,1)S(1)}, u32[]{:S(2)}, u32[]{:S(2)}) %collective-permute-start.13) | collective-permute-done | bytes 98336 | tf_op jit(solution)/shard_map/ppermute | solution.py:30
  69.4 1.2 %collective-permute-start.14 = (bf16[64,768]{1,0:T(8,128)(2,1)S(1)}, bf16[64,768]{1,0:T(8,128)(2,1)S(1)}, u32[]{:S(2)}, u32[]{:S(2)}) collective-permute-start(bf16[64,768]{1,0:T(8,128)(2,1)S(1)} %add_convert_fusion.2), channel_id=1, source_target_pairs={{2,0},{3,1},{0,2},{1,3},{6,4},{7,5},{4,6},{5,7},{10,8},{11,9},{8,1... | collective-permute-start | bytes 294920 | tf_op jit(solution)/shard_map/ppermute | solution.py:30
  70.6 3.5 %collective-permute-done.14 = bf16[64,768]{1,0:T(8,128)(2,1)S(1)} collective-permute-done((bf16[64,768]{1,0:T(8,128)(2,1)S(1)}, bf16[64,768]{1,0:T(8,128)(2,1)S(1)}, u32[]{:S(2)}, u32[]{:S(2)}) %collective-permute-start.14) | collective-permute-done | bytes 98336 | tf_op jit(solution)/shard_map/ppermute | solution.py:30
  74.1 1.7 %collective-permute-start.15 = (bf16[64,768]{1,0:T(8,128)(2,1)S(1)}, bf16[64,768]{1,0:T(8,128)(2,1)S(1)}, u32[]{:S(2)}, u32[]{:S(2)}) collective-permute-start(bf16[64,768]{1,0:T(8,128)(2,1)S(1)} %add_convert_fusion.1), channel_id=1, source_target_pairs={{4,0},{5,1},{6,2},{7,3},{0,4},{1,5},{2,6},{3,7},{12,8},{13,9},{14,... | collective-permute-start | bytes 294920 | tf_op jit(solution)/shard_map/ppermute | solution.py:30
  75.8 3.0 %collective-permute-done.15 = bf16[64,768]{1,0:T(8,128)(2,1)S(1)} collective-permute-done((bf16[64,768]{1,0:T(8,128)(2,1)S(1)}, bf16[64,768]{1,0:T(8,128)(2,1)S(1)}, u32[]{:S(2)}, u32[]{:S(2)}) %collective-permute-start.15) | collective-permute-done | bytes 98336 | tf_op jit(solution)/shard_map/ppermute | solution.py:30
  78.9 2.0 %collective-permute-start.16 = (bf16[64,768]{1,0:T(8,128)(2,1)S(1)}, bf16[64,768]{1,0:T(8,128)(2,1)S(1)}, u32[]{:S(2)}, u32[]{:S(2)}) collective-permute-start(bf16[64,768]{1,0:T(8,128)(2,1)S(1)} %add_convert_fusion), channel_id=1, source_target_pairs={{8,0},{9,1},{10,2},{11,3},{12,4},{13,5},{14,6},{15,7},{0,8},{1,9},... | collective-permute-start | bytes 294920 | tf_op jit(solution)/shard_map/ppermute | solution.py:30
  80.9 1.1 %shard_map.146 = (f32[128,768]{1,0:T(8,128)}, bf16[128,768]{1,0:T(8,128)(2,1)}, f32[128,1]{1,0:T(8,128)S(1)}) custom-call(bf16[128,128]{1,0:T(8,128)(2,1)S(1)} %get-tuple-element.44.weights_ref, bf16[128,768]{1,0:T(8,128)(2,1)S(1)} %get-tuple-element.45.updated_ref, f32[128,1]{1,0:T(8,128)S(1)} %get-tuple-element.46.loss_ref, bf16[64,768]{1,0:T(8,128)(2,1)S(1)} %copy-done.3, ...), custom_call_target="tpu_custom_call" | custom-call | tf_op jit(solution)/shard_map/pallas_call | solution.py:38
  82.6 1.9 %collective-permute-done.16 = bf16[64,768]{1,0:T(8,128)(2,1)S(1)} collective-permute-done((bf16[64,768]{1,0:T(8,128)(2,1)S(1)}, bf16[64,768]{1,0:T(8,128)(2,1)S(1)}, u32[]{:S(2)}, u32[]{:S(2)}) %collective-permute-start.16) | collective-permute-done | bytes 98336 | tf_op jit(solution)/shard_map/ppermute | solution.py:30
  84.4 0.7 add_multiply_fusion
  (49 shorter events, 6.7 us)
Async XLA Ops:
  0.6 1.1 %copy-start.9 = (bf16[192,768]{1,0:T(8,128)(2,1)S(1)}, bf16[192,768]{1,0:T(8,128)(2,1)}, u32[]{:S(2)}) copy-start(bf16[192,768]{1,0:T(8,128)(2,1)} %param.18) | copy-start | bytes 884740
  1.7 3.1 %copy-start.11 = (bf16[192]{0:T(256)(128)(2,1)S(1)}, bf16[192]{0:T(256)(128)(2,1)}, u32[]{:S(2)}) copy-start(bf16[192]{0:T(256)(128)(2,1)} %param.17) | copy-start | bytes 1156
  1.7 20.3 %copy-start.2 = (bf16[256,768]{1,0:T(8,128)(2,1)S(1)}, bf16[256,768]{1,0:T(8,128)(2,1)}, u32[]{:S(2)}) copy-start(bf16[256,768]{1,0:T(8,128)(2,1)} %table_ref.1) | copy-start | bytes 1179652
  1.7 19.7 %collective-permute-start = (bf16[384,768]{1,0:T(8,128)(2,1)S(1)}, bf16[384,768]{1,0:T(8,128)(2,1)S(1)}, u32[]{:S(2)}, u32[]{:S(2)}) collective-permute-start(bf16[384,768]{1,0:T(8,128)(2,1)S(1)} %constant_dynamic-update-slice_fusion.refs_0_), channel_id=1, source_target_pairs={{1,0},{0,1},{3,2},{2,3},{5,4},{4,5},{7,6},{6,7},{9,8},{8,9},{11,10... | collective-permute-start | bytes 1769480 | tf_op jit(solution)/shard_map/ppermute | solution.py:30
  4.7 0.7 copy-start.5
  4.7 0.7 copy-start.8
  5.8 17.5 %collective-permute-start.1 = (bf16[384,768]{1,0:T(8,128)(2,1)S(1)}, bf16[384,768]{1,0:T(8,128)(2,1)S(1)}, u32[]{:S(2)}, u32[]{:S(2)}) collective-permute-start(bf16[384,768]{1,0:T(8,128)(2,1)S(1)} %constant_dynamic-update-slice_fusion.refs_0_), channel_id=1, source_target_pairs={{2,0},{3,1},{0,2},{1,3},{6,4},{7,5},{4,6},{5,7},{10,8},{11,9},{8,1... | collective-permute-start | bytes 1769480 | tf_op jit(solution)/shard_map/ppermute | solution.py:30
  21.4 10.1 %collective-permute-start.3 = (bf16[384,768]{1,0:T(8,128)(2,1)S(1)}, bf16[384,768]{1,0:T(8,128)(2,1)S(1)}, u32[]{:S(2)}, u32[]{:S(2)}) collective-permute-start(bf16[384,768]{1,0:T(8,128)(2,1)S(1)} %collective-permute-done.refs_1_), channel_id=1, source_target_pairs={{2,0},{3,1},{0,2},{1,3},{6,4},{7,5},{4,6},{5,7},{10,8},{11,9},{8,1... | collective-permute-start | bytes 1769480 | tf_op jit(solution)/shard_map/ppermute | solution.py:30
  23.3 17.6 %all-to-all-start.1 = ((bf16[16,16,768]{2,1,0:T(8,128)(2,1)}), bf16[16,16,768]{2,1,0:T(8,128)(2,1)}, u32[]{:S(2)}, u32[]{:S(2)}) async-start(bf16[16,16,768]{2,1,0:T(8,128)(2,1)} %bitcast.3), calls=%async_computation.1 | async-start | bytes 786432 | tf_op jit(solution)/shard_map/all_to_all | solution.py:293
  27.5 5.4 %copy-start.10 = (bf16[768]{0:T(1024)(128)(2,1)S(1)}, bf16[768]{0:T(1024)(128)(2,1)}, u32[]{:S(2)}) copy-start(bf16[768]{0:T(1024)(128)(2,1)} %param.19) | copy-start | bytes 4612
  27.5 17.4 %collective-permute-start.4 = (bf16[384,768]{1,0:T(8,128)(2,1)S(1)}, bf16[384,768]{1,0:T(8,128)(2,1)S(1)}, u32[]{:S(2)}, u32[]{:S(2)}) collective-permute-start(bf16[384,768]{1,0:T(8,128)(2,1)S(1)} %collective-permute-done.refs_1_), channel_id=1, source_target_pairs={{18,16},{19,17},{16,18},{17,19},{22,20},{23,21},{20,22},{21,23},{2... | collective-permute-start | bytes 1769480 | tf_op jit(solution)/shard_map/ppermute | solution.py:30
  31.5 13.5 %collective-permute-start.5 = (bf16[384,768]{1,0:T(8,128)(2,1)S(1)}, bf16[384,768]{1,0:T(8,128)(2,1)S(1)}, u32[]{:S(2)}, u32[]{:S(2)}) collective-permute-start(bf16[384,768]{1,0:T(8,128)(2,1)S(1)} %collective-permute-done.3.refs_2_), channel_id=1, source_target_pairs={{18,16},{19,17},{16,18},{17,19},{22,20},{23,21},{20,22},{21,23},{2... | collective-permute-start | bytes 1769480 | tf_op jit(solution)/shard_map/ppermute | solution.py:30
  32.9 0.7 copy-start.6
  32.9 0.7 copy-start.7
  33.5 0.9 %copy-start.4 = (bf16[128,768]{1,0:T(8,128)(2,1)S(1)}, bf16[128,768]{1,0:T(8,128)(2,1)}, u32[]{:S(2)}) copy-start(bf16[128,768]{1,0:T(8,128)(2,1)} %queries_ref.1) | copy-start | bytes 589828
  34.6 0.7 copy-start
  40.8 0.9 %copy-start.1 = (bf16[144,768]{1,0:T(8,128)(2,1)S(1)}, bf16[144,768]{1,0:T(8,128)(2,1)}, u32[]{:S(2)}) copy-start(bf16[144,768]{1,0:T(8,128)(2,1)} %copy-done) | copy-start | bytes 663556
  43.2 1.7 %collective-permute-start.2 = (bf16[128,768]{1,0:T(8,128)(2,1)S(1)}, bf16[128,768]{1,0:T(8,128)(2,1)S(1)}, u32[]{:S(2)}, u32[]{:S(2)}) collective-permute-start(bf16[128,768]{1,0:T(8,128)(2,1)S(1)} %get-tuple-element.34.normed_ref), channel_id=1, source_target_pairs={{0,16},{16,0},{1,17},{17,1},{2,18},{18,2},{3,19},{19,3},{4,20},{20... | collective-permute-start | bytes 589832 | tf_op jit(solution)/shard_map/ppermute | solution.py:19
  43.3 7.3 %collective-permute-start.7 = (bf16[128,768]{1,0:T(8,128)(2,1)S(1)}, bf16[128,768]{1,0:T(8,128)(2,1)S(1)}, u32[]{:S(2)}, u32[]{:S(2)}) collective-permute-start(bf16[128,768]{1,0:T(8,128)(2,1)S(1)} %get-tuple-element.34.normed_ref), channel_id=1, source_target_pairs={{0,4},{1,5},{2,6},{3,7},{4,0},{5,1},{6,2},{7,3},{8,12},{9,13},{10,... | collective-permute-start | bytes 589832 | tf_op jit(solution)/shard_map/ppermute | solution.py:19
  50.6 1.4 %collective-permute-start.8 = (bf16[128,768]{1,0:T(8,128)(2,1)S(1)}, bf16[128,768]{1,0:T(8,128)(2,1)S(1)}, u32[]{:S(2)}, u32[]{:S(2)}) collective-permute-start(bf16[128,768]{1,0:T(8,128)(2,1)S(1)} %collective-permute-done.7.normed_ref), channel_id=1, source_target_pairs={{0,16},{16,0},{1,17},{17,1},{2,18},{18,2},{3,19},{19,3},{4,20},{20... | collective-permute-start | bytes 589832 | tf_op jit(solution)/shard_map/ppermute | solution.py:19
  54.0 1.5 %collective-permute-start.9 = (bf16[128,768]{1,0:T(8,128)(2,1)S(1)}, bf16[128,768]{1,0:T(8,128)(2,1)S(1)}, u32[]{:S(2)}, u32[]{:S(2)}) collective-permute-start(bf16[128,768]{1,0:T(8,128)(2,1)S(1)} %get-tuple-element.41), channel_id=1, source_target_pairs={{0,16},{16,0},{1,17},{17,1},{2,18},{18,2},{3,19},{19,3},{4,20},{20... | collective-permute-start | bytes 589832 | tf_op jit(solution)/shard_map/ppermute | solution.py:19
  54.2 4.3 %collective-permute-start.6 = (f32[128,768]{1,0:T(8,128)S(1)}, f32[128,768]{1,0:T(8,128)S(1)}, u32[]{:S(2)}, u32[]{:S(2)}) collective-permute-start(f32[128,768]{1,0:T(8,128)S(1)} %get-tuple-element.38), channel_id=1, source_target_pairs={{0,16},{16,0},{1,17},{17,1},{2,18},{18,2},{3,19},{19,3},{4,20},{20... | collective-permute-start | bytes 1179656 | tf_op jit(solution)/shard_map/ppermute | solution.py:19
  55.5 1.7 %copy-start.3 = (bf16[64,768]{1,0:T(8,128)(2,1)S(1)}, bf16[64,768]{1,0:T(8,128)(2,1)}, u32[]{:S(2)}) copy-start(bf16[64,768]{1,0:T(8,128)(2,1)} %refs_0_.3) | copy-start | bytes 294916
  55.5 7.0 %collective-permute-start.10 = (bf16[128,768]{1,0:T(8,128)(2,1)S(1)}, bf16[128,768]{1,0:T(8,128)(2,1)S(1)}, u32[]{:S(2)}, u32[]{:S(2)}) collective-permute-start(bf16[128,768]{1,0:T(8,128)(2,1)S(1)} %shard_map.144), channel_id=1, source_target_pairs={{0,4},{1,5},{2,6},{3,7},{4,0},{5,1},{6,2},{7,3},{8,12},{9,13},{10,... | collective-permute-start | bytes 589832 | tf_op jit(solution)/shard_map/ppermute | solution.py:19
  57.1 1.3 %collective-permute-start.11 = (bf16[64,768]{1,0:T(8,128)(2,1)S(1)}, bf16[64,768]{1,0:T(8,128)(2,1)S(1)}, u32[]{:S(2)}, u32[]{:S(2)}) collective-permute-start(bf16[64,768]{1,0:T(8,128)(2,1)S(1)} %copy-done.3), channel_id=1, source_target_pairs={{0,16},{16,0},{1,17},{17,1},{2,18},{18,2},{3,19},{19,3},{4,20},{20... | collective-permute-start | bytes 294920 | tf_op jit(solution)/shard_map/ppermute | solution.py:19
  63.3 1.4 %collective-permute-start.12 = (bf16[64,768]{1,0:T(8,128)(2,1)S(1)}, bf16[64,768]{1,0:T(8,128)(2,1)S(1)}, u32[]{:S(2)}, u32[]{:S(2)}) collective-permute-start(bf16[64,768]{1,0:T(8,128)(2,1)S(1)} %get-tuple-element.51), channel_id=1, source_target_pairs={{0,16},{16,0},{1,17},{17,1},{2,18},{18,2},{3,19},{19,3},{4,20},{20... | collective-permute-start | bytes 294920 | tf_op jit(solution)/shard_map/ppermute | solution.py:19
  64.7 4.7 %collective-permute-start.13 = (bf16[64,768]{1,0:T(8,128)(2,1)S(1)}, bf16[64,768]{1,0:T(8,128)(2,1)S(1)}, u32[]{:S(2)}, u32[]{:S(2)}) collective-permute-start(bf16[64,768]{1,0:T(8,128)(2,1)S(1)} %add_convert_fusion.3), channel_id=1, source_target_pairs={{1,0},{0,1},{3,2},{2,3},{5,4},{4,5},{7,6},{6,7},{9,8},{8,9},{11,10... | collective-permute-start | bytes 294920 | tf_op jit(solution)/shard_map/ppermute | solution.py:30
  69.4 4.7 %collective-permute-start.14 = (bf16[64,768]{1,0:T(8,128)(2,1)S(1)}, bf16[64,768]{1,0:T(8,128)(2,1)S(1)}, u32[]{:S(2)}, u32[]{:S(2)}) collective-permute-start(bf16[64,768]{1,0:T(8,128)(2,1)S(1)} %add_convert_fusion.2), channel_id=1, source_target_pairs={{2,0},{3,1},{0,2},{1,3},{6,4},{7,5},{4,6},{5,7},{10,8},{11,9},{8,1... | collective-permute-start | bytes 294920 | tf_op jit(solution)/shard_map/ppermute | solution.py:30
  74.1 4.7 %collective-permute-start.15 = (bf16[64,768]{1,0:T(8,128)(2,1)S(1)}, bf16[64,768]{1,0:T(8,128)(2,1)S(1)}, u32[]{:S(2)}, u32[]{:S(2)}) collective-permute-start(bf16[64,768]{1,0:T(8,128)(2,1)S(1)} %add_convert_fusion.1), channel_id=1, source_target_pairs={{4,0},{5,1},{6,2},{7,3},{0,4},{1,5},{2,6},{3,7},{12,8},{13,9},{14,... | collective-permute-start | bytes 294920 | tf_op jit(solution)/shard_map/ppermute | solution.py:30
  78.9 5.6 %collective-permute-start.16 = (bf16[64,768]{1,0:T(8,128)(2,1)S(1)}, bf16[64,768]{1,0:T(8,128)(2,1)S(1)}, u32[]{:S(2)}, u32[]{:S(2)}) collective-permute-start(bf16[64,768]{1,0:T(8,128)(2,1)S(1)} %add_convert_fusion), channel_id=1, source_target_pairs={{8,0},{9,1},{10,2},{11,3},{12,4},{13,5},{14,6},{15,7},{0,8},{1,9},... | collective-permute-start | bytes 294920 | tf_op jit(solution)/shard_map/ppermute | solution.py:30

commit v6 on v5

--- a/solution.py
+++ b/solution.py
@@ -117,9 +117,9 @@
     return 0.5 * u * (1.0 + jnp.tanh(0.7978845608028654 * (u + 0.044715 * (u * u * u))))
 
 
-def hidden_body(plan, normed_ref, normed2_ref, message_ref, *refs):
-    shards, (total_ref, total2_ref, held_in, held_out, sems) = refs[:-5], refs[-5:]
-    chains, units = total_ref.shape[0], held_in.shape[0] // len(plan)
+def hidden_body(plan, normed_ref, message_ref, *refs):
+    shards, (total_ref, held_in, held_out, sems) = refs[:-4], refs[-4:]
+    units = held_in.shape[0] // len(plan)
     me, first_core = lax.axis_index("mp"), lax.axis_index("dp") % 2 == 0
     held = (held_in, held_out)
 
@@ -142,7 +142,7 @@
                 def _():
                     copy(other_at, p, side).start()
 
-    normed = jnp.concatenate([normed_ref[...], normed2_ref[...]], axis=0)
+    normed = normed_ref[...]
     places = [me ^ jnp.where(first_core, mask, other_mask) for mask, _, other_mask, _ in plan]
     bias = jnp.concatenate(
         [message_ref[pl.ds(place, 1)].reshape(1, message_ref.shape[2])[:, :units] for place in places], axis=1
@@ -153,20 +153,13 @@
     activated = gelu(preact + bias).astype(BF16)
     for p, (_, at, _, _) in enumerate(plan):
         copy(at, p, 1).wait()
-    total = jnp.dot(activated, held_out[...], preferred_element_type=F32)
-    total_ref[...] = total[:chains, :]
-    total2_ref[...] = total[chains:, :].astype(total2_ref.dtype)
-
-
-def add_body(total_ref, received_ref, sum_ref):
-    sum_ref[...] = (total_ref[...] + received_ref[...].astype(F32)).astype(sum_ref.dtype)
+    total_ref[...] = jnp.dot(activated, held_out[...], preferred_element_type=F32).astype(total_ref.dtype)
 
 
 def score_body(
     blocks,
     shifted_ref,
     total_ref,
-    received_ref,
     other_ref,
     positive_ref,
     *refs,
@@ -174,7 +167,7 @@
     tools = [ref[...] for ref in refs[:blocks]]
     updated_ref, loss_ref, weights_ref, *grad_refs = refs[blocks:]
     block_rows = tools[0].shape[0]
-    branch = total_ref[...] + received_ref[...] + other_ref[...].astype(F32)
+    branch = total_ref[...] + other_ref[...].astype(F32)
     updated = (shifted_ref[...] + branch).astype(BF16)
     updated_ref[...] = updated
     scores = jnp.concatenate(
@@ -222,12 +215,23 @@
     turned = moved(first, (0, 0, 2), (1, 1, 1))
     far_y = moved(first, (1, 1, 2))
     far_both = moved(turned, (1, 1, 2))
-    pieces = [(0, own, 8, near), (1, near, 9, turned), (2, near_y, 10, far_y), (3, turned, 11, far_both)]
+    levels = []
     for level in range(16, groups, 16):
         base = moved(own, (0, 0, level), (1, 1, level ^ 8))
         by_x, by_y = (moved(base, (0, 0, bit), (1, 1, bit)) for bit in (1, 2))
         both = moved(by_x, (0, 0, 2), (1, 1, 2))
-        pieces += [(level ^ m, s, level ^ 8 ^ m, s) for m, s in enumerate((base, by_x, by_y, both))]
+        levels += [(level ^ m, shard, level ^ 8 ^ m) for m, shard in enumerate((base, by_x, by_y, both))]
+    return [(1, near, 8), (3, turned, 9), *levels], (near_y, far_y, far_both)
+
+
+def shared_pieces(own, symmetric, near_y, far_y, far_both, ready):
+    pieces = [(0, own, 0, own)]
+    for mask, shard, other_mask in symmetric:
+        given = flipped(after(shard, ready), "dp", 1)
+        pieces += [(mask, shard, other_mask, shard), (other_mask, given, mask, given)]
+    pieces.append((2, near_y, 2, flipped(after(near_y, ready), "dp", 1)))
+    pieces.append((10, flipped(after(far_y, ready), "dp", 1), 10, far_y))
+    pieces.append((11, flipped(after(far_both, ready), "dp", 1), 11, far_both))
     return pieces
 
 
@@ -289,8 +293,16 @@
         held.append(early_and_served[-1])
         return early_and_served[:-1]
 
-    pieces = weight_pieces(own, own_later, groups, hold, asked)
+    symmetric, single = weight_pieces(own, own_later, groups, hold, asked)
     fetched = lax.all_to_all(held[0], "mp", split_axis=0, concat_axis=0, tiled=True)
+    shifted, normed, positive_row = kernel_call(
+        select_body,
+        (whole((chains, features), F32), whole((chains, features), BF16), whole((1, chains), jnp.int32)),
+        packed,
+        fetched,
+    )
+
+    pieces = shared_pieces(own, symmetric, *single, normed)
     shards = []
     for piece in pieces:
         for shard in (piece[1], piece[3]):
@@ -299,22 +311,14 @@
     index_of = {id(s): i for i, s in enumerate(shards)}
     plan = tuple((mask, index_of[id(s)], other, index_of[id(t)]) for mask, s, other, t in pieces)
 
-    shifted, normed, positive_row = kernel_call(
-        select_body,
-        (whole((chains, features), F32), whole((chains, features), BF16), whole((1, chains), jnp.int32)),
-        packed,
-        fetched,
-    )
-
-    def hidden(own_rows, to_share, given):
+    def hidden(rows, held_as):
         return kernel_call(
             functools.partial(hidden_body, plan),
-            (whole((chains, features), F32), whole((chains, features), given)),
-            own_rows,
-            flipped(to_share, "dp", 1),
+            whole((chains, features), held_as),
+            rows,
             asked,
             *shards,
-            in_place=range(3, 3 + len(shards)),
+            in_place=range(2, 2 + len(shards)),
             scratch=(
                 pltpu.VMEM((len(plan) * units, features), BF16),
                 pltpu.VMEM((len(plan) * units, features), BF16),
@@ -323,13 +327,9 @@
             vmem=LARGE_VMEM,
         )
 
-    total, total_for = hidden(normed, after(normed, pieces[2][1]), F32)
-    neighbour_normed = after(flipped(normed, "mp", 4), total)
-    neighbour, neighbour_for = hidden(neighbour_normed, neighbour_normed, BF16)
-    neighbour_sum = kernel_call(
-        add_body, whole((chains, features), BF16), neighbour, flipped(neighbour_for, "dp", 1)
-    )
-    late_tools = after(tool_embeds, total)
+    neighbour = hidden(flipped(normed, "mp", 4), BF16)
+    total = hidden(after(normed, neighbour), F32)
+    late_tools = after(tool_embeds, neighbour)
     tools = [tool_embeds] + [flipped(late_tools, "dp", j) for j in range(1, cycle)]
     updated, loss, weights, *grads = kernel_call(
         functools.partial(score_body, cycle),
@@ -341,8 +341,7 @@
         ),
         shifted,
         total,
-        flipped(total_for, "dp", 1),
-        flipped(neighbour_sum, "mp", 4),
+        flipped(neighbour, "mp", 4),
         positive_row,
         *tools,
     )

time: 85.6 us -> 84.8 us (level)
  waiting for transfers between devices: 33.4 us -> 28.2 us
  starting transfers between devices: 22.8 us -> 25.4 us
  Pallas kernels: 8.9 us -> 10.6 us
    ppermute x8 -> x9, waiting for transfers between devices: 12.8 us -> 7.31 us  [flipped(): lax.ppermute(block, axis, [(i, i ^ mask) for i in range(lax.axis_size(axi...]
    ppermute x8 -> x9, starting transfers between devices: 3.98 us -> 6.98 us  [flipped(): lax.ppermute(block, axis, [(i, i ^ mask) for i in range(lax.axis_size(axi...]
    pallas_call x9 -> x8, Pallas kernels: 8.9 us -> 10.6 us  [kernel_call(): pl.pallas_call(body, out_shape=out_shape, in_specs=[pl.BlockSpec(memory_s...]
  transfers between devices with their start and end apart: 18 -> 19, of which waited for: 12 -> 10; matrix products, arithmetic and copies ran while one was open for 2% -> 2% of each run, Pallas kernels for 7% -> 8%
where the time goes in v6:
time: 84.8 us; the launch traced here: 84.4 us
  waiting for transfers between devices  28.2 us (33%)
  starting transfers between devices  25.4 us (30%)
  blocking collectives  12.2 us (14%)
  Pallas kernels  10.6 us (12%)
  local copies, waits for them, and re-layouts  5.65 us (7%)
  other arithmetic  1.43 us (2%)
  between operations  0.86 us (1%)
    ppermute x9, waiting for transfers between devices, moved(): return lax.ppermute(block, ('dp', 'mp'), route)  15.4 us
    ppermute x9, starting transfers between devices, moved(): return lax.ppermute(block, ('dp', 'mp'), route)  14.2 us
    all_to_all x1, blocking collectives, local(): lax.all_to_all(message, 'mp', split_axis=0, concat_axis=0, tiled=True)  12.2 us
    pallas_call x8, Pallas kernels, kernel_call(): pl.pallas_call(body, out_shape=out_shape, in_specs=[pl.BlockSpec(memory_s...  10.6 us
    ppermute x9, waiting for transfers between devices, flipped(): lax.ppermute(block, axis, [(i, i ^ mask) for i in range(lax.axis_size(axi...  7.31 us
    ppermute x9, starting transfers between devices, flipped(): lax.ppermute(block, axis, [(i, i ^ mask) for i in range(lax.axis_size(axi...  6.98 us
    all_to_all x1, waiting for transfers between devices, local(): lax.all_to_all(held[0], 'mp', split_axis=0, concat_axis=0, tiled=True)  5.51 us
    unnamed x25, local copies, waits for them, and re-layouts  4.93 us
  transfers between devices with their start and end apart: 19, of which 10 were waited for; matrix products, arithmetic and copies ran while one was open for 2% of the time, Pallas kernels for 8%

profile of v6, /device:TPU:0, one launch (start us, length us, event | category | flops | bytes accessed | tf_op | source)
XLA Modules:
  0.0 84.4 jit_solution(12139425337927978550)
XLA Ops:
  0.6 1.0 %constant_dynamic-update-slice_fusion.1 = bf16[384,768]{1,0:T(8,128)(2,1)S(1)} fusion(bf16[192,768]{1,0:T(8,128)(2,1)} %param.16), kind=kLoop, calls=%fused_computation.6 | loop fusion | bytes 589824
  1.7 3.0 %collective-permute-start = (bf16[384,768]{1,0:T(8,128)(2,1)S(1)}, bf16[384,768]{1,0:T(8,128)(2,1)S(1)}, u32[]{:S(2)}, u32[]{:S(2)}) collective-permute-start(bf16[384,768]{1,0:T(8,128)(2,1)S(1)} %constant_dynamic-update-slice_fusion.refs_0_), channel_id=1, source_target_pairs={{1,0},{0,1},{3,2},{2,3},{5,4},{4,5},{7,6},{6,7},{9,8},{8,9},{11,10... | collective-permute-start | bytes 1769480 | tf_op jit(solution)/shard_map/ppermute | solution.py:30
  5.8 3.4 %collective-permute-start.1 = (bf16[384,768]{1,0:T(8,128)(2,1)S(1)}, bf16[384,768]{1,0:T(8,128)(2,1)S(1)}, u32[]{:S(2)}, u32[]{:S(2)}) collective-permute-start(bf16[384,768]{1,0:T(8,128)(2,1)S(1)} %constant_dynamic-update-slice_fusion.refs_0_), channel_id=1, source_target_pairs={{2,0},{3,1},{0,2},{1,3},{6,4},{7,5},{4,6},{5,7},{10,8},{11,9},{8,1... | collective-permute-start | bytes 1769480 | tf_op jit(solution)/shard_map/ppermute | solution.py:30
  9.2 12.2 %all_to_all.16.message_ref = f32[16,1,256]{2,1,0:T(1,128)S(1)} all-to-all(f32[16,1,256]{2,1,0:T(1,128)S(1)} %shard_map.138), channel_id=1, replica_groups=mesh['dp'=2,'mp'=16] {'mp'}, dimensions={0} | all-to-all | bytes 32768 | tf_op jit(solution)/shard_map/all_to_all | solution.py:271
  22.0 1.3 %shard_map.139 = bf16[256,768]{1,0:T(8,128)(2,1)} custom-call(f32[16,1,256]{2,1,0:T(1,128)S(1)} %all_to_all.16.message_ref, bf16[256,768]{1,0:T(8,128)(2,1)S(1)} %copy-done.2), custom_call_target="tpu_custom_call" | custom-call | tf_op jit(solution)/shard_map/pallas_call | solution.py:38
  23.3 4.2 %all-to-all-start.1 = ((bf16[16,16,768]{2,1,0:T(8,128)(2,1)}), bf16[16,16,768]{2,1,0:T(8,128)(2,1)}, u32[]{:S(2)}, u32[]{:S(2)}) async-start(bf16[16,16,768]{2,1,0:T(8,128)(2,1)} %bitcast.3), calls=%async_computation.1 | async-start | bytes 786432 | tf_op jit(solution)/shard_map/all_to_all | solution.py:297
  27.5 0.7 collective-permute-start.7
  28.2 3.3 %collective-permute-done.4.refs_3_ = bf16[384,768]{1,0:T(8,128)(2,1)S(1)} collective-permute-done((bf16[384,768]{1,0:T(8,128)(2,1)S(1)}, bf16[384,768]{1,0:T(8,128)(2,1)S(1)}, u32[]{:S(2)}, u32[]{:S(2)}) %collective-permute-start.4) | collective-permute-done | bytes 589856 | tf_op jit(solution)/shard_map/ppermute | solution.py:30
  33.5 0.9 %copy-done.4 = bf16[128,768]{1,0:T(8,128)(2,1)S(1)} copy-done((bf16[128,768]{1,0:T(8,128)(2,1)S(1)}, bf16[128,768]{1,0:T(8,128)(2,1)}, u32[]{:S(2)}) %copy-start.4) | copy-done | bytes 196632
  35.3 5.5 %all-to-all-done.1 = bf16[16,16,768]{2,1,0:T(8,128)(2,1)} async-done(((bf16[16,16,768]{2,1,0:T(8,128)(2,1)}), bf16[16,16,768]{2,1,0:T(8,128)(2,1)}, u32[]{:S(2)}, u32[]{:S(2)}) %all-to-all-start.1) | async-done | bytes 393248 | tf_op jit(solution)/shard_map/all_to_all | solution.py:297
  40.8 0.9 %copy-done.1 = bf16[144,768]{1,0:T(8,128)(2,1)S(1)} copy-done((bf16[144,768]{1,0:T(8,128)(2,1)S(1)}, bf16[144,768]{1,0:T(8,128)(2,1)}, u32[]{:S(2)}) %copy-start.1) | copy-done | bytes 221208
  41.8 1.4 %shard_map.141 = (f32[128,768]{1,0:T(8,128)S(1)}, bf16[128,768]{1,0:T(8,128)(2,1)S(1)}, s32[1,128]{1,0:T(1,128)S(1)}) custom-call(bf16[144,768]{1,0:T(8,128)(2,1)S(1)} %copy-done.1, bf16[256,768]{1,0:T(8,128)(2,1)} %bitcast.4.fetched_ref), custom_call_target="tpu_custom_call" | custom-call | tf_op jit(solution)/shard_map/pallas_call | solution.py:38
  43.2 1.6 %collective-permute-start.2 = (bf16[128,768]{1,0:T(8,128)(2,1)S(1)}, bf16[128,768]{1,0:T(8,128)(2,1)S(1)}, u32[]{:S(2)}, u32[]{:S(2)}) collective-permute-start(bf16[128,768]{1,0:T(8,128)(2,1)S(1)} %get-tuple-element.41.normed_ref), channel_id=1, source_target_pairs={{0,4},{1,5},{2,6},{3,7},{4,0},{5,1},{6,2},{7,3},{8,12},{9,13},{10,... | collective-permute-start | bytes 589832 | tf_op jit(solution)/shard_map/ppermute | solution.py:19
  45.4 3.0 %collective-permute-start.5 = (bf16[384,768]{1,0:T(8,128)(2,1)S(1)}, bf16[384,768]{1,0:T(8,128)(2,1)S(1)}, u32[]{:S(2)}, u32[]{:S(2)}) collective-permute-start(bf16[384,768]{1,0:T(8,128)(2,1)S(1)} %collective-permute-done.4.refs_3_), channel_id=1, source_target_pairs={{0,16},{16,0},{1,17},{17,1},{2,18},{18,2},{3,19},{19,3},{4,20},{20... | collective-permute-start | bytes 1769480 | tf_op jit(solution)/shard_map/ppermute | solution.py:19
  48.3 1.6 %collective-permute-done.2.normed_ref = bf16[128,768]{1,0:T(8,128)(2,1)S(1)} collective-permute-done((bf16[128,768]{1,0:T(8,128)(2,1)S(1)}, bf16[128,768]{1,0:T(8,128)(2,1)S(1)}, u32[]{:S(2)}, u32[]{:S(2)}) %collective-permute-start.2) | collective-permute-done | bytes 196640 | tf_op jit(solution)/shard_map/ppermute | solution.py:19
  50.0 2.0 %collective-permute-done.10.refs_9_ = bf16[384,768]{1,0:T(8,128)(2,1)S(1)} collective-permute-done((bf16[384,768]{1,0:T(8,128)(2,1)S(1)}, bf16[384,768]{1,0:T(8,128)(2,1)S(1)}, u32[]{:S(2)}, u32[]{:S(2)}) %collective-permute-start.10) | collective-permute-done | bytes 589856 | tf_op jit(solution)/shard_map/ppermute | solution.py:19
  52.0 2.8 %shard_map.142 = bf16[128,768]{1,0:T(8,128)(2,1)S(1)} custom-call(bf16[128,768]{1,0:T(8,128)(2,1)S(1)} %collective-permute-done.2.normed_ref, f32[16,1,256]{2,1,0:T(1,128)S(1)} %all_to_all.16.message_ref, bf16[384,768]{1,0:T(8,128)(2,1)S(1)} %constant_dynamic-update-slice_fusion.refs_0_, bf16[384,768]{1,0:T(8,128)(2,1)S(1)} %collective-permute-done.refs_1_, ...), custom_call_target="tpu_custom_call" | custom-call | tf_op jit(solution)/shard_map/pallas_call | solution.py:38
  54.7 1.8 %collective-permute-start.11 = (bf16[128,768]{1,0:T(8,128)(2,1)S(1)}, bf16[128,768]{1,0:T(8,128)(2,1)S(1)}, u32[]{:S(2)}, u32[]{:S(2)}) collective-permute-start(bf16[128,768]{1,0:T(8,128)(2,1)S(1)} %shard_map.142), channel_id=1, source_target_pairs={{0,4},{1,5},{2,6},{3,7},{4,0},{5,1},{6,2},{7,3},{8,12},{9,13},{10,... | collective-permute-start | bytes 589832 | tf_op jit(solution)/shard_map/ppermute | solution.py:19
  56.5 2.8 %shard_map.143.total_ref = f32[128,768]{1,0:T(8,128)S(1)} custom-call(bf16[128,768]{1,0:T(8,128)(2,1)S(1)} %get-tuple-element.41.normed_ref, f32[16,1,256]{2,1,0:T(1,128)S(1)} %all_to_all.16.message_ref, bf16[384,768]{1,0:T(8,128)(2,1)S(1)} %constant_dynamic-update-slice_fusion.refs_0_, bf16[384,768]{1,0:T(8,128)(2,1)S(1)} %collective-permute-done.refs_1_, ...), custom_call_target="tpu_custom_call" | custom-call | tf_op jit(solution)/shard_map/pallas_call | solution.py:38
  59.3 2.4 %collective-permute-done.11.other_ref = bf16[128,768]{1,0:T(8,128)(2,1)S(1)} collective-permute-done((bf16[128,768]{1,0:T(8,128)(2,1)S(1)}, bf16[128,768]{1,0:T(8,128)(2,1)S(1)}, u32[]{:S(2)}, u32[]{:S(2)}) %collective-permute-start.11) | collective-permute-done | bytes 196640 | tf_op jit(solution)/shard_map/ppermute | solution.py:19
  61.7 0.8 shard_map.144
  62.6 1.3 %collective-permute-done.13 = bf16[64,768]{1,0:T(8,128)(2,1)S(1)} collective-permute-done((bf16[64,768]{1,0:T(8,128)(2,1)S(1)}, bf16[64,768]{1,0:T(8,128)(2,1)S(1)}, u32[]{:S(2)}, u32[]{:S(2)}) %collective-permute-start.13) | collective-permute-done | bytes 98336 | tf_op jit(solution)/shard_map/ppermute | solution.py:19
  63.9 1.2 %collective-permute-start.14 = (bf16[64,768]{1,0:T(8,128)(2,1)S(1)}, bf16[64,768]{1,0:T(8,128)(2,1)S(1)}, u32[]{:S(2)}, u32[]{:S(2)}) collective-permute-start(bf16[64,768]{1,0:T(8,128)(2,1)S(1)} %add_convert_fusion.3), channel_id=1, source_target_pairs={{1,0},{0,1},{3,2},{2,3},{5,4},{4,5},{7,6},{6,7},{9,8},{8,9},{11,10... | collective-permute-start | bytes 294920 | tf_op jit(solution)/shard_map/ppermute | solution.py:30
  65.1 3.5 %collective-permute-done.14 = bf16[64,768]{1,0:T(8,128)(2,1)S(1)} collective-permute-done((bf16[64,768]{1,0:T(8,128)(2,1)S(1)}, bf16[64,768]{1,0:T(8,128)(2,1)S(1)}, u32[]{:S(2)}, u32[]{:S(2)}) %collective-permute-start.14) | collective-permute-done | bytes 98336 | tf_op jit(solution)/shard_map/ppermute | solution.py:30
  68.7 1.3 %collective-permute-start.15 = (bf16[64,768]{1,0:T(8,128)(2,1)S(1)}, bf16[64,768]{1,0:T(8,128)(2,1)S(1)}, u32[]{:S(2)}, u32[]{:S(2)}) collective-permute-start(bf16[64,768]{1,0:T(8,128)(2,1)S(1)} %add_convert_fusion.2), channel_id=1, source_target_pairs={{2,0},{3,1},{0,2},{1,3},{6,4},{7,5},{4,6},{5,7},{10,8},{11,9},{8,1... | collective-permute-start | bytes 294920 | tf_op jit(solution)/shard_map/ppermute | solution.py:30
  70.0 3.4 %collective-permute-done.15 = bf16[64,768]{1,0:T(8,128)(2,1)S(1)} collective-permute-done((bf16[64,768]{1,0:T(8,128)(2,1)S(1)}, bf16[64,768]{1,0:T(8,128)(2,1)S(1)}, u32[]{:S(2)}, u32[]{:S(2)}) %collective-permute-start.15) | collective-permute-done | bytes 98336 | tf_op jit(solution)/shard_map/ppermute | solution.py:30
  73.4 1.8 %collective-permute-start.16 = (bf16[64,768]{1,0:T(8,128)(2,1)S(1)}, bf16[64,768]{1,0:T(8,128)(2,1)S(1)}, u32[]{:S(2)}, u32[]{:S(2)}) collective-permute-start(bf16[64,768]{1,0:T(8,128)(2,1)S(1)} %add_convert_fusion.1), channel_id=1, source_target_pairs={{4,0},{5,1},{6,2},{7,3},{0,4},{1,5},{2,6},{3,7},{12,8},{13,9},{14,... | collective-permute-start | bytes 294920 | tf_op jit(solution)/shard_map/ppermute | solution.py:30
  75.2 2.9 %collective-permute-done.16 = bf16[64,768]{1,0:T(8,128)(2,1)S(1)} collective-permute-done((bf16[64,768]{1,0:T(8,128)(2,1)S(1)}, bf16[64,768]{1,0:T(8,128)(2,1)S(1)}, u32[]{:S(2)}, u32[]{:S(2)}) %collective-permute-start.16) | collective-permute-done | bytes 98336 | tf_op jit(solution)/shard_map/ppermute | solution.py:30
  78.1 1.6 %collective-permute-start.17 = (bf16[64,768]{1,0:T(8,128)(2,1)S(1)}, bf16[64,768]{1,0:T(8,128)(2,1)S(1)}, u32[]{:S(2)}, u32[]{:S(2)}) collective-permute-start(bf16[64,768]{1,0:T(8,128)(2,1)S(1)} %add_convert_fusion), channel_id=1, source_target_pairs={{8,0},{9,1},{10,2},{11,3},{12,4},{13,5},{14,6},{15,7},{0,8},{1,9},... | collective-permute-start | bytes 294920 | tf_op jit(solution)/shard_map/ppermute | solution.py:30
  79.6 1.1 %shard_map.145 = (f32[128,768]{1,0:T(8,128)}, bf16[128,768]{1,0:T(8,128)(2,1)}, f32[128,1]{1,0:T(8,128)S(1)}) custom-call(bf16[128,128]{1,0:T(8,128)(2,1)S(1)} %get-tuple-element.44.weights_ref, bf16[128,768]{1,0:T(8,128)(2,1)S(1)} %get-tuple-element.45.updated_ref, f32[128,1]{1,0:T(8,128)S(1)} %get-tuple-element.46.loss_ref, bf16[64,768]{1,0:T(8,128)(2,1)S(1)} %copy-done.3, ...), custom_call_target="tpu_custom_call" | custom-call | tf_op jit(solution)/shard_map/pallas_call | solution.py:38
  81.3 2.3 %collective-permute-done.17 = bf16[64,768]{1,0:T(8,128)(2,1)S(1)} collective-permute-done((bf16[64,768]{1,0:T(8,128)(2,1)S(1)}, bf16[64,768]{1,0:T(8,128)(2,1)S(1)}, u32[]{:S(2)}, u32[]{:S(2)}) %collective-permute-start.17) | collective-permute-done | bytes 98336 | tf_op jit(solution)/shard_map/ppermute | solution.py:30
  83.7 0.7 add_multiply_fusion
  (50 shorter events, 5.9 us)
Async XLA Ops:
  0.6 1.1 %copy-start.9 = (bf16[192,768]{1,0:T(8,128)(2,1)S(1)}, bf16[192,768]{1,0:T(8,128)(2,1)}, u32[]{:S(2)}) copy-start(bf16[192,768]{1,0:T(8,128)(2,1)} %param.18) | copy-start | bytes 884740
  1.7 3.1 %copy-start.11 = (bf16[192]{0:T(256)(128)(2,1)S(1)}, bf16[192]{0:T(256)(128)(2,1)}, u32[]{:S(2)}) copy-start(bf16[192]{0:T(256)(128)(2,1)} %param.17) | copy-start | bytes 1156
  1.7 20.3 %copy-start.2 = (bf16[256,768]{1,0:T(8,128)(2,1)S(1)}, bf16[256,768]{1,0:T(8,128)(2,1)}, u32[]{:S(2)}) copy-start(bf16[256,768]{1,0:T(8,128)(2,1)} %table_ref.1) | copy-start | bytes 1179652
  1.7 19.7 %collective-permute-start = (bf16[384,768]{1,0:T(8,128)(2,1)S(1)}, bf16[384,768]{1,0:T(8,128)(2,1)S(1)}, u32[]{:S(2)}, u32[]{:S(2)}) collective-permute-start(bf16[384,768]{1,0:T(8,128)(2,1)S(1)} %constant_dynamic-update-slice_fusion.refs_0_), channel_id=1, source_target_pairs={{1,0},{0,1},{3,2},{2,3},{5,4},{4,5},{7,6},{6,7},{9,8},{8,9},{11,10... | collective-permute-start | bytes 1769480 | tf_op jit(solution)/shard_map/ppermute | solution.py:30
  4.7 0.7 copy-start.5
  4.7 0.7 copy-start.8
  5.8 17.5 %collective-permute-start.1 = (bf16[384,768]{1,0:T(8,128)(2,1)S(1)}, bf16[384,768]{1,0:T(8,128)(2,1)S(1)}, u32[]{:S(2)}, u32[]{:S(2)}) collective-permute-start(bf16[384,768]{1,0:T(8,128)(2,1)S(1)} %constant_dynamic-update-slice_fusion.refs_0_), channel_id=1, source_target_pairs={{2,0},{3,1},{0,2},{1,3},{6,4},{7,5},{4,6},{5,7},{10,8},{11,9},{8,1... | collective-permute-start | bytes 1769480 | tf_op jit(solution)/shard_map/ppermute | solution.py:30
  21.4 10.1 %collective-permute-start.4 = (bf16[384,768]{1,0:T(8,128)(2,1)S(1)}, bf16[384,768]{1,0:T(8,128)(2,1)S(1)}, u32[]{:S(2)}, u32[]{:S(2)}) collective-permute-start(bf16[384,768]{1,0:T(8,128)(2,1)S(1)} %collective-permute-done.refs_1_), channel_id=1, source_target_pairs={{2,0},{3,1},{0,2},{1,3},{6,4},{7,5},{4,6},{5,7},{10,8},{11,9},{8,1... | collective-permute-start | bytes 1769480 | tf_op jit(solution)/shard_map/ppermute | solution.py:30
  23.3 17.6 %all-to-all-start.1 = ((bf16[16,16,768]{2,1,0:T(8,128)(2,1)}), bf16[16,16,768]{2,1,0:T(8,128)(2,1)}, u32[]{:S(2)}, u32[]{:S(2)}) async-start(bf16[16,16,768]{2,1,0:T(8,128)(2,1)} %bitcast.3), calls=%async_computation.1 | async-start | bytes 786432 | tf_op jit(solution)/shard_map/all_to_all | solution.py:297
  27.5 5.4 %copy-start.10 = (bf16[768]{0:T(1024)(128)(2,1)S(1)}, bf16[768]{0:T(1024)(128)(2,1)}, u32[]{:S(2)}) copy-start(bf16[768]{0:T(1024)(128)(2,1)} %param.19) | copy-start | bytes 4612
  27.5 17.9 %collective-permute-start.7 = (bf16[384,768]{1,0:T(8,128)(2,1)S(1)}, bf16[384,768]{1,0:T(8,128)(2,1)S(1)}, u32[]{:S(2)}, u32[]{:S(2)}) collective-permute-start(bf16[384,768]{1,0:T(8,128)(2,1)S(1)} %collective-permute-done.refs_1_), channel_id=1, source_target_pairs={{18,16},{19,17},{16,18},{17,19},{22,20},{23,21},{20,22},{21,23},{2... | collective-permute-start | bytes 1769480 | tf_op jit(solution)/shard_map/ppermute | solution.py:30
  31.5 13.9 %collective-permute-start.9 = (bf16[384,768]{1,0:T(8,128)(2,1)S(1)}, bf16[384,768]{1,0:T(8,128)(2,1)S(1)}, u32[]{:S(2)}, u32[]{:S(2)}) collective-permute-start(bf16[384,768]{1,0:T(8,128)(2,1)S(1)} %collective-permute-done.4.refs_3_), channel_id=1, source_target_pairs={{18,16},{19,17},{16,18},{17,19},{22,20},{23,21},{20,22},{21,23},{2... | collective-permute-start | bytes 1769480 | tf_op jit(solution)/shard_map/ppermute | solution.py:30
  32.9 0.7 copy-start.6
  32.9 0.7 copy-start.7
  33.5 0.9 %copy-start.4 = (bf16[128,768]{1,0:T(8,128)(2,1)S(1)}, bf16[128,768]{1,0:T(8,128)(2,1)}, u32[]{:S(2)}) copy-start(bf16[128,768]{1,0:T(8,128)(2,1)} %queries_ref.1) | copy-start | bytes 589828
  34.6 0.7 copy-start
  40.8 0.9 %copy-start.1 = (bf16[144,768]{1,0:T(8,128)(2,1)S(1)}, bf16[144,768]{1,0:T(8,128)(2,1)}, u32[]{:S(2)}) copy-start(bf16[144,768]{1,0:T(8,128)(2,1)} %copy-done) | copy-start | bytes 663556
  43.2 13.3 %copy-start.3 = (bf16[64,768]{1,0:T(8,128)(2,1)S(1)}, bf16[64,768]{1,0:T(8,128)(2,1)}, u32[]{:S(2)}) copy-start(bf16[64,768]{1,0:T(8,128)(2,1)} %refs_0_.3) | copy-start | bytes 294916
  43.2 6.7 %collective-permute-start.2 = (bf16[128,768]{1,0:T(8,128)(2,1)S(1)}, bf16[128,768]{1,0:T(8,128)(2,1)S(1)}, u32[]{:S(2)}, u32[]{:S(2)}) collective-permute-start(bf16[128,768]{1,0:T(8,128)(2,1)S(1)} %get-tuple-element.41.normed_ref), channel_id=1, source_target_pairs={{0,4},{1,5},{2,6},{3,7},{4,0},{5,1},{6,2},{7,3},{8,12},{9,13},{10,... | collective-permute-start | bytes 589832 | tf_op jit(solution)/shard_map/ppermute | solution.py:19
  44.9 5.1 %collective-permute-start.3 = (bf16[384,768]{1,0:T(8,128)(2,1)S(1)}, bf16[384,768]{1,0:T(8,128)(2,1)S(1)}, u32[]{:S(2)}, u32[]{:S(2)}) collective-permute-start(bf16[384,768]{1,0:T(8,128)(2,1)S(1)} %collective-permute-done.refs_1_), channel_id=1, source_target_pairs={{0,16},{16,0},{1,17},{17,1},{2,18},{18,2},{3,19},{19,3},{4,20},{20... | collective-permute-start | bytes 1769480 | tf_op jit(solution)/shard_map/ppermute | solution.py:19
  44.9 5.1 %collective-permute-start.6 = (bf16[384,768]{1,0:T(8,128)(2,1)S(1)}, bf16[384,768]{1,0:T(8,128)(2,1)S(1)}, u32[]{:S(2)}, u32[]{:S(2)}) collective-permute-start(bf16[384,768]{1,0:T(8,128)(2,1)S(1)} %collective-permute-done.1.refs_5_), channel_id=1, source_target_pairs={{0,16},{16,0},{1,17},{17,1},{2,18},{18,2},{3,19},{19,3},{4,20},{20... | collective-permute-start | bytes 1769480 | tf_op jit(solution)/shard_map/ppermute | solution.py:19
  45.4 4.6 %collective-permute-start.8 = (bf16[384,768]{1,0:T(8,128)(2,1)S(1)}, bf16[384,768]{1,0:T(8,128)(2,1)S(1)}, u32[]{:S(2)}, u32[]{:S(2)}) collective-permute-start(bf16[384,768]{1,0:T(8,128)(2,1)S(1)} %collective-permute-done.7.refs_8_), channel_id=1, source_target_pairs={{0,16},{16,0},{1,17},{17,1},{2,18},{18,2},{3,19},{19,3},{4,20},{20... | collective-permute-start | bytes 1769480 | tf_op jit(solution)/shard_map/ppermute | solution.py:19
  45.4 4.6 %collective-permute-start.5 = (bf16[384,768]{1,0:T(8,128)(2,1)S(1)}, bf16[384,768]{1,0:T(8,128)(2,1)S(1)}, u32[]{:S(2)}, u32[]{:S(2)}) collective-permute-start(bf16[384,768]{1,0:T(8,128)(2,1)S(1)} %collective-permute-done.4.refs_3_), channel_id=1, source_target_pairs={{0,16},{16,0},{1,17},{17,1},{2,18},{18,2},{3,19},{19,3},{4,20},{20... | collective-permute-start | bytes 1769480 | tf_op jit(solution)/shard_map/ppermute | solution.py:19
  50.0 2.0 %collective-permute-start.10 = (bf16[384,768]{1,0:T(8,128)(2,1)S(1)}, bf16[384,768]{1,0:T(8,128)(2,1)S(1)}, u32[]{:S(2)}, u32[]{:S(2)}) collective-permute-start(bf16[384,768]{1,0:T(8,128)(2,1)S(1)} %collective-permute-done.9.refs_10_), channel_id=1, source_target_pairs={{0,16},{16,0},{1,17},{17,1},{2,18},{18,2},{3,19},{19,3},{4,20},{20... | collective-permute-start | bytes 1769480 | tf_op jit(solution)/shard_map/ppermute | solution.py:19
  54.7 7.0 %collective-permute-start.11 = (bf16[128,768]{1,0:T(8,128)(2,1)S(1)}, bf16[128,768]{1,0:T(8,128)(2,1)S(1)}, u32[]{:S(2)}, u32[]{:S(2)}) collective-permute-start(bf16[128,768]{1,0:T(8,128)(2,1)S(1)} %shard_map.142), channel_id=1, source_target_pairs={{0,4},{1,5},{2,6},{3,7},{4,0},{5,1},{6,2},{7,3},{8,12},{9,13},{10,... | collective-permute-start | bytes 589832 | tf_op jit(solution)/shard_map/ppermute | solution.py:19
  56.5 2.8 %collective-permute-start.12 = (bf16[64,768]{1,0:T(8,128)(2,1)S(1)}, bf16[64,768]{1,0:T(8,128)(2,1)S(1)}, u32[]{:S(2)}, u32[]{:S(2)}) collective-permute-start(bf16[64,768]{1,0:T(8,128)(2,1)S(1)} %copy-done.3), channel_id=1, source_target_pairs={{0,16},{16,0},{1,17},{17,1},{2,18},{18,2},{3,19},{19,3},{4,20},{20... | collective-permute-start | bytes 294920 | tf_op jit(solution)/shard_map/ppermute | solution.py:19
  62.6 1.4 %collective-permute-start.13 = (bf16[64,768]{1,0:T(8,128)(2,1)S(1)}, bf16[64,768]{1,0:T(8,128)(2,1)S(1)}, u32[]{:S(2)}, u32[]{:S(2)}) collective-permute-start(bf16[64,768]{1,0:T(8,128)(2,1)S(1)} %get-tuple-element.51), channel_id=1, source_target_pairs={{0,16},{16,0},{1,17},{17,1},{2,18},{18,2},{3,19},{19,3},{4,20},{20... | collective-permute-start | bytes 294920 | tf_op jit(solution)/shard_map/ppermute | solution.py:19
  63.9 4.7 %collective-permute-start.14 = (bf16[64,768]{1,0:T(8,128)(2,1)S(1)}, bf16[64,768]{1,0:T(8,128)(2,1)S(1)}, u32[]{:S(2)}, u32[]{:S(2)}) collective-permute-start(bf16[64,768]{1,0:T(8,128)(2,1)S(1)} %add_convert_fusion.3), channel_id=1, source_target_pairs={{1,0},{0,1},{3,2},{2,3},{5,4},{4,5},{7,6},{6,7},{9,8},{8,9},{11,10... | collective-permute-start | bytes 294920 | tf_op jit(solution)/shard_map/ppermute | solution.py:30
  68.7 4.7 %collective-permute-start.15 = (bf16[64,768]{1,0:T(8,128)(2,1)S(1)}, bf16[64,768]{1,0:T(8,128)(2,1)S(1)}, u32[]{:S(2)}, u32[]{:S(2)}) collective-permute-start(bf16[64,768]{1,0:T(8,128)(2,1)S(1)} %add_convert_fusion.2), channel_id=1, source_target_pairs={{2,0},{3,1},{0,2},{1,3},{6,4},{7,5},{4,6},{5,7},{10,8},{11,9},{8,1... | collective-permute-start | bytes 294920 | tf_op jit(solution)/shard_map/ppermute | solution.py:30
  73.4 4.7 %collective-permute-start.16 = (bf16[64,768]{1,0:T(8,128)(2,1)S(1)}, bf16[64,768]{1,0:T(8,128)(2,1)S(1)}, u32[]{:S(2)}, u32[]{:S(2)}) collective-permute-start(bf16[64,768]{1,0:T(8,128)(2,1)S(1)} %add_convert_fusion.1), channel_id=1, source_target_pairs={{4,0},{5,1},{6,2},{7,3},{0,4},{1,5},{2,6},{3,7},{12,8},{13,9},{14,... | collective-permute-start | bytes 294920 | tf_op jit(solution)/shard_map/ppermute | solution.py:30
  78.1 5.6 %collective-permute-start.17 = (bf16[64,768]{1,0:T(8,128)(2,1)S(1)}, bf16[64,768]{1,0:T(8,128)(2,1)S(1)}, u32[]{:S(2)}, u32[]{:S(2)}) collective-permute-start(bf16[64,768]{1,0:T(8,128)(2,1)S(1)} %add_convert_fusion), channel_id=1, source_target_pairs={{8,0},{9,1},{10,2},{11,3},{12,4},{13,5},{14,6},{15,7},{0,8},{1,9},... | collective-permute-start | bytes 294920 | tf_op jit(solution)/shard_map/ppermute | solution.py:30

commit v7 on v6

--- a/solution.py
+++ b/solution.py
@@ -61,13 +61,13 @@
 
 def request_body(capacity, owner_ref, row_ref, bias_ref, message_ref):
     groups, _, width = message_ref.shape
-    bias_count = bias_ref.shape[1]
+    bias_count = bias_ref.shape[0]
     marks, rank = slots_of(owner_ref[...], groups)
     ranked = (rank.astype(jnp.int32) == iota((capacity, rank.shape[1]), 0)).astype(F32) * row_ref[...].astype(F32)
     request = lax.dot_general(
         marks.astype(BF16), ranked.astype(BF16), (((1,), (1,)), ((), ())), preferred_element_type=F32
     )
-    bias = jnp.broadcast_to(bias_ref[...].astype(F32), (groups, bias_count))
+    bias = jnp.broadcast_to(bias_ref[...].astype(F32)[None, :], (groups, bias_count))
     rest = jnp.zeros((groups, width - bias_count - capacity), F32)
     message_ref[...] = jnp.concatenate([bias, request, rest], axis=1).reshape(message_ref.shape)
 
@@ -92,7 +92,7 @@
     slot = owner * capacity + rank.astype(jnp.int32)
     small = jnp.concatenate([slot, positive // DIGIT, positive % DIGIT], axis=0).astype(F32)
     small = jnp.concatenate([small, jnp.zeros((3, features - chains), F32)], axis=1)
-    wide = jnp.concatenate([gain_ref[...], bias_ref[...]], axis=0).astype(F32)
+    wide = jnp.concatenate([ref[...].astype(F32)[None, :] for ref in (gain_ref, bias_ref)], axis=0)
     rest = jnp.zeros((TILE_ROWS - 5, features), F32)
     packed_ref[:chains, :] = queries_ref[...]
     packed_ref[chains:, :] = jnp.concatenate([small, wide, rest], axis=0).astype(BF16)
@@ -117,8 +117,8 @@
     return 0.5 * u * (1.0 + jnp.tanh(0.7978845608028654 * (u + 0.044715 * (u * u * u))))
 
 
-def hidden_body(plan, normed_ref, message_ref, *refs):
-    shards, (total_ref, held_in, held_out, sems) = refs[:-4], refs[-4:]
+def hidden_body(plan, continued, normed_ref, message_ref, *refs):
+    sums, shards, (total_ref, held_in, held_out, sems) = refs[:continued], refs[continued:-4], refs[-4:]
     units = held_in.shape[0] // len(plan)
     me, first_core = lax.axis_index("mp"), lax.axis_index("dp") % 2 == 0
     held = (held_in, held_out)
@@ -153,7 +153,10 @@
     activated = gelu(preact + bias).astype(BF16)
     for p, (_, at, _, _) in enumerate(plan):
         copy(at, p, 1).wait()
-    total_ref[...] = jnp.dot(activated, held_out[...], preferred_element_type=F32).astype(total_ref.dtype)
+    total = jnp.dot(activated, held_out[...], preferred_element_type=F32)
+    for sum_ref in sums:
+        total = total + sum_ref[...]
+    total_ref[...] = total.astype(total_ref.dtype)
 
 
 def score_body(
@@ -266,7 +269,7 @@
         whole((groups, 1, width), F32),
         owner_row,
         first_row.reshape(1, chains),
-        bias_in.reshape(1, units),
+        bias_in,
     )
     asked = lax.all_to_all(message, "mp", split_axis=0, concat_axis=0, tiled=True)
     served = kernel_call(
@@ -280,8 +283,8 @@
         whole((chains + TILE_ROWS, features), BF16),
         after(owner_row, served),
         positive.reshape(1, chains),
-        norm_gain.reshape(1, features),
-        bias_out.reshape(1, features),
+        norm_gain,
+        bias_out,
         queries,
     )
     own = jnp.concatenate([weight_in, weight_out], axis=0)
@@ -303,22 +306,23 @@
     )
 
     pieces = shared_pieces(own, symmetric, *single, normed)
-    shards = []
-    for piece in pieces:
-        for shard in (piece[1], piece[3]):
-            if all(shard is not s for s in shards):
-                shards.append(shard)
-    index_of = {id(s): i for i, s in enumerate(shards)}
-    plan = tuple((mask, index_of[id(s)], other, index_of[id(t)]) for mask, s, other, t in pieces)
-
-    def hidden(rows, held_as):
+    def hidden(rows, some, held_as, *so_far):
+        shards = []
+        for piece in some:
+            for shard in (piece[1], piece[3]):
+                if all(shard is not s for s in shards):
+                    shards.append(shard)
+        index_of = {id(s): i for i, s in enumerate(shards)}
+        plan = tuple((mask, index_of[id(s)], other, index_of[id(t)]) for mask, s, other, t in some)
+        first = 2 + len(so_far)
         return kernel_call(
-            functools.partial(hidden_body, plan),
+            functools.partial(hidden_body, plan, len(so_far)),
             whole((chains, features), held_as),
             rows,
             asked,
+            *so_far,
             *shards,
-            in_place=range(2, 2 + len(shards)),
+            in_place=range(first, first + len(shards)),
             scratch=(
                 pltpu.VMEM((len(plan) * units, features), BF16),
                 pltpu.VMEM((len(plan) * units, features), BF16),
@@ -327,8 +331,11 @@
             vmem=LARGE_VMEM,
         )
 
-    neighbour = hidden(flipped(normed, "mp", 4), BF16)
-    total = hidden(after(normed, neighbour), F32)
+    neighbour_normed = flipped(normed, "mp", 4)
+    neighbour = hidden(
+        neighbour_normed, pieces[-1:], BF16, hidden(neighbour_normed, pieces[:-1], F32)
+    )
+    total = hidden(after(normed, neighbour), pieces, F32)
     late_tools = after(tool_embeds, neighbour)
     tools = [tool_embeds] + [flipped(late_tools, "dp", j) for j in range(1, cycle)]
     updated, loss, weights, *grads = kernel_call(

time: 84.8 us -> 83.9 us (0.989)
  waiting for transfers between devices: 28.2 us -> 25.5 us
  starting transfers between devices: 25.4 us -> 26.6 us
    ppermute x9, waiting for transfers between devices: 7.31 us -> 5.48 us  [flipped(): lax.ppermute(block, axis, [(i, i ^ mask) for i in range(lax.axis_size(axi...]
    unnamed x25 -> x27, local copies, waits for them, and re-layouts: 4.93 us -> 5.64 us
    pallas_call x8 -> x9, Pallas kernels: 10.6 us -> 11.1 us  [kernel_call(): pl.pallas_call(body, out_shape=out_shape, in_specs=[pl.BlockSpec(memory_s...]
  transfers between devices with their start and end apart: 19 -> 19, of which waited for: 10 -> 9; matrix products, arithmetic and copies ran while one was open for 2% -> 1% of each run, Pallas kernels for 8% -> 12%
where the time goes in v7:
time: 83.9 us; the launch traced here: 83.4 us
  starting transfers between devices  26.6 us (32%)
  waiting for transfers between devices  25.5 us (30%)
  blocking collectives  12.2 us (15%)
  Pallas kernels  11.1 us (13%)
  local copies, waits for them, and re-layouts  5.67 us (7%)
  other arithmetic  1.43 us (2%)
  between operations  0.87 us (1%)
    ppermute x9, starting transfers between devices, moved(): return lax.ppermute(block, ('dp', 'mp'), route)  15 us
    ppermute x9, waiting for transfers between devices, moved(): return lax.ppermute(block, ('dp', 'mp'), route)  14.6 us
    all_to_all x1, blocking collectives, local(): lax.all_to_all(message, 'mp', split_axis=0, concat_axis=0, tiled=True)  12.2 us
    pallas_call x9, Pallas kernels, kernel_call(): pl.pallas_call(body, out_shape=out_shape, in_specs=[pl.BlockSpec(memory_s...  11.1 us
    ppermute x9, starting transfers between devices, flipped(): lax.ppermute(block, axis, [(i, i ^ mask) for i in range(lax.axis_size(axi...  7.36 us
    unnamed x27, local copies, waits for them, and re-layouts  5.64 us
    all_to_all x1, waiting for transfers between devices, local(): lax.all_to_all(held[0], 'mp', split_axis=0, concat_axis=0, tiled=True)  5.5 us
    ppermute x9, waiting for transfers between devices, flipped(): lax.ppermute(block, axis, [(i, i ^ mask) for i in range(lax.axis_size(axi...  5.48 us
  transfers between devices with their start and end apart: 19, of which 9 were waited for; matrix products, arithmetic and copies ran while one was open for 1% of the time, Pallas kernels for 12%

profile of v7, /device:TPU:0, one launch (start us, length us, event | category | flops | bytes accessed | tf_op | source)
XLA Modules:
  0.0 83.4 jit_solution(5272699427554062202)
XLA Ops:
  0.6 1.0 %constant_dynamic-update-slice_fusion.1 = bf16[384,768]{1,0:T(8,128)(2,1)S(1)} fusion(bf16[192,768]{1,0:T(8,128)(2,1)} %param.16), kind=kLoop, calls=%fused_computation.6 | loop fusion | bytes 589824
  1.7 3.0 %collective-permute-start = (bf16[384,768]{1,0:T(8,128)(2,1)S(1)}, bf16[384,768]{1,0:T(8,128)(2,1)S(1)}, u32[]{:S(2)}, u32[]{:S(2)}) collective-permute-start(bf16[384,768]{1,0:T(8,128)(2,1)S(1)} %constant_dynamic-update-slice_fusion.refs_0_), channel_id=1, source_target_pairs={{1,0},{0,1},{3,2},{2,3},{5,4},{4,5},{7,6},{6,7},{9,8},{8,9},{11,10... | collective-permute-start | bytes 1769480 | tf_op jit(solution)/shard_map/ppermute | solution.py:30
  5.8 3.4 %collective-permute-start.1 = (bf16[384,768]{1,0:T(8,128)(2,1)S(1)}, bf16[384,768]{1,0:T(8,128)(2,1)S(1)}, u32[]{:S(2)}, u32[]{:S(2)}) collective-permute-start(bf16[384,768]{1,0:T(8,128)(2,1)S(1)} %constant_dynamic-update-slice_fusion.refs_0_), channel_id=1, source_target_pairs={{2,0},{3,1},{0,2},{1,3},{6,4},{7,5},{4,6},{5,7},{10,8},{11,9},{8,1... | collective-permute-start | bytes 1769480 | tf_op jit(solution)/shard_map/ppermute | solution.py:30
  9.2 12.2 %all_to_all.16.message_ref = f32[16,1,256]{2,1,0:T(1,128)S(1)} all-to-all(f32[16,1,256]{2,1,0:T(1,128)S(1)} %shard_map.138), channel_id=1, replica_groups=mesh['dp'=2,'mp'=16] {'mp'}, dimensions={0} | all-to-all | bytes 32768 | tf_op jit(solution)/shard_map/all_to_all | solution.py:274
  22.0 1.3 %shard_map.139 = bf16[256,768]{1,0:T(8,128)(2,1)} custom-call(f32[16,1,256]{2,1,0:T(1,128)S(1)} %all_to_all.16.message_ref, bf16[256,768]{1,0:T(8,128)(2,1)S(1)} %copy-done.2), custom_call_target="tpu_custom_call" | custom-call | tf_op jit(solution)/shard_map/pallas_call | solution.py:38
  23.3 4.2 %all-to-all-start.1 = ((bf16[16,16,768]{2,1,0:T(8,128)(2,1)}), bf16[16,16,768]{2,1,0:T(8,128)(2,1)}, u32[]{:S(2)}, u32[]{:S(2)}) async-start(bf16[16,16,768]{2,1,0:T(8,128)(2,1)} %bitcast.3), calls=%async_computation.1 | async-start | bytes 786432 | tf_op jit(solution)/shard_map/all_to_all | solution.py:300
  27.5 0.7 collective-permute-start.7
  28.2 3.3 %collective-permute-done.4.refs_3_ = bf16[384,768]{1,0:T(8,128)(2,1)S(1)} collective-permute-done((bf16[384,768]{1,0:T(8,128)(2,1)S(1)}, bf16[384,768]{1,0:T(8,128)(2,1)S(1)}, u32[]{:S(2)}, u32[]{:S(2)}) %collective-permute-start.4) | collective-permute-done | bytes 589856 | tf_op jit(solution)/shard_map/ppermute | solution.py:30
  32.2 0.9 %copy-done.4 = bf16[128,768]{1,0:T(8,128)(2,1)S(1)} copy-done((bf16[128,768]{1,0:T(8,128)(2,1)S(1)}, bf16[128,768]{1,0:T(8,128)(2,1)}, u32[]{:S(2)}) %copy-start.4) | copy-done | bytes 196632
  35.3 5.5 %all-to-all-done.1 = bf16[16,16,768]{2,1,0:T(8,128)(2,1)} async-done(((bf16[16,16,768]{2,1,0:T(8,128)(2,1)}), bf16[16,16,768]{2,1,0:T(8,128)(2,1)}, u32[]{:S(2)}, u32[]{:S(2)}) %all-to-all-start.1) | async-done | bytes 393248 | tf_op jit(solution)/shard_map/all_to_all | solution.py:300
  40.8 0.9 %copy-done.1 = bf16[144,768]{1,0:T(8,128)(2,1)S(1)} copy-done((bf16[144,768]{1,0:T(8,128)(2,1)S(1)}, bf16[144,768]{1,0:T(8,128)(2,1)}, u32[]{:S(2)}) %copy-start.1) | copy-done | bytes 221208
  41.8 1.4 %shard_map.141 = (f32[128,768]{1,0:T(8,128)S(1)}, bf16[128,768]{1,0:T(8,128)(2,1)S(1)}, s32[1,128]{1,0:T(1,128)S(1)}) custom-call(bf16[144,768]{1,0:T(8,128)(2,1)S(1)} %copy-done.1, bf16[256,768]{1,0:T(8,128)(2,1)} %bitcast.4.fetched_ref), custom_call_target="tpu_custom_call" | custom-call | tf_op jit(solution)/shard_map/pallas_call | solution.py:38
  43.2 1.6 %collective-permute-start.2 = (bf16[128,768]{1,0:T(8,128)(2,1)S(1)}, bf16[128,768]{1,0:T(8,128)(2,1)S(1)}, u32[]{:S(2)}, u32[]{:S(2)}) collective-permute-start(bf16[128,768]{1,0:T(8,128)(2,1)S(1)} %get-tuple-element.41.normed_ref), channel_id=1, source_target_pairs={{0,4},{1,5},{2,6},{3,7},{4,0},{5,1},{6,2},{7,3},{8,12},{9,13},{10,... | collective-permute-start | bytes 589832 | tf_op jit(solution)/shard_map/ppermute | solution.py:19
  45.4 3.0 %collective-permute-start.5 = (bf16[384,768]{1,0:T(8,128)(2,1)S(1)}, bf16[384,768]{1,0:T(8,128)(2,1)S(1)}, u32[]{:S(2)}, u32[]{:S(2)}) collective-permute-start(bf16[384,768]{1,0:T(8,128)(2,1)S(1)} %collective-permute-done.4.refs_3_), channel_id=1, source_target_pairs={{0,16},{16,0},{1,17},{17,1},{2,18},{18,2},{3,19},{19,3},{4,20},{20... | collective-permute-start | bytes 1769480 | tf_op jit(solution)/shard_map/ppermute | solution.py:19
  48.3 1.6 %collective-permute-done.2.normed_ref = bf16[128,768]{1,0:T(8,128)(2,1)S(1)} collective-permute-done((bf16[128,768]{1,0:T(8,128)(2,1)S(1)}, bf16[128,768]{1,0:T(8,128)(2,1)S(1)}, u32[]{:S(2)}, u32[]{:S(2)}) %collective-permute-start.2) | collective-permute-done | bytes 196640 | tf_op jit(solution)/shard_map/ppermute | solution.py:19
  50.0 2.6 %shard_map.142.refs_0_ = f32[128,768]{1,0:T(8,128)S(1)} custom-call(bf16[128,768]{1,0:T(8,128)(2,1)S(1)} %collective-permute-done.2.normed_ref, f32[16,1,256]{2,1,0:T(1,128)S(1)} %all_to_all.16.message_ref, bf16[384,768]{1,0:T(8,128)(2,1)S(1)} %constant_dynamic-update-slice_fusion.refs_0_, bf16[384,768]{1,0:T(8,128)(2,1)S(1)} %collective-permute-done.refs_1_, ...), custom_call_target="tpu_custom_call" | custom-call | tf_op jit(solution)/shard_map/pallas_call | solution.py:38
  52.6 0.7 shard_map.143
  53.3 2.1 %collective-permute-start.11 = (bf16[128,768]{1,0:T(8,128)(2,1)S(1)}, bf16[128,768]{1,0:T(8,128)(2,1)S(1)}, u32[]{:S(2)}, u32[]{:S(2)}) collective-permute-start(bf16[128,768]{1,0:T(8,128)(2,1)S(1)} %shard_map.143), channel_id=1, source_target_pairs={{0,4},{1,5},{2,6},{3,7},{4,0},{5,1},{6,2},{7,3},{8,12},{9,13},{10,... | collective-permute-start | bytes 589832 | tf_op jit(solution)/shard_map/ppermute | solution.py:19
  55.5 2.8 %shard_map.144.total_ref = f32[128,768]{1,0:T(8,128)S(1)} custom-call(bf16[128,768]{1,0:T(8,128)(2,1)S(1)} %get-tuple-element.41.normed_ref, f32[16,1,256]{2,1,0:T(1,128)S(1)} %all_to_all.16.message_ref, bf16[384,768]{1,0:T(8,128)(2,1)S(1)} %constant_dynamic-update-slice_fusion.refs_0_, bf16[384,768]{1,0:T(8,128)(2,1)S(1)} %collective-permute-done.refs_1_, ...), custom_call_target="tpu_custom_call" | custom-call | tf_op jit(solution)/shard_map/pallas_call | solution.py:38
  58.3 2.6 %collective-permute-done.11.other_ref = bf16[128,768]{1,0:T(8,128)(2,1)S(1)} collective-permute-done((bf16[128,768]{1,0:T(8,128)(2,1)S(1)}, bf16[128,768]{1,0:T(8,128)(2,1)S(1)}, u32[]{:S(2)}, u32[]{:S(2)}) %collective-permute-start.11) | collective-permute-done | bytes 196640 | tf_op jit(solution)/shard_map/ppermute | solution.py:19
  60.8 0.8 shard_map.145
  61.7 1.3 %collective-permute-done.13 = bf16[64,768]{1,0:T(8,128)(2,1)S(1)} collective-permute-done((bf16[64,768]{1,0:T(8,128)(2,1)S(1)}, bf16[64,768]{1,0:T(8,128)(2,1)S(1)}, u32[]{:S(2)}, u32[]{:S(2)}) %collective-permute-start.13) | collective-permute-done | bytes 98336 | tf_op jit(solution)/shard_map/ppermute | solution.py:19
  63.0 1.5 %collective-permute-start.14 = (bf16[64,768]{1,0:T(8,128)(2,1)S(1)}, bf16[64,768]{1,0:T(8,128)(2,1)S(1)}, u32[]{:S(2)}, u32[]{:S(2)}) collective-permute-start(bf16[64,768]{1,0:T(8,128)(2,1)S(1)} %add_convert_fusion.3), channel_id=1, source_target_pairs={{1,0},{0,1},{3,2},{2,3},{5,4},{4,5},{7,6},{6,7},{9,8},{8,9},{11,10... | collective-permute-start | bytes 294920 | tf_op jit(solution)/shard_map/ppermute | solution.py:30
  64.5 3.2 %collective-permute-done.14 = bf16[64,768]{1,0:T(8,128)(2,1)S(1)} collective-permute-done((bf16[64,768]{1,0:T(8,128)(2,1)S(1)}, bf16[64,768]{1,0:T(8,128)(2,1)S(1)}, u32[]{:S(2)}, u32[]{:S(2)}) %collective-permute-start.14) | collective-permute-done | bytes 98336 | tf_op jit(solution)/shard_map/ppermute | solution.py:30
  67.7 1.1 %collective-permute-start.15 = (bf16[64,768]{1,0:T(8,128)(2,1)S(1)}, bf16[64,768]{1,0:T(8,128)(2,1)S(1)}, u32[]{:S(2)}, u32[]{:S(2)}) collective-permute-start(bf16[64,768]{1,0:T(8,128)(2,1)S(1)} %add_convert_fusion.2), channel_id=1, source_target_pairs={{2,0},{3,1},{0,2},{1,3},{6,4},{7,5},{4,6},{5,7},{10,8},{11,9},{8,1... | collective-permute-start | bytes 294920 | tf_op jit(solution)/shard_map/ppermute | solution.py:30
  68.9 3.5 %collective-permute-done.15 = bf16[64,768]{1,0:T(8,128)(2,1)S(1)} collective-permute-done((bf16[64,768]{1,0:T(8,128)(2,1)S(1)}, bf16[64,768]{1,0:T(8,128)(2,1)S(1)}, u32[]{:S(2)}, u32[]{:S(2)}) %collective-permute-start.15) | collective-permute-done | bytes 98336 | tf_op jit(solution)/shard_map/ppermute | solution.py:30
  72.4 1.8 %collective-permute-start.16 = (bf16[64,768]{1,0:T(8,128)(2,1)S(1)}, bf16[64,768]{1,0:T(8,128)(2,1)S(1)}, u32[]{:S(2)}, u32[]{:S(2)}) collective-permute-start(bf16[64,768]{1,0:T(8,128)(2,1)S(1)} %add_convert_fusion.1), channel_id=1, source_target_pairs={{4,0},{5,1},{6,2},{7,3},{0,4},{1,5},{2,6},{3,7},{12,8},{13,9},{14,... | collective-permute-start | bytes 294920 | tf_op jit(solution)/shard_map/ppermute | solution.py:30
  74.2 2.9 %collective-permute-done.16 = bf16[64,768]{1,0:T(8,128)(2,1)S(1)} collective-permute-done((bf16[64,768]{1,0:T(8,128)(2,1)S(1)}, bf16[64,768]{1,0:T(8,128)(2,1)S(1)}, u32[]{:S(2)}, u32[]{:S(2)}) %collective-permute-start.16) | collective-permute-done | bytes 98336 | tf_op jit(solution)/shard_map/ppermute | solution.py:30
  77.2 2.2 %collective-permute-start.17 = (bf16[64,768]{1,0:T(8,128)(2,1)S(1)}, bf16[64,768]{1,0:T(8,128)(2,1)S(1)}, u32[]{:S(2)}, u32[]{:S(2)}) collective-permute-start(bf16[64,768]{1,0:T(8,128)(2,1)S(1)} %add_convert_fusion), channel_id=1, source_target_pairs={{8,0},{9,1},{10,2},{11,3},{12,4},{13,5},{14,6},{15,7},{0,8},{1,9},... | collective-permute-start | bytes 294920 | tf_op jit(solution)/shard_map/ppermute | solution.py:30
  79.3 1.1 %shard_map.146 = (f32[128,768]{1,0:T(8,128)}, bf16[128,768]{1,0:T(8,128)(2,1)}, f32[128,1]{1,0:T(8,128)S(1)}) custom-call(bf16[128,128]{1,0:T(8,128)(2,1)S(1)} %get-tuple-element.44.weights_ref, bf16[128,768]{1,0:T(8,128)(2,1)S(1)} %get-tuple-element.45.updated_ref, f32[128,1]{1,0:T(8,128)S(1)} %get-tuple-element.46.loss_ref, bf16[64,768]{1,0:T(8,128)(2,1)S(1)} %copy-done.3, ...), custom_call_target="tpu_custom_call" | custom-call | tf_op jit(solution)/shard_map/pallas_call | solution.py:38
  81.0 1.7 %collective-permute-done.17 = bf16[64,768]{1,0:T(8,128)(2,1)S(1)} collective-permute-done((bf16[64,768]{1,0:T(8,128)(2,1)S(1)}, bf16[64,768]{1,0:T(8,128)(2,1)S(1)}, u32[]{:S(2)}, u32[]{:S(2)}) %collective-permute-start.17) | collective-permute-done | bytes 98336 | tf_op jit(solution)/shard_map/ppermute | solution.py:30
  82.7 0.7 add_multiply_fusion
  (50 shorter events, 6.0 us)
Async XLA Ops:
  0.6 1.1 %copy-start.12 = (bf16[192,768]{1,0:T(8,128)(2,1)S(1)}, bf16[192,768]{1,0:T(8,128)(2,1)}, u32[]{:S(2)}) copy-start(bf16[192,768]{1,0:T(8,128)(2,1)} %param.18) | copy-start | bytes 884740
  1.7 20.3 %copy-start.2 = (bf16[256,768]{1,0:T(8,128)(2,1)S(1)}, bf16[256,768]{1,0:T(8,128)(2,1)}, u32[]{:S(2)}) copy-start(bf16[256,768]{1,0:T(8,128)(2,1)} %table_ref.1) | copy-start | bytes 1179652
  1.7 19.7 %collective-permute-start = (bf16[384,768]{1,0:T(8,128)(2,1)S(1)}, bf16[384,768]{1,0:T(8,128)(2,1)S(1)}, u32[]{:S(2)}, u32[]{:S(2)}) collective-permute-start(bf16[384,768]{1,0:T(8,128)(2,1)S(1)} %constant_dynamic-update-slice_fusion.refs_0_), channel_id=1, source_target_pairs={{1,0},{0,1},{3,2},{2,3},{5,4},{4,5},{7,6},{6,7},{9,8},{8,9},{11,10... | collective-permute-start | bytes 1769480 | tf_op jit(solution)/shard_map/ppermute | solution.py:30
  4.7 0.7 copy-start.7
  4.7 0.7 copy-start.10
  4.7 0.7 copy-start.11
  5.8 17.5 %collective-permute-start.1 = (bf16[384,768]{1,0:T(8,128)(2,1)S(1)}, bf16[384,768]{1,0:T(8,128)(2,1)S(1)}, u32[]{:S(2)}, u32[]{:S(2)}) collective-permute-start(bf16[384,768]{1,0:T(8,128)(2,1)S(1)} %constant_dynamic-update-slice_fusion.refs_0_), channel_id=1, source_target_pairs={{2,0},{3,1},{0,2},{1,3},{6,4},{7,5},{4,6},{5,7},{10,8},{11,9},{8,1... | collective-permute-start | bytes 1769480 | tf_op jit(solution)/shard_map/ppermute | solution.py:30
  21.4 10.1 %collective-permute-start.4 = (bf16[384,768]{1,0:T(8,128)(2,1)S(1)}, bf16[384,768]{1,0:T(8,128)(2,1)S(1)}, u32[]{:S(2)}, u32[]{:S(2)}) collective-permute-start(bf16[384,768]{1,0:T(8,128)(2,1)S(1)} %collective-permute-done.refs_1_), channel_id=1, source_target_pairs={{2,0},{3,1},{0,2},{1,3},{6,4},{7,5},{4,6},{5,7},{10,8},{11,9},{8,1... | collective-permute-start | bytes 1769480 | tf_op jit(solution)/shard_map/ppermute | solution.py:30
  23.3 17.6 %all-to-all-start.1 = ((bf16[16,16,768]{2,1,0:T(8,128)(2,1)}), bf16[16,16,768]{2,1,0:T(8,128)(2,1)}, u32[]{:S(2)}, u32[]{:S(2)}) async-start(bf16[16,16,768]{2,1,0:T(8,128)(2,1)} %bitcast.3), calls=%async_computation.1 | async-start | bytes 786432 | tf_op jit(solution)/shard_map/all_to_all | solution.py:300
  27.5 4.7 %copy-start.8 = (s32[128,1]{0,1:T(1,128)S(1)}, s32[128,1]{0,1:T(1,128)}, u32[]{:S(2)}) copy-start(s32[128,1]{0,1:T(1,128)} %param.12) | copy-start | bytes 1540
  27.5 4.7 %copy-start.9 = (s32[128]{0:T(128)S(1)}, s32[128]{0:T(128)}, u32[]{:S(2)}) copy-start(s32[128]{0:T(128)} %param.21) | copy-start | bytes 1540
  27.5 17.8 %collective-permute-start.7 = (bf16[384,768]{1,0:T(8,128)(2,1)S(1)}, bf16[384,768]{1,0:T(8,128)(2,1)S(1)}, u32[]{:S(2)}, u32[]{:S(2)}) collective-permute-start(bf16[384,768]{1,0:T(8,128)(2,1)S(1)} %collective-permute-done.refs_1_), channel_id=1, source_target_pairs={{18,16},{19,17},{16,18},{17,19},{22,20},{23,21},{20,22},{21,23},{2... | collective-permute-start | bytes 1769480 | tf_op jit(solution)/shard_map/ppermute | solution.py:30
  31.5 13.9 %collective-permute-start.9 = (bf16[384,768]{1,0:T(8,128)(2,1)S(1)}, bf16[384,768]{1,0:T(8,128)(2,1)S(1)}, u32[]{:S(2)}, u32[]{:S(2)}) collective-permute-start(bf16[384,768]{1,0:T(8,128)(2,1)S(1)} %collective-permute-done.4.refs_3_), channel_id=1, source_target_pairs={{18,16},{19,17},{16,18},{17,19},{22,20},{23,21},{20,22},{21,23},{2... | collective-permute-start | bytes 1769480 | tf_op jit(solution)/shard_map/ppermute | solution.py:30
  32.2 0.9 %copy-start.4 = (bf16[128,768]{1,0:T(8,128)(2,1)S(1)}, bf16[128,768]{1,0:T(8,128)(2,1)}, u32[]{:S(2)}) copy-start(bf16[128,768]{1,0:T(8,128)(2,1)} %queries_ref.1) | copy-start | bytes 589828
  33.1 0.7 copy-start.5
  33.8 0.7 copy-start.6
  34.6 0.7 copy-start
  40.8 0.9 %copy-start.1 = (bf16[144,768]{1,0:T(8,128)(2,1)S(1)}, bf16[144,768]{1,0:T(8,128)(2,1)}, u32[]{:S(2)}) copy-start(bf16[144,768]{1,0:T(8,128)(2,1)} %copy-done) | copy-start | bytes 663556
  43.2 6.7 %collective-permute-start.2 = (bf16[128,768]{1,0:T(8,128)(2,1)S(1)}, bf16[128,768]{1,0:T(8,128)(2,1)S(1)}, u32[]{:S(2)}, u32[]{:S(2)}) collective-permute-start(bf16[128,768]{1,0:T(8,128)(2,1)S(1)} %get-tuple-element.41.normed_ref), channel_id=1, source_target_pairs={{0,4},{1,5},{2,6},{3,7},{4,0},{5,1},{6,2},{7,3},{8,12},{9,13},{10,... | collective-permute-start | bytes 589832 | tf_op jit(solution)/shard_map/ppermute | solution.py:19
  44.8 5.1 %collective-permute-start.3 = (bf16[384,768]{1,0:T(8,128)(2,1)S(1)}, bf16[384,768]{1,0:T(8,128)(2,1)S(1)}, u32[]{:S(2)}, u32[]{:S(2)}) collective-permute-start(bf16[384,768]{1,0:T(8,128)(2,1)S(1)} %collective-permute-done.refs_1_), channel_id=1, source_target_pairs={{0,16},{16,0},{1,17},{17,1},{2,18},{18,2},{3,19},{19,3},{4,20},{20... | collective-permute-start | bytes 1769480 | tf_op jit(solution)/shard_map/ppermute | solution.py:19
  44.8 5.1 %collective-permute-start.6 = (bf16[384,768]{1,0:T(8,128)(2,1)S(1)}, bf16[384,768]{1,0:T(8,128)(2,1)S(1)}, u32[]{:S(2)}, u32[]{:S(2)}) collective-permute-start(bf16[384,768]{1,0:T(8,128)(2,1)S(1)} %collective-permute-done.1.refs_5_), channel_id=1, source_target_pairs={{0,16},{16,0},{1,17},{17,1},{2,18},{18,2},{3,19},{19,3},{4,20},{20... | collective-permute-start | bytes 1769480 | tf_op jit(solution)/shard_map/ppermute | solution.py:19
  45.3 4.6 %collective-permute-start.8 = (bf16[384,768]{1,0:T(8,128)(2,1)S(1)}, bf16[384,768]{1,0:T(8,128)(2,1)S(1)}, u32[]{:S(2)}, u32[]{:S(2)}) collective-permute-start(bf16[384,768]{1,0:T(8,128)(2,1)S(1)} %collective-permute-done.7.refs_8_), channel_id=1, source_target_pairs={{0,16},{16,0},{1,17},{17,1},{2,18},{18,2},{3,19},{19,3},{4,20},{20... | collective-permute-start | bytes 1769480 | tf_op jit(solution)/shard_map/ppermute | solution.py:19
  45.4 4.6 %collective-permute-start.5 = (bf16[384,768]{1,0:T(8,128)(2,1)S(1)}, bf16[384,768]{1,0:T(8,128)(2,1)S(1)}, u32[]{:S(2)}, u32[]{:S(2)}) collective-permute-start(bf16[384,768]{1,0:T(8,128)(2,1)S(1)} %collective-permute-done.4.refs_3_), channel_id=1, source_target_pairs={{0,16},{16,0},{1,17},{17,1},{2,18},{18,2},{3,19},{19,3},{4,20},{20... | collective-permute-start | bytes 1769480 | tf_op jit(solution)/shard_map/ppermute | solution.py:19
  49.9 2.6 %collective-permute-start.10 = (bf16[384,768]{1,0:T(8,128)(2,1)S(1)}, bf16[384,768]{1,0:T(8,128)(2,1)S(1)}, u32[]{:S(2)}, u32[]{:S(2)}) collective-permute-start(bf16[384,768]{1,0:T(8,128)(2,1)S(1)} %collective-permute-done.9.refs_2_.refs_10_), channel_id=1, source_target_pairs={{0,16},{16,0},{1,17},{17,1},{2,18},{18,2},{3,19},{19,3},{4,20},{20... | collective-permute-start | bytes 1769480 | tf_op jit(solution)/shard_map/ppermute | solution.py:19
  52.6 2.9 %copy-start.3 = (bf16[64,768]{1,0:T(8,128)(2,1)S(1)}, bf16[64,768]{1,0:T(8,128)(2,1)}, u32[]{:S(2)}) copy-start(bf16[64,768]{1,0:T(8,128)(2,1)} %refs_0_.3) | copy-start | bytes 294916
  53.3 7.5 %collective-permute-start.11 = (bf16[128,768]{1,0:T(8,128)(2,1)S(1)}, bf16[128,768]{1,0:T(8,128)(2,1)S(1)}, u32[]{:S(2)}, u32[]{:S(2)}) collective-permute-start(bf16[128,768]{1,0:T(8,128)(2,1)S(1)} %shard_map.143), channel_id=1, source_target_pairs={{0,4},{1,5},{2,6},{3,7},{4,0},{5,1},{6,2},{7,3},{8,12},{9,13},{10,... | collective-permute-start | bytes 589832 | tf_op jit(solution)/shard_map/ppermute | solution.py:19
  55.4 2.8 %collective-permute-start.12 = (bf16[64,768]{1,0:T(8,128)(2,1)S(1)}, bf16[64,768]{1,0:T(8,128)(2,1)S(1)}, u32[]{:S(2)}, u32[]{:S(2)}) collective-permute-start(bf16[64,768]{1,0:T(8,128)(2,1)S(1)} %copy-done.3), channel_id=1, source_target_pairs={{0,16},{16,0},{1,17},{17,1},{2,18},{18,2},{3,19},{19,3},{4,20},{20... | collective-permute-start | bytes 294920 | tf_op jit(solution)/shard_map/ppermute | solution.py:19
  61.6 1.4 %collective-permute-start.13 = (bf16[64,768]{1,0:T(8,128)(2,1)S(1)}, bf16[64,768]{1,0:T(8,128)(2,1)S(1)}, u32[]{:S(2)}, u32[]{:S(2)}) collective-permute-start(bf16[64,768]{1,0:T(8,128)(2,1)S(1)} %get-tuple-element.51), channel_id=1, source_target_pairs={{0,16},{16,0},{1,17},{17,1},{2,18},{18,2},{3,19},{19,3},{4,20},{20... | collective-permute-start | bytes 294920 | tf_op jit(solution)/shard_map/ppermute | solution.py:19
  63.0 4.7 %collective-permute-start.14 = (bf16[64,768]{1,0:T(8,128)(2,1)S(1)}, bf16[64,768]{1,0:T(8,128)(2,1)S(1)}, u32[]{:S(2)}, u32[]{:S(2)}) collective-permute-start(bf16[64,768]{1,0:T(8,128)(2,1)S(1)} %add_convert_fusion.3), channel_id=1, source_target_pairs={{1,0},{0,1},{3,2},{2,3},{5,4},{4,5},{7,6},{6,7},{9,8},{8,9},{11,10... | collective-permute-start | bytes 294920 | tf_op jit(solution)/shard_map/ppermute | solution.py:30
  67.7 4.7 %collective-permute-start.15 = (bf16[64,768]{1,0:T(8,128)(2,1)S(1)}, bf16[64,768]{1,0:T(8,128)(2,1)S(1)}, u32[]{:S(2)}, u32[]{:S(2)}) collective-permute-start(bf16[64,768]{1,0:T(8,128)(2,1)S(1)} %add_convert_fusion.2), channel_id=1, source_target_pairs={{2,0},{3,1},{0,2},{1,3},{6,4},{7,5},{4,6},{5,7},{10,8},{11,9},{8,1... | collective-permute-start | bytes 294920 | tf_op jit(solution)/shard_map/ppermute | solution.py:30
  72.4 4.7 %collective-permute-start.16 = (bf16[64,768]{1,0:T(8,128)(2,1)S(1)}, bf16[64,768]{1,0:T(8,128)(2,1)S(1)}, u32[]{:S(2)}, u32[]{:S(2)}) collective-permute-start(bf16[64,768]{1,0:T(8,128)(2,1)S(1)} %add_convert_fusion.1), channel_id=1, source_target_pairs={{4,0},{5,1},{6,2},{7,3},{0,4},{1,5},{2,6},{3,7},{12,8},{13,9},{14,... | collective-permute-start | bytes 294920 | tf_op jit(solution)/shard_map/ppermute | solution.py:30
  77.2 5.6 %collective-permute-start.17 = (bf16[64,768]{1,0:T(8,128)(2,1)S(1)}, bf16[64,768]{1,0:T(8,128)(2,1)S(1)}, u32[]{:S(2)}, u32[]{:S(2)}) collective-permute-start(bf16[64,768]{1,0:T(8,128)(2,1)S(1)} %add_convert_fusion), channel_id=1, source_target_pairs={{8,0},{9,1},{10,2},{11,3},{12,4},{13,5},{14,6},{15,7},{0,8},{1,9},... | collective-permute-start | bytes 294920 | tf_op jit(solution)/shard_map/ppermute | solution.py:30

commit v8 on v7

--- a/solution.py
+++ b/solution.py
@@ -227,14 +227,13 @@
     return [(1, near, 8), (3, turned, 9), *levels], (near_y, far_y, far_both)
 
 
-def shared_pieces(own, symmetric, near_y, far_y, far_both, ready):
+def shared_pieces(own, symmetric, exchanged, near_y, far_y, far_both, later, last):
     pieces = [(0, own, 0, own)]
-    for mask, shard, other_mask in symmetric:
-        given = flipped(after(shard, ready), "dp", 1)
+    for (mask, shard, other_mask), given in zip(symmetric, exchanged):
         pieces += [(mask, shard, other_mask, shard), (other_mask, given, mask, given)]
-    pieces.append((2, near_y, 2, flipped(after(near_y, ready), "dp", 1)))
-    pieces.append((10, flipped(after(far_y, ready), "dp", 1), 10, far_y))
-    pieces.append((11, flipped(after(far_both, ready), "dp", 1), 11, far_both))
+    pieces.append((2, near_y, 2, flipped(after(near_y, later), "dp", 1)))
+    pieces.append((10, flipped(after(far_y, later), "dp", 1), 10, far_y))
+    pieces.append((11, flipped(after(far_both, last), "dp", 1), 11, far_both))
     return pieces
 
 
@@ -298,14 +297,18 @@
 
     symmetric, single = weight_pieces(own, own_later, groups, hold, asked)
     fetched = lax.all_to_all(held[0], "mp", split_axis=0, concat_axis=0, tiled=True)
+    exchanged = [flipped(after(shard, packed), "dp", 1) for _, shard, _ in symmetric]
     shifted, normed, positive_row = kernel_call(
         select_body,
         (whole((chains, features), F32), whole((chains, features), BF16), whole((1, chains), jnp.int32)),
         packed,
-        fetched,
-    )
-
-    pieces = shared_pieces(own, symmetric, *single, normed)
+        after(fetched, exchanged[0]),
+    )
+
+    neighbour_normed = flipped(normed, "mp", 4)
+    pieces = shared_pieces(own, symmetric, exchanged, *single, normed, neighbour_normed)
+    early = (own, symmetric[0][1], exchanged[0])
+
     def hidden(rows, some, held_as, *so_far):
         shards = []
         for piece in some:
@@ -321,7 +324,7 @@
             rows,
             asked,
             *so_far,
-            *shards,
+            *(pltpu.with_memory_space_constraint(s, pltpu.HBM) if any(s is e for e in early) else s for s in shards),
             in_place=range(first, first + len(shards)),
             scratch=(
                 pltpu.VMEM((len(plan) * units, features), BF16),
@@ -331,7 +334,6 @@
             vmem=LARGE_VMEM,
         )
 
-    neighbour_normed = flipped(normed, "mp", 4)
     neighbour = hidden(
         neighbour_normed, pieces[-1:], BF16, hidden(neighbour_normed, pieces[:-1], F32)
     )

time: 83.9 us -> 82 us (0.977)
  local copies, waits for them, and re-layouts: 5.67 us -> 2.39 us
  waiting for transfers between devices: 25.5 us -> 27 us
    unnamed x27 -> x23, local copies, waits for them, and re-layouts: 5.64 us -> 2.37 us
    ppermute x9, waiting for transfers between devices: 5.48 us -> 8.03 us  [flipped(): lax.ppermute(block, axis, [(i, i ^ mask) for i in range(lax.axis_size(axi...]
  transfers between devices with their start and end apart: 19 -> 19, of which waited for: 9 -> 9; matrix products, arithmetic and copies ran while one was open for 1% -> 1% of each run, Pallas kernels for 12% -> 11%
where the time goes in v8:
time: 82 us; the launch traced here: 81.6 us
  starting transfers between devices  27.3 us (33%)
  waiting for transfers between devices  27 us (33%)
  blocking collectives  12.2 us (15%)
  Pallas kernels  10.4 us (13%)
  local copies, waits for them, and re-layouts  2.39 us (3%)
  other arithmetic  1.43 us (2%)
  between operations  0.87 us (1%)
    ppermute x9, starting transfers between devices, moved(): return lax.ppermute(block, ('dp', 'mp'), route)  15.8 us
    ppermute x9, waiting for transfers between devices, moved(): return lax.ppermute(block, ('dp', 'mp'), route)  14 us
    all_to_all x1, blocking collectives, local(): lax.all_to_all(message, 'mp', split_axis=0, concat_axis=0, tiled=True)  12.2 us
    pallas_call x9, Pallas kernels, kernel_call(): pl.pallas_call(body, out_shape=out_shape, in_specs=[pl.BlockSpec(memory_s...  10.4 us
    ppermute x9, waiting for transfers between devices, flipped(): lax.ppermute(block, axis, [(i, i ^ mask) for i in range(lax.axis_size(axi...  8.03 us
    ppermute x9, starting transfers between devices, flipped(): lax.ppermute(block, axis, [(i, i ^ mask) for i in range(lax.axis_size(axi...  7.81 us
    all_to_all x1, waiting for transfers between devices, local(): lax.all_to_all(held[0], 'mp', split_axis=0, concat_axis=0, tiled=True)  4.92 us
    all_to_all x1, starting transfers between devices, local(): lax.all_to_all(held[0], 'mp', split_axis=0, concat_axis=0, tiled=True)  3.7 us
  transfers between devices with their start and end apart: 19, of which 9 were waited for; matrix products, arithmetic and copies ran while one was open for 1% of the time, Pallas kernels for 11%

profile of v8, /device:TPU:0, one launch (start us, length us, event | category | flops | bytes accessed | tf_op | source)
XLA Modules:
  0.0 81.6 jit_solution(7522945697431459846)
XLA Ops:
  0.6 1.0 %constant_dynamic-update-slice_fusion.1 = bf16[384,768]{1,0:T(8,128)(2,1)S(1)} fusion(bf16[192,768]{1,0:T(8,128)(2,1)} %param.16), kind=kLoop, calls=%fused_computation.6 | loop fusion | bytes 589824
  1.7 3.0 %collective-permute-start = (bf16[384,768]{1,0:T(8,128)(2,1)S(1)}, bf16[384,768]{1,0:T(8,128)(2,1)}, u32[]{:S(2)}, u32[]{:S(2)}) collective-permute-start(bf16[384,768]{1,0:T(8,128)(2,1)S(1)} %constant_dynamic-update-slice_fusion.refs_0_), channel_id=1, source_target_pairs={{1,0},{0,1},{3,2},{2,3},{5,4},{4,5},{7,6},{6,7},{9,8},{8,9},{11,10... | collective-permute-start | bytes 1769480 | tf_op jit(solution)/shard_map/ppermute | solution.py:30
  4.7 0.6 copy-done.5
  5.8 3.4 %collective-permute-start.1 = (bf16[384,768]{1,0:T(8,128)(2,1)S(1)}, bf16[384,768]{1,0:T(8,128)(2,1)S(1)}, u32[]{:S(2)}, u32[]{:S(2)}) collective-permute-start(bf16[384,768]{1,0:T(8,128)(2,1)S(1)} %constant_dynamic-update-slice_fusion.refs_0_), channel_id=1, source_target_pairs={{2,0},{3,1},{0,2},{1,3},{6,4},{7,5},{4,6},{5,7},{10,8},{11,9},{8,1... | collective-permute-start | bytes 1769480 | tf_op jit(solution)/shard_map/ppermute | solution.py:30
  9.2 12.2 %all_to_all.17.message_ref = f32[16,1,256]{2,1,0:T(1,128)S(1)} all-to-all(f32[16,1,256]{2,1,0:T(1,128)S(1)} %shard_map.138), channel_id=1, replica_groups=mesh['dp'=2,'mp'=16] {'mp'}, dimensions={0} | all-to-all | bytes 32768 | tf_op jit(solution)/shard_map/all_to_all | solution.py:273
  22.0 1.3 %shard_map.139 = bf16[256,768]{1,0:T(8,128)(2,1)} custom-call(f32[16,1,256]{2,1,0:T(1,128)S(1)} %all_to_all.17.message_ref, bf16[256,768]{1,0:T(8,128)(2,1)S(1)} %copy-done), custom_call_target="tpu_custom_call" | custom-call | tf_op jit(solution)/shard_map/pallas_call | solution.py:38
  23.3 3.7 %all-to-all-start.1 = ((bf16[16,16,768]{2,1,0:T(8,128)(2,1)}), bf16[16,16,768]{2,1,0:T(8,128)(2,1)S(1)}, u32[]{:S(2)}, u32[]{:S(2)}) async-start(bf16[16,16,768]{2,1,0:T(8,128)(2,1)} %bitcast.3), calls=%async_computation.1 | async-start | bytes 786432 | tf_op jit(solution)/shard_map/all_to_all | solution.py:299
  27.8 1.6 %collective-permute-start.2 = (bf16[384,768]{1,0:T(8,128)(2,1)}, bf16[384,768]{1,0:T(8,128)(2,1)}, u32[]{:S(2)}, u32[]{:S(2)}) collective-permute-start(bf16[384,768]{1,0:T(8,128)(2,1)} %collective-permute-done.refs_1_), channel_id=1, source_target_pairs={{0,16},{16,0},{1,17},{17,1},{2,18},{18,2},{3,19},{19,3},{4,20},{20... | collective-permute-start | bytes 1769480 | tf_op jit(solution)/shard_map/ppermute | solution.py:19
  29.4 0.7 collective-permute-start.7
  30.1 3.5 %collective-permute-done.4.refs_3_ = bf16[384,768]{1,0:T(8,128)(2,1)S(1)} collective-permute-done((bf16[384,768]{1,0:T(8,128)(2,1)}, bf16[384,768]{1,0:T(8,128)(2,1)S(1)}, u32[]{:S(2)}, u32[]{:S(2)}) %collective-permute-start.4) | collective-permute-done | bytes 589856 | tf_op jit(solution)/shard_map/ppermute | solution.py:30
  33.6 0.7 collective-permute-start.9
  34.3 4.9 %all-to-all-done.1 = bf16[16,16,768]{2,1,0:T(8,128)(2,1)S(1)} async-done(((bf16[16,16,768]{2,1,0:T(8,128)(2,1)}), bf16[16,16,768]{2,1,0:T(8,128)(2,1)S(1)}, u32[]{:S(2)}, u32[]{:S(2)}) %all-to-all-start.1) | async-done | bytes 393248 | tf_op jit(solution)/shard_map/all_to_all | solution.py:299
  39.7 2.1 %collective-permute-start.3 = (bf16[128,768]{1,0:T(8,128)(2,1)S(1)}, bf16[128,768]{1,0:T(8,128)(2,1)S(1)}, u32[]{:S(2)}, u32[]{:S(2)}) collective-permute-start(bf16[128,768]{1,0:T(8,128)(2,1)S(1)} %get-tuple-element.43.normed_ref), channel_id=1, source_target_pairs={{0,4},{1,5},{2,6},{3,7},{4,0},{5,1},{6,2},{7,3},{8,12},{9,13},{10,... | collective-permute-start | bytes 589832 | tf_op jit(solution)/shard_map/ppermute | solution.py:19
  42.7 4.5 %collective-permute-done.3.normed_ref = bf16[128,768]{1,0:T(8,128)(2,1)S(1)} collective-permute-done((bf16[128,768]{1,0:T(8,128)(2,1)S(1)}, bf16[128,768]{1,0:T(8,128)(2,1)S(1)}, u32[]{:S(2)}, u32[]{:S(2)}) %collective-permute-start.3) | collective-permute-done | bytes 196640 | tf_op jit(solution)/shard_map/ppermute | solution.py:19
  47.2 1.2 %collective-permute-start.10 = (bf16[384,768]{1,0:T(8,128)(2,1)S(1)}, bf16[384,768]{1,0:T(8,128)(2,1)S(1)}, u32[]{:S(2)}, u32[]{:S(2)}) collective-permute-start(bf16[384,768]{1,0:T(8,128)(2,1)S(1)} %collective-permute-done.9.refs_2_.refs_10_), channel_id=1, source_target_pairs={{0,16},{16,0},{1,17},{17,1},{2,18},{18,2},{3,19},{19,3},{4,20},{20... | collective-permute-start | bytes 1769480 | tf_op jit(solution)/shard_map/ppermute | solution.py:19
  48.4 2.8 %shard_map.142.refs_0_ = f32[128,768]{1,0:T(8,128)S(1)} custom-call(bf16[128,768]{1,0:T(8,128)(2,1)S(1)} %collective-permute-done.3.normed_ref, f32[16,1,256]{2,1,0:T(1,128)S(1)} %all_to_all.17.message_ref, bf16[384,768]{1,0:T(8,128)(2,1)} %copy-done.9, bf16[384,768]{1,0:T(8,128)(2,1)} %collective-permute-done.refs_1_, ...), custom_call_target="tpu_custom_call" | custom-call | tf_op jit(solution)/shard_map/pallas_call | solution.py:38
  51.2 0.7 shard_map.143
  51.9 2.0 %collective-permute-start.11 = (bf16[128,768]{1,0:T(8,128)(2,1)S(1)}, bf16[128,768]{1,0:T(8,128)(2,1)S(1)}, u32[]{:S(2)}, u32[]{:S(2)}) collective-permute-start(bf16[128,768]{1,0:T(8,128)(2,1)S(1)} %shard_map.143), channel_id=1, source_target_pairs={{0,4},{1,5},{2,6},{3,7},{4,0},{5,1},{6,2},{7,3},{8,12},{9,13},{10,... | collective-permute-start | bytes 589832 | tf_op jit(solution)/shard_map/ppermute | solution.py:19
  53.9 2.8 %shard_map.144.total_ref = f32[128,768]{1,0:T(8,128)S(1)} custom-call(bf16[128,768]{1,0:T(8,128)(2,1)S(1)} %get-tuple-element.43.normed_ref, f32[16,1,256]{2,1,0:T(1,128)S(1)} %all_to_all.17.message_ref, bf16[384,768]{1,0:T(8,128)(2,1)} %copy-done.9, bf16[384,768]{1,0:T(8,128)(2,1)} %collective-permute-done.refs_1_, ...), custom_call_target="tpu_custom_call" | custom-call | tf_op jit(solution)/shard_map/pallas_call | solution.py:38
  56.7 2.2 %collective-permute-done.11.other_ref = bf16[128,768]{1,0:T(8,128)(2,1)S(1)} collective-permute-done((bf16[128,768]{1,0:T(8,128)(2,1)S(1)}, bf16[128,768]{1,0:T(8,128)(2,1)S(1)}, u32[]{:S(2)}, u32[]{:S(2)}) %collective-permute-start.11) | collective-permute-done | bytes 196640 | tf_op jit(solution)/shard_map/ppermute | solution.py:19
  59.0 0.8 shard_map.145
  59.8 1.3 %collective-permute-done.13 = bf16[64,768]{1,0:T(8,128)(2,1)S(1)} collective-permute-done((bf16[64,768]{1,0:T(8,128)(2,1)S(1)}, bf16[64,768]{1,0:T(8,128)(2,1)S(1)}, u32[]{:S(2)}, u32[]{:S(2)}) %collective-permute-start.13) | collective-permute-done | bytes 98336 | tf_op jit(solution)/shard_map/ppermute | solution.py:19
  61.1 1.6 %collective-permute-start.14 = (bf16[64,768]{1,0:T(8,128)(2,1)S(1)}, bf16[64,768]{1,0:T(8,128)(2,1)S(1)}, u32[]{:S(2)}, u32[]{:S(2)}) collective-permute-start(bf16[64,768]{1,0:T(8,128)(2,1)S(1)} %add_convert_fusion.3), channel_id=1, source_target_pairs={{1,0},{0,1},{3,2},{2,3},{5,4},{4,5},{7,6},{6,7},{9,8},{8,9},{11,10... | collective-permute-start | bytes 294920 | tf_op jit(solution)/shard_map/ppermute | solution.py:30
  62.7 3.1 %collective-permute-done.14 = bf16[64,768]{1,0:T(8,128)(2,1)S(1)} collective-permute-done((bf16[64,768]{1,0:T(8,128)(2,1)S(1)}, bf16[64,768]{1,0:T(8,128)(2,1)S(1)}, u32[]{:S(2)}, u32[]{:S(2)}) %collective-permute-start.14) | collective-permute-done | bytes 98336 | tf_op jit(solution)/shard_map/ppermute | solution.py:30
  65.9 1.4 %collective-permute-start.15 = (bf16[64,768]{1,0:T(8,128)(2,1)S(1)}, bf16[64,768]{1,0:T(8,128)(2,1)S(1)}, u32[]{:S(2)}, u32[]{:S(2)}) collective-permute-start(bf16[64,768]{1,0:T(8,128)(2,1)S(1)} %add_convert_fusion.2), channel_id=1, source_target_pairs={{2,0},{3,1},{0,2},{1,3},{6,4},{7,5},{4,6},{5,7},{10,8},{11,9},{8,1... | collective-permute-start | bytes 294920 | tf_op jit(solution)/shard_map/ppermute | solution.py:30
  67.2 3.3 %collective-permute-done.15 = bf16[64,768]{1,0:T(8,128)(2,1)S(1)} collective-permute-done((bf16[64,768]{1,0:T(8,128)(2,1)S(1)}, bf16[64,768]{1,0:T(8,128)(2,1)S(1)}, u32[]{:S(2)}, u32[]{:S(2)}) %collective-permute-start.15) | collective-permute-done | bytes 98336 | tf_op jit(solution)/shard_map/ppermute | solution.py:30
  70.6 1.8 %collective-permute-start.16 = (bf16[64,768]{1,0:T(8,128)(2,1)S(1)}, bf16[64,768]{1,0:T(8,128)(2,1)S(1)}, u32[]{:S(2)}, u32[]{:S(2)}) collective-permute-start(bf16[64,768]{1,0:T(8,128)(2,1)S(1)} %add_convert_fusion.1), channel_id=1, source_target_pairs={{4,0},{5,1},{6,2},{7,3},{0,4},{1,5},{2,6},{3,7},{12,8},{13,9},{14,... | collective-permute-start | bytes 294920 | tf_op jit(solution)/shard_map/ppermute | solution.py:30
  72.4 2.9 %collective-permute-done.16 = bf16[64,768]{1,0:T(8,128)(2,1)S(1)} collective-permute-done((bf16[64,768]{1,0:T(8,128)(2,1)S(1)}, bf16[64,768]{1,0:T(8,128)(2,1)S(1)}, u32[]{:S(2)}, u32[]{:S(2)}) %collective-permute-start.16) | collective-permute-done | bytes 98336 | tf_op jit(solution)/shard_map/ppermute | solution.py:30
  75.3 2.7 %collective-permute-start.17 = (bf16[64,768]{1,0:T(8,128)(2,1)S(1)}, bf16[64,768]{1,0:T(8,128)(2,1)S(1)}, u32[]{:S(2)}, u32[]{:S(2)}) collective-permute-start(bf16[64,768]{1,0:T(8,128)(2,1)S(1)} %add_convert_fusion), channel_id=1, source_target_pairs={{8,0},{9,1},{10,2},{11,3},{12,4},{13,5},{14,6},{15,7},{0,8},{1,9},... | collective-permute-start | bytes 294920 | tf_op jit(solution)/shard_map/ppermute | solution.py:30
  78.0 1.0 %shard_map.146 = (f32[128,768]{1,0:T(8,128)}, bf16[128,768]{1,0:T(8,128)(2,1)}, f32[128,1]{1,0:T(8,128)S(1)}) custom-call(bf16[128,128]{1,0:T(8,128)(2,1)S(1)} %get-tuple-element.46.weights_ref, bf16[128,768]{1,0:T(8,128)(2,1)S(1)} %get-tuple-element.47.updated_ref, f32[128,1]{1,0:T(8,128)S(1)} %get-tuple-element.48.loss_ref, bf16[64,768]{1,0:T(8,128)(2,1)S(1)} %copy-done.1, ...), custom_call_target="tpu_custom_call" | custom-call | tf_op jit(solution)/shard_map/pallas_call | solution.py:38
  79.7 1.2 %collective-permute-done.17 = bf16[64,768]{1,0:T(8,128)(2,1)S(1)} collective-permute-done((bf16[64,768]{1,0:T(8,128)(2,1)S(1)}, bf16[64,768]{1,0:T(8,128)(2,1)S(1)}, u32[]{:S(2)}, u32[]{:S(2)}) %collective-permute-start.17) | collective-permute-done | bytes 98336 | tf_op jit(solution)/shard_map/ppermute | solution.py:30
  80.9 0.7 add_multiply_fusion
  (46 shorter events, 4.0 us)
Async XLA Ops:
  0.6 1.1 %copy-start.10 = (bf16[192,768]{1,0:T(8,128)(2,1)S(1)}, bf16[192,768]{1,0:T(8,128)(2,1)}, u32[]{:S(2)}) copy-start(bf16[192,768]{1,0:T(8,128)(2,1)} %param.18) | copy-start | bytes 884740
  1.7 20.3 %copy-start = (bf16[256,768]{1,0:T(8,128)(2,1)S(1)}, bf16[256,768]{1,0:T(8,128)(2,1)}, u32[]{:S(2)}) copy-start(bf16[256,768]{1,0:T(8,128)(2,1)} %table_ref.1) | copy-start | bytes 1179652
  1.7 21.6 %copy-start.9 = (bf16[384,768]{1,0:T(8,128)(2,1)}, bf16[384,768]{1,0:T(8,128)(2,1)S(1)}, u32[]{:S(2)}) copy-start(bf16[384,768]{1,0:T(8,128)(2,1)S(1)} %constant_dynamic-update-slice_fusion.refs_0_) | copy-start | bytes 1769476
  1.7 19.7 %collective-permute-start = (bf16[384,768]{1,0:T(8,128)(2,1)S(1)}, bf16[384,768]{1,0:T(8,128)(2,1)}, u32[]{:S(2)}, u32[]{:S(2)}) collective-permute-start(bf16[384,768]{1,0:T(8,128)(2,1)S(1)} %constant_dynamic-update-slice_fusion.refs_0_), channel_id=1, source_target_pairs={{1,0},{0,1},{3,2},{2,3},{5,4},{4,5},{7,6},{6,7},{9,8},{8,9},{11,10... | collective-permute-start | bytes 1769480 | tf_op jit(solution)/shard_map/ppermute | solution.py:30
  4.7 0.7 copy-start.5
  4.7 0.7 copy-start.7
  4.7 0.7 copy-start.8
  5.8 17.5 %collective-permute-start.1 = (bf16[384,768]{1,0:T(8,128)(2,1)S(1)}, bf16[384,768]{1,0:T(8,128)(2,1)S(1)}, u32[]{:S(2)}, u32[]{:S(2)}) collective-permute-start(bf16[384,768]{1,0:T(8,128)(2,1)S(1)} %constant_dynamic-update-slice_fusion.refs_0_), channel_id=1, source_target_pairs={{2,0},{3,1},{0,2},{1,3},{6,4},{7,5},{4,6},{5,7},{10,8},{11,9},{8,1... | collective-permute-start | bytes 1769480 | tf_op jit(solution)/shard_map/ppermute | solution.py:30
  21.4 12.2 %collective-permute-start.4 = (bf16[384,768]{1,0:T(8,128)(2,1)}, bf16[384,768]{1,0:T(8,128)(2,1)S(1)}, u32[]{:S(2)}, u32[]{:S(2)}) collective-permute-start(bf16[384,768]{1,0:T(8,128)(2,1)} %collective-permute-done.refs_1_), channel_id=1, source_target_pairs={{2,0},{3,1},{0,2},{1,3},{6,4},{7,5},{4,6},{5,7},{10,8},{11,9},{8,1... | collective-permute-start | bytes 1769480 | tf_op jit(solution)/shard_map/ppermute | solution.py:30
  23.3 3.7 %copy-start.2 = (bf16[128,768]{1,0:T(8,128)(2,1)S(1)}, bf16[128,768]{1,0:T(8,128)(2,1)}, u32[]{:S(2)}) copy-start(bf16[128,768]{1,0:T(8,128)(2,1)} %queries_ref.1) | copy-start | bytes 589828
  23.3 3.7 %copy-start.3 = (bf16[768]{0:T(1024)(128)(2,1)S(1)}, bf16[768]{0:T(1024)(128)(2,1)}, u32[]{:S(2)}) copy-start(bf16[768]{0:T(1024)(128)(2,1)} %gain_ref.1) | copy-start | bytes 4612
  23.3 3.8 %copy-start.4 = (bf16[768]{0:T(1024)(128)(2,1)S(1)}, bf16[768]{0:T(1024)(128)(2,1)}, u32[]{:S(2)}) copy-start(bf16[768]{0:T(1024)(128)(2,1)} %bias_ref.3) | copy-start | bytes 4612
  23.3 15.9 %all-to-all-start.1 = ((bf16[16,16,768]{2,1,0:T(8,128)(2,1)}), bf16[16,16,768]{2,1,0:T(8,128)(2,1)S(1)}, u32[]{:S(2)}, u32[]{:S(2)}) async-start(bf16[16,16,768]{2,1,0:T(8,128)(2,1)} %bitcast.3), calls=%async_computation.1 | async-start | bytes 786432 | tf_op jit(solution)/shard_map/all_to_all | solution.py:299
  27.0 0.7 copy-start.6
  27.8 6.5 %collective-permute-start.2 = (bf16[384,768]{1,0:T(8,128)(2,1)}, bf16[384,768]{1,0:T(8,128)(2,1)}, u32[]{:S(2)}, u32[]{:S(2)}) collective-permute-start(bf16[384,768]{1,0:T(8,128)(2,1)} %collective-permute-done.refs_1_), channel_id=1, source_target_pairs={{0,16},{16,0},{1,17},{17,1},{2,18},{18,2},{3,19},{19,3},{4,20},{20... | collective-permute-start | bytes 1769480 | tf_op jit(solution)/shard_map/ppermute | solution.py:19
  29.4 12.9 %collective-permute-start.7 = (bf16[384,768]{1,0:T(8,128)(2,1)}, bf16[384,768]{1,0:T(8,128)(2,1)S(1)}, u32[]{:S(2)}, u32[]{:S(2)}) collective-permute-start(bf16[384,768]{1,0:T(8,128)(2,1)} %collective-permute-done.refs_1_), channel_id=1, source_target_pairs={{18,16},{19,17},{16,18},{17,19},{22,20},{23,21},{20,22},{21,23},{2... | collective-permute-start | bytes 1769480 | tf_op jit(solution)/shard_map/ppermute | solution.py:30
  33.6 13.7 %collective-permute-start.9 = (bf16[384,768]{1,0:T(8,128)(2,1)S(1)}, bf16[384,768]{1,0:T(8,128)(2,1)S(1)}, u32[]{:S(2)}, u32[]{:S(2)}) collective-permute-start(bf16[384,768]{1,0:T(8,128)(2,1)S(1)} %collective-permute-done.4.refs_3_), channel_id=1, source_target_pairs={{18,16},{19,17},{16,18},{17,19},{22,20},{23,21},{20,22},{21,23},{2... | collective-permute-start | bytes 1769480 | tf_op jit(solution)/shard_map/ppermute | solution.py:30
  39.7 7.6 %collective-permute-start.3 = (bf16[128,768]{1,0:T(8,128)(2,1)S(1)}, bf16[128,768]{1,0:T(8,128)(2,1)S(1)}, u32[]{:S(2)}, u32[]{:S(2)}) collective-permute-start(bf16[128,768]{1,0:T(8,128)(2,1)S(1)} %get-tuple-element.43.normed_ref), channel_id=1, source_target_pairs={{0,4},{1,5},{2,6},{3,7},{4,0},{5,1},{6,2},{7,3},{8,12},{9,13},{10,... | collective-permute-start | bytes 589832 | tf_op jit(solution)/shard_map/ppermute | solution.py:19
  41.8 6.6 %collective-permute-start.5 = (bf16[384,768]{1,0:T(8,128)(2,1)S(1)}, bf16[384,768]{1,0:T(8,128)(2,1)S(1)}, u32[]{:S(2)}, u32[]{:S(2)}) collective-permute-start(bf16[384,768]{1,0:T(8,128)(2,1)S(1)} %collective-permute-done.4.refs_3_), channel_id=1, source_target_pairs={{0,16},{16,0},{1,17},{17,1},{2,18},{18,2},{3,19},{19,3},{4,20},{20... | collective-permute-start | bytes 1769480 | tf_op jit(solution)/shard_map/ppermute | solution.py:19
  42.2 6.2 %collective-permute-start.6 = (bf16[384,768]{1,0:T(8,128)(2,1)S(1)}, bf16[384,768]{1,0:T(8,128)(2,1)S(1)}, u32[]{:S(2)}, u32[]{:S(2)}) collective-permute-start(bf16[384,768]{1,0:T(8,128)(2,1)S(1)} %collective-permute-done.1.refs_5_), channel_id=1, source_target_pairs={{0,16},{16,0},{1,17},{17,1},{2,18},{18,2},{3,19},{19,3},{4,20},{20... | collective-permute-start | bytes 1769480 | tf_op jit(solution)/shard_map/ppermute | solution.py:19
  42.3 6.1 %collective-permute-start.8 = (bf16[384,768]{1,0:T(8,128)(2,1)S(1)}, bf16[384,768]{1,0:T(8,128)(2,1)S(1)}, u32[]{:S(2)}, u32[]{:S(2)}) collective-permute-start(bf16[384,768]{1,0:T(8,128)(2,1)S(1)} %collective-permute-done.7.refs_8_), channel_id=1, source_target_pairs={{0,16},{16,0},{1,17},{17,1},{2,18},{18,2},{3,19},{19,3},{4,20},{20... | collective-permute-start | bytes 1769480 | tf_op jit(solution)/shard_map/ppermute | solution.py:19
  47.2 4.0 %collective-permute-start.10 = (bf16[384,768]{1,0:T(8,128)(2,1)S(1)}, bf16[384,768]{1,0:T(8,128)(2,1)S(1)}, u32[]{:S(2)}, u32[]{:S(2)}) collective-permute-start(bf16[384,768]{1,0:T(8,128)(2,1)S(1)} %collective-permute-done.9.refs_2_.refs_10_), channel_id=1, source_target_pairs={{0,16},{16,0},{1,17},{17,1},{2,18},{18,2},{3,19},{19,3},{4,20},{20... | collective-permute-start | bytes 1769480 | tf_op jit(solution)/shard_map/ppermute | solution.py:19
  51.2 2.7 %copy-start.1 = (bf16[64,768]{1,0:T(8,128)(2,1)S(1)}, bf16[64,768]{1,0:T(8,128)(2,1)}, u32[]{:S(2)}) copy-start(bf16[64,768]{1,0:T(8,128)(2,1)} %refs_0_.3) | copy-start | bytes 294916
  51.9 7.0 %collective-permute-start.11 = (bf16[128,768]{1,0:T(8,128)(2,1)S(1)}, bf16[128,768]{1,0:T(8,128)(2,1)S(1)}, u32[]{:S(2)}, u32[]{:S(2)}) collective-permute-start(bf16[128,768]{1,0:T(8,128)(2,1)S(1)} %shard_map.143), channel_id=1, source_target_pairs={{0,4},{1,5},{2,6},{3,7},{4,0},{5,1},{6,2},{7,3},{8,12},{9,13},{10,... | collective-permute-start | bytes 589832 | tf_op jit(solution)/shard_map/ppermute | solution.py:19
  53.9 2.8 %collective-permute-start.12 = (bf16[64,768]{1,0:T(8,128)(2,1)S(1)}, bf16[64,768]{1,0:T(8,128)(2,1)S(1)}, u32[]{:S(2)}, u32[]{:S(2)}) collective-permute-start(bf16[64,768]{1,0:T(8,128)(2,1)S(1)} %copy-done.1), channel_id=1, source_target_pairs={{0,16},{16,0},{1,17},{17,1},{2,18},{18,2},{3,19},{19,3},{4,20},{20... | collective-permute-start | bytes 294920 | tf_op jit(solution)/shard_map/ppermute | solution.py:19
  59.7 1.4 %collective-permute-start.13 = (bf16[64,768]{1,0:T(8,128)(2,1)S(1)}, bf16[64,768]{1,0:T(8,128)(2,1)S(1)}, u32[]{:S(2)}, u32[]{:S(2)}) collective-permute-start(bf16[64,768]{1,0:T(8,128)(2,1)S(1)} %get-tuple-element.53), channel_id=1, source_target_pairs={{0,16},{16,0},{1,17},{17,1},{2,18},{18,2},{3,19},{19,3},{4,20},{20... | collective-permute-start | bytes 294920 | tf_op jit(solution)/shard_map/ppermute | solution.py:19
  61.1 4.7 %collective-permute-start.14 = (bf16[64,768]{1,0:T(8,128)(2,1)S(1)}, bf16[64,768]{1,0:T(8,128)(2,1)S(1)}, u32[]{:S(2)}, u32[]{:S(2)}) collective-permute-start(bf16[64,768]{1,0:T(8,128)(2,1)S(1)} %add_convert_fusion.3), channel_id=1, source_target_pairs={{1,0},{0,1},{3,2},{2,3},{5,4},{4,5},{7,6},{6,7},{9,8},{8,9},{11,10... | collective-permute-start | bytes 294920 | tf_op jit(solution)/shard_map/ppermute | solution.py:30
  65.9 4.7 %collective-permute-start.15 = (bf16[64,768]{1,0:T(8,128)(2,1)S(1)}, bf16[64,768]{1,0:T(8,128)(2,1)S(1)}, u32[]{:S(2)}, u32[]{:S(2)}) collective-permute-start(bf16[64,768]{1,0:T(8,128)(2,1)S(1)} %add_convert_fusion.2), channel_id=1, source_target_pairs={{2,0},{3,1},{0,2},{1,3},{6,4},{7,5},{4,6},{5,7},{10,8},{11,9},{8,1... | collective-permute-start | bytes 294920 | tf_op jit(solution)/shard_map/ppermute | solution.py:30
  70.6 4.7 %collective-permute-start.16 = (bf16[64,768]{1,0:T(8,128)(2,1)S(1)}, bf16[64,768]{1,0:T(8,128)(2,1)S(1)}, u32[]{:S(2)}, u32[]{:S(2)}) collective-permute-start(bf16[64,768]{1,0:T(8,128)(2,1)S(1)} %add_convert_fusion.1), channel_id=1, source_target_pairs={{4,0},{5,1},{6,2},{7,3},{0,4},{1,5},{2,6},{3,7},{12,8},{13,9},{14,... | collective-permute-start | bytes 294920 | tf_op jit(solution)/shard_map/ppermute | solution.py:30
  75.3 5.6 %collective-permute-start.17 = (bf16[64,768]{1,0:T(8,128)(2,1)S(1)}, bf16[64,768]{1,0:T(8,128)(2,1)S(1)}, u32[]{:S(2)}, u32[]{:S(2)}) collective-permute-start(bf16[64,768]{1,0:T(8,128)(2,1)S(1)} %add_convert_fusion), channel_id=1, source_target_pairs={{8,0},{9,1},{10,2},{11,3},{12,4},{13,5},{14,6},{15,7},{0,8},{1,9},... | collective-permute-start | bytes 294920 | tf_op jit(solution)/shard_map/ppermute | solution.py:30

commit v9 on v8

--- a/solution.py
+++ b/solution.py
@@ -212,7 +212,7 @@
 
 def weight_pieces(own, own_later, groups, hold, asked):
     near = moved(own, (0, 0, 1), (1, 1, 8))
-    near_y = moved(own_later, (0, 0, 2))
+    near_y = moved(own_later, (0, 0, 2), (1, 1, 0))
     first = after(near, asked)
     near, near_y = hold(near, near_y)
     turned = moved(first, (0, 0, 2), (1, 1, 1))

time: 82 us -> 82 us (level)
  no operation moved by 1% of the time
where the time goes in v9:
time: 82 us; the launch traced here: 81.6 us
  starting transfers between devices  27.3 us (33%)
  waiting for transfers between devices  27 us (33%)
  blocking collectives  12.2 us (15%)
  Pallas kernels  10.4 us (13%)
  local copies, waits for them, and re-layouts  2.39 us (3%)
  other arithmetic  1.43 us (2%)
  between operations  0.87 us (1%)
    ppermute x9, starting transfers between devices, moved(): return lax.ppermute(block, ('dp', 'mp'), route)  15.8 us
    ppermute x9, waiting for transfers between devices, moved(): return lax.ppermute(block, ('dp', 'mp'), route)  14 us
    all_to_all x1, blocking collectives, local(): lax.all_to_all(message, 'mp', split_axis=0, concat_axis=0, tiled=True)  12.2 us
    pallas_call x9, Pallas kernels, kernel_call(): pl.pallas_call(body, out_shape=out_shape, in_specs=[pl.BlockSpec(memory_s...  10.4 us
    ppermute x9, waiting for transfers between devices, flipped(): lax.ppermute(block, axis, [(i, i ^ mask) for i in range(lax.axis_size(axi...  8.03 us
    ppermute x9, starting transfers between devices, flipped(): lax.ppermute(block, axis, [(i, i ^ mask) for i in range(lax.axis_size(axi...  7.81 us
    all_to_all x1, waiting for transfers between devices, local(): lax.all_to_all(held[0], 'mp', split_axis=0, concat_axis=0, tiled=True)  4.92 us
    all_to_all x1, starting transfers between devices, local(): lax.all_to_all(held[0], 'mp', split_axis=0, concat_axis=0, tiled=True)  3.7 us
  transfers between devices with their start and end apart: 19, of which 9 were waited for; matrix products, arithmetic and copies ran while one was open for 1% of the time, Pallas kernels for 11%

profile of v9, /device:TPU:0, one launch (start us, length us, event | category | flops | bytes accessed | tf_op | source)
XLA Modules:
  0.0 81.6 jit_solution(3696809325600043523)
XLA Ops:
  0.6 1.0 %constant_dynamic-update-slice_fusion.1 = bf16[384,768]{1,0:T(8,128)(2,1)S(1)} fusion(bf16[192,768]{1,0:T(8,128)(2,1)} %param.16), kind=kLoop, calls=%fused_computation.6 | loop fusion | bytes 589824
  1.7 3.0 %collective-permute-start = (bf16[384,768]{1,0:T(8,128)(2,1)S(1)}, bf16[384,768]{1,0:T(8,128)(2,1)}, u32[]{:S(2)}, u32[]{:S(2)}) collective-permute-start(bf16[384,768]{1,0:T(8,128)(2,1)S(1)} %constant_dynamic-update-slice_fusion.refs_0_), channel_id=1, source_target_pairs={{1,0},{0,1},{3,2},{2,3},{5,4},{4,5},{7,6},{6,7},{9,8},{8,9},{11,10... | collective-permute-start | bytes 1769480 | tf_op jit(solution)/shard_map/ppermute | solution.py:30
  4.7 0.6 copy-done.5
  5.8 3.4 %collective-permute-start.1 = (bf16[384,768]{1,0:T(8,128)(2,1)S(1)}, bf16[384,768]{1,0:T(8,128)(2,1)S(1)}, u32[]{:S(2)}, u32[]{:S(2)}) collective-permute-start(bf16[384,768]{1,0:T(8,128)(2,1)S(1)} %constant_dynamic-update-slice_fusion.refs_0_), channel_id=1, source_target_pairs={{2,0},{3,1},{0,2},{1,3},{6,4},{7,5},{4,6},{5,7},{10,8},{11,9},{8,1... | collective-permute-start | bytes 1769480 | tf_op jit(solution)/shard_map/ppermute | solution.py:30
  9.2 12.2 %all_to_all.17.message_ref = f32[16,1,256]{2,1,0:T(1,128)S(1)} all-to-all(f32[16,1,256]{2,1,0:T(1,128)S(1)} %shard_map.138), channel_id=1, replica_groups=mesh['dp'=2,'mp'=16] {'mp'}, dimensions={0} | all-to-all | bytes 32768 | tf_op jit(solution)/shard_map/all_to_all | solution.py:273
  22.0 1.3 %shard_map.139 = bf16[256,768]{1,0:T(8,128)(2,1)} custom-call(f32[16,1,256]{2,1,0:T(1,128)S(1)} %all_to_all.17.message_ref, bf16[256,768]{1,0:T(8,128)(2,1)S(1)} %copy-done), custom_call_target="tpu_custom_call" | custom-call | tf_op jit(solution)/shard_map/pallas_call | solution.py:38
  23.3 3.7 %all-to-all-start.1 = ((bf16[16,16,768]{2,1,0:T(8,128)(2,1)}), bf16[16,16,768]{2,1,0:T(8,128)(2,1)S(1)}, u32[]{:S(2)}, u32[]{:S(2)}) async-start(bf16[16,16,768]{2,1,0:T(8,128)(2,1)} %bitcast.3), calls=%async_computation.1 | async-start | bytes 786432 | tf_op jit(solution)/shard_map/all_to_all | solution.py:299
  27.8 1.6 %collective-permute-start.2 = (bf16[384,768]{1,0:T(8,128)(2,1)}, bf16[384,768]{1,0:T(8,128)(2,1)}, u32[]{:S(2)}, u32[]{:S(2)}) collective-permute-start(bf16[384,768]{1,0:T(8,128)(2,1)} %collective-permute-done.refs_1_), channel_id=1, source_target_pairs={{0,16},{16,0},{1,17},{17,1},{2,18},{18,2},{3,19},{19,3},{4,20},{20... | collective-permute-start | bytes 1769480 | tf_op jit(solution)/shard_map/ppermute | solution.py:19
  29.4 0.7 collective-permute-start.7
  30.1 3.5 %collective-permute-done.4.refs_3_ = bf16[384,768]{1,0:T(8,128)(2,1)S(1)} collective-permute-done((bf16[384,768]{1,0:T(8,128)(2,1)}, bf16[384,768]{1,0:T(8,128)(2,1)S(1)}, u32[]{:S(2)}, u32[]{:S(2)}) %collective-permute-start.4) | collective-permute-done | bytes 589856 | tf_op jit(solution)/shard_map/ppermute | solution.py:30
  33.6 0.7 collective-permute-start.9
  34.3 4.9 %all-to-all-done.1 = bf16[16,16,768]{2,1,0:T(8,128)(2,1)S(1)} async-done(((bf16[16,16,768]{2,1,0:T(8,128)(2,1)}), bf16[16,16,768]{2,1,0:T(8,128)(2,1)S(1)}, u32[]{:S(2)}, u32[]{:S(2)}) %all-to-all-start.1) | async-done | bytes 393248 | tf_op jit(solution)/shard_map/all_to_all | solution.py:299
  39.7 2.1 %collective-permute-start.3 = (bf16[128,768]{1,0:T(8,128)(2,1)S(1)}, bf16[128,768]{1,0:T(8,128)(2,1)S(1)}, u32[]{:S(2)}, u32[]{:S(2)}) collective-permute-start(bf16[128,768]{1,0:T(8,128)(2,1)S(1)} %get-tuple-element.43.normed_ref), channel_id=1, source_target_pairs={{0,4},{1,5},{2,6},{3,7},{4,0},{5,1},{6,2},{7,3},{8,12},{9,13},{10,... | collective-permute-start | bytes 589832 | tf_op jit(solution)/shard_map/ppermute | solution.py:19
  42.7 4.5 %collective-permute-done.3.normed_ref = bf16[128,768]{1,0:T(8,128)(2,1)S(1)} collective-permute-done((bf16[128,768]{1,0:T(8,128)(2,1)S(1)}, bf16[128,768]{1,0:T(8,128)(2,1)S(1)}, u32[]{:S(2)}, u32[]{:S(2)}) %collective-permute-start.3) | collective-permute-done | bytes 196640 | tf_op jit(solution)/shard_map/ppermute | solution.py:19
  47.2 1.2 %collective-permute-start.10 = (bf16[384,768]{1,0:T(8,128)(2,1)S(1)}, bf16[384,768]{1,0:T(8,128)(2,1)S(1)}, u32[]{:S(2)}, u32[]{:S(2)}) collective-permute-start(bf16[384,768]{1,0:T(8,128)(2,1)S(1)} %collective-permute-done.9.refs_2_.refs_10_), channel_id=1, source_target_pairs={{0,16},{16,0},{1,17},{17,1},{2,18},{18,2},{3,19},{19,3},{4,20},{20... | collective-permute-start | bytes 1769480 | tf_op jit(solution)/shard_map/ppermute | solution.py:19
  48.4 2.8 %shard_map.142.refs_0_ = f32[128,768]{1,0:T(8,128)S(1)} custom-call(bf16[128,768]{1,0:T(8,128)(2,1)S(1)} %collective-permute-done.3.normed_ref, f32[16,1,256]{2,1,0:T(1,128)S(1)} %all_to_all.17.message_ref, bf16[384,768]{1,0:T(8,128)(2,1)} %copy-done.9, bf16[384,768]{1,0:T(8,128)(2,1)} %collective-permute-done.refs_1_, ...), custom_call_target="tpu_custom_call" | custom-call | tf_op jit(solution)/shard_map/pallas_call | solution.py:38
  51.2 0.7 shard_map.143
  51.9 2.0 %collective-permute-start.11 = (bf16[128,768]{1,0:T(8,128)(2,1)S(1)}, bf16[128,768]{1,0:T(8,128)(2,1)S(1)}, u32[]{:S(2)}, u32[]{:S(2)}) collective-permute-start(bf16[128,768]{1,0:T(8,128)(2,1)S(1)} %shard_map.143), channel_id=1, source_target_pairs={{0,4},{1,5},{2,6},{3,7},{4,0},{5,1},{6,2},{7,3},{8,12},{9,13},{10,... | collective-permute-start | bytes 589832 | tf_op jit(solution)/shard_map/ppermute | solution.py:19
  53.9 2.8 %shard_map.144.total_ref = f32[128,768]{1,0:T(8,128)S(1)} custom-call(bf16[128,768]{1,0:T(8,128)(2,1)S(1)} %get-tuple-element.43.normed_ref, f32[16,1,256]{2,1,0:T(1,128)S(1)} %all_to_all.17.message_ref, bf16[384,768]{1,0:T(8,128)(2,1)} %copy-done.9, bf16[384,768]{1,0:T(8,128)(2,1)} %collective-permute-done.refs_1_, ...), custom_call_target="tpu_custom_call" | custom-call | tf_op jit(solution)/shard_map/pallas_call | solution.py:38
  56.7 2.2 %collective-permute-done.11.other_ref = bf16[128,768]{1,0:T(8,128)(2,1)S(1)} collective-permute-done((bf16[128,768]{1,0:T(8,128)(2,1)S(1)}, bf16[128,768]{1,0:T(8,128)(2,1)S(1)}, u32[]{:S(2)}, u32[]{:S(2)}) %collective-permute-start.11) | collective-permute-done | bytes 196640 | tf_op jit(solution)/shard_map/ppermute | solution.py:19
  59.0 0.8 shard_map.145
  59.8 1.3 %collective-permute-done.13 = bf16[64,768]{1,0:T(8,128)(2,1)S(1)} collective-permute-done((bf16[64,768]{1,0:T(8,128)(2,1)S(1)}, bf16[64,768]{1,0:T(8,128)(2,1)S(1)}, u32[]{:S(2)}, u32[]{:S(2)}) %collective-permute-start.13) | collective-permute-done | bytes 98336 | tf_op jit(solution)/shard_map/ppermute | solution.py:19
  61.1 1.6 %collective-permute-start.14 = (bf16[64,768]{1,0:T(8,128)(2,1)S(1)}, bf16[64,768]{1,0:T(8,128)(2,1)S(1)}, u32[]{:S(2)}, u32[]{:S(2)}) collective-permute-start(bf16[64,768]{1,0:T(8,128)(2,1)S(1)} %add_convert_fusion.3), channel_id=1, source_target_pairs={{1,0},{0,1},{3,2},{2,3},{5,4},{4,5},{7,6},{6,7},{9,8},{8,9},{11,10... | collective-permute-start | bytes 294920 | tf_op jit(solution)/shard_map/ppermute | solution.py:30
  62.7 3.1 %collective-permute-done.14 = bf16[64,768]{1,0:T(8,128)(2,1)S(1)} collective-permute-done((bf16[64,768]{1,0:T(8,128)(2,1)S(1)}, bf16[64,768]{1,0:T(8,128)(2,1)S(1)}, u32[]{:S(2)}, u32[]{:S(2)}) %collective-permute-start.14) | collective-permute-done | bytes 98336 | tf_op jit(solution)/shard_map/ppermute | solution.py:30
  65.9 1.4 %collective-permute-start.15 = (bf16[64,768]{1,0:T(8,128)(2,1)S(1)}, bf16[64,768]{1,0:T(8,128)(2,1)S(1)}, u32[]{:S(2)}, u32[]{:S(2)}) collective-permute-start(bf16[64,768]{1,0:T(8,128)(2,1)S(1)} %add_convert_fusion.2), channel_id=1, source_target_pairs={{2,0},{3,1},{0,2},{1,3},{6,4},{7,5},{4,6},{5,7},{10,8},{11,9},{8,1... | collective-permute-start | bytes 294920 | tf_op jit(solution)/shard_map/ppermute | solution.py:30
  67.2 3.3 %collective-permute-done.15 = bf16[64,768]{1,0:T(8,128)(2,1)S(1)} collective-permute-done((bf16[64,768]{1,0:T(8,128)(2,1)S(1)}, bf16[64,768]{1,0:T(8,128)(2,1)S(1)}, u32[]{:S(2)}, u32[]{:S(2)}) %collective-permute-start.15) | collective-permute-done | bytes 98336 | tf_op jit(solution)/shard_map/ppermute | solution.py:30
  70.6 1.8 %collective-permute-start.16 = (bf16[64,768]{1,0:T(8,128)(2,1)S(1)}, bf16[64,768]{1,0:T(8,128)(2,1)S(1)}, u32[]{:S(2)}, u32[]{:S(2)}) collective-permute-start(bf16[64,768]{1,0:T(8,128)(2,1)S(1)} %add_convert_fusion.1), channel_id=1, source_target_pairs={{4,0},{5,1},{6,2},{7,3},{0,4},{1,5},{2,6},{3,7},{12,8},{13,9},{14,... | collective-permute-start | bytes 294920 | tf_op jit(solution)/shard_map/ppermute | solution.py:30
  72.4 2.9 %collective-permute-done.16 = bf16[64,768]{1,0:T(8,128)(2,1)S(1)} collective-permute-done((bf16[64,768]{1,0:T(8,128)(2,1)S(1)}, bf16[64,768]{1,0:T(8,128)(2,1)S(1)}, u32[]{:S(2)}, u32[]{:S(2)}) %collective-permute-start.16) | collective-permute-done | bytes 98336 | tf_op jit(solution)/shard_map/ppermute | solution.py:30
  75.3 2.7 %collective-permute-start.17 = (bf16[64,768]{1,0:T(8,128)(2,1)S(1)}, bf16[64,768]{1,0:T(8,128)(2,1)S(1)}, u32[]{:S(2)}, u32[]{:S(2)}) collective-permute-start(bf16[64,768]{1,0:T(8,128)(2,1)S(1)} %add_convert_fusion), channel_id=1, source_target_pairs={{8,0},{9,1},{10,2},{11,3},{12,4},{13,5},{14,6},{15,7},{0,8},{1,9},... | collective-permute-start | bytes 294920 | tf_op jit(solution)/shard_map/ppermute | solution.py:30
  78.0 1.0 %shard_map.146 = (f32[128,768]{1,0:T(8,128)}, bf16[128,768]{1,0:T(8,128)(2,1)}, f32[128,1]{1,0:T(8,128)S(1)}) custom-call(bf16[128,128]{1,0:T(8,128)(2,1)S(1)} %get-tuple-element.46.weights_ref, bf16[128,768]{1,0:T(8,128)(2,1)S(1)} %get-tuple-element.47.updated_ref, f32[128,1]{1,0:T(8,128)S(1)} %get-tuple-element.48.loss_ref, bf16[64,768]{1,0:T(8,128)(2,1)S(1)} %copy-done.1, ...), custom_call_target="tpu_custom_call" | custom-call | tf_op jit(solution)/shard_map/pallas_call | solution.py:38
  79.7 1.2 %collective-permute-done.17 = bf16[64,768]{1,0:T(8,128)(2,1)S(1)} collective-permute-done((bf16[64,768]{1,0:T(8,128)(2,1)S(1)}, bf16[64,768]{1,0:T(8,128)(2,1)S(1)}, u32[]{:S(2)}, u32[]{:S(2)}) %collective-permute-start.17) | collective-permute-done | bytes 98336 | tf_op jit(solution)/shard_map/ppermute | solution.py:30
  80.9 0.7 add_multiply_fusion
  (46 shorter events, 4.0 us)
Async XLA Ops:
  0.6 1.1 %copy-start.10 = (bf16[192,768]{1,0:T(8,128)(2,1)S(1)}, bf16[192,768]{1,0:T(8,128)(2,1)}, u32[]{:S(2)}) copy-start(bf16[192,768]{1,0:T(8,128)(2,1)} %param.18) | copy-start | bytes 884740
  1.7 20.3 %copy-start = (bf16[256,768]{1,0:T(8,128)(2,1)S(1)}, bf16[256,768]{1,0:T(8,128)(2,1)}, u32[]{:S(2)}) copy-start(bf16[256,768]{1,0:T(8,128)(2,1)} %table_ref.1) | copy-start | bytes 1179652
  1.7 21.6 %copy-start.9 = (bf16[384,768]{1,0:T(8,128)(2,1)}, bf16[384,768]{1,0:T(8,128)(2,1)S(1)}, u32[]{:S(2)}) copy-start(bf16[384,768]{1,0:T(8,128)(2,1)S(1)} %constant_dynamic-update-slice_fusion.refs_0_) | copy-start | bytes 1769476
  1.7 19.7 %collective-permute-start = (bf16[384,768]{1,0:T(8,128)(2,1)S(1)}, bf16[384,768]{1,0:T(8,128)(2,1)}, u32[]{:S(2)}, u32[]{:S(2)}) collective-permute-start(bf16[384,768]{1,0:T(8,128)(2,1)S(1)} %constant_dynamic-update-slice_fusion.refs_0_), channel_id=1, source_target_pairs={{1,0},{0,1},{3,2},{2,3},{5,4},{4,5},{7,6},{6,7},{9,8},{8,9},{11,10... | collective-permute-start | bytes 1769480 | tf_op jit(solution)/shard_map/ppermute | solution.py:30
  4.7 0.7 copy-start.5
  4.7 0.7 copy-start.7
  4.7 0.7 copy-start.8
  5.8 17.5 %collective-permute-start.1 = (bf16[384,768]{1,0:T(8,128)(2,1)S(1)}, bf16[384,768]{1,0:T(8,128)(2,1)S(1)}, u32[]{:S(2)}, u32[]{:S(2)}) collective-permute-start(bf16[384,768]{1,0:T(8,128)(2,1)S(1)} %constant_dynamic-update-slice_fusion.refs_0_), channel_id=1, source_target_pairs={{2,0},{3,1},{0,2},{1,3},{6,4},{7,5},{4,6},{5,7},{10,8},{11,9},{8,1... | collective-permute-start | bytes 1769480 | tf_op jit(solution)/shard_map/ppermute | solution.py:30
  21.4 12.2 %collective-permute-start.4 = (bf16[384,768]{1,0:T(8,128)(2,1)}, bf16[384,768]{1,0:T(8,128)(2,1)S(1)}, u32[]{:S(2)}, u32[]{:S(2)}) collective-permute-start(bf16[384,768]{1,0:T(8,128)(2,1)} %collective-permute-done.refs_1_), channel_id=1, source_target_pairs={{2,0},{3,1},{0,2},{1,3},{6,4},{7,5},{4,6},{5,7},{10,8},{11,9},{8,1... | collective-permute-start | bytes 1769480 | tf_op jit(solution)/shard_map/ppermute | solution.py:30
  23.3 3.7 %copy-start.2 = (bf16[128,768]{1,0:T(8,128)(2,1)S(1)}, bf16[128,768]{1,0:T(8,128)(2,1)}, u32[]{:S(2)}) copy-start(bf16[128,768]{1,0:T(8,128)(2,1)} %queries_ref.1) | copy-start | bytes 589828
  23.3 3.7 %copy-start.3 = (bf16[768]{0:T(1024)(128)(2,1)S(1)}, bf16[768]{0:T(1024)(128)(2,1)}, u32[]{:S(2)}) copy-start(bf16[768]{0:T(1024)(128)(2,1)} %gain_ref.1) | copy-start | bytes 4612
  23.3 3.8 %copy-start.4 = (bf16[768]{0:T(1024)(128)(2,1)S(1)}, bf16[768]{0:T(1024)(128)(2,1)}, u32[]{:S(2)}) copy-start(bf16[768]{0:T(1024)(128)(2,1)} %bias_ref.3) | copy-start | bytes 4612
  23.3 15.9 %all-to-all-start.1 = ((bf16[16,16,768]{2,1,0:T(8,128)(2,1)}), bf16[16,16,768]{2,1,0:T(8,128)(2,1)S(1)}, u32[]{:S(2)}, u32[]{:S(2)}) async-start(bf16[16,16,768]{2,1,0:T(8,128)(2,1)} %bitcast.3), calls=%async_computation.1 | async-start | bytes 786432 | tf_op jit(solution)/shard_map/all_to_all | solution.py:299
  27.0 0.7 copy-start.6
  27.8 6.5 %collective-permute-start.2 = (bf16[384,768]{1,0:T(8,128)(2,1)}, bf16[384,768]{1,0:T(8,128)(2,1)}, u32[]{:S(2)}, u32[]{:S(2)}) collective-permute-start(bf16[384,768]{1,0:T(8,128)(2,1)} %collective-permute-done.refs_1_), channel_id=1, source_target_pairs={{0,16},{16,0},{1,17},{17,1},{2,18},{18,2},{3,19},{19,3},{4,20},{20... | collective-permute-start | bytes 1769480 | tf_op jit(solution)/shard_map/ppermute | solution.py:19
  29.4 12.9 %collective-permute-start.7 = (bf16[384,768]{1,0:T(8,128)(2,1)}, bf16[384,768]{1,0:T(8,128)(2,1)S(1)}, u32[]{:S(2)}, u32[]{:S(2)}) collective-permute-start(bf16[384,768]{1,0:T(8,128)(2,1)} %collective-permute-done.refs_1_), channel_id=1, source_target_pairs={{18,16},{19,17},{16,18},{17,19},{22,20},{23,21},{20,22},{21,23},{2... | collective-permute-start | bytes 1769480 | tf_op jit(solution)/shard_map/ppermute | solution.py:30
  33.6 13.7 %collective-permute-start.9 = (bf16[384,768]{1,0:T(8,128)(2,1)S(1)}, bf16[384,768]{1,0:T(8,128)(2,1)S(1)}, u32[]{:S(2)}, u32[]{:S(2)}) collective-permute-start(bf16[384,768]{1,0:T(8,128)(2,1)S(1)} %collective-permute-done.4.refs_3_), channel_id=1, source_target_pairs={{18,16},{19,17},{16,18},{17,19},{22,20},{23,21},{20,22},{21,23},{2... | collective-permute-start | bytes 1769480 | tf_op jit(solution)/shard_map/ppermute | solution.py:30
  39.7 7.6 %collective-permute-start.3 = (bf16[128,768]{1,0:T(8,128)(2,1)S(1)}, bf16[128,768]{1,0:T(8,128)(2,1)S(1)}, u32[]{:S(2)}, u32[]{:S(2)}) collective-permute-start(bf16[128,768]{1,0:T(8,128)(2,1)S(1)} %get-tuple-element.43.normed_ref), channel_id=1, source_target_pairs={{0,4},{1,5},{2,6},{3,7},{4,0},{5,1},{6,2},{7,3},{8,12},{9,13},{10,... | collective-permute-start | bytes 589832 | tf_op jit(solution)/shard_map/ppermute | solution.py:19
  41.8 6.6 %collective-permute-start.5 = (bf16[384,768]{1,0:T(8,128)(2,1)S(1)}, bf16[384,768]{1,0:T(8,128)(2,1)S(1)}, u32[]{:S(2)}, u32[]{:S(2)}) collective-permute-start(bf16[384,768]{1,0:T(8,128)(2,1)S(1)} %collective-permute-done.4.refs_3_), channel_id=1, source_target_pairs={{0,16},{16,0},{1,17},{17,1},{2,18},{18,2},{3,19},{19,3},{4,20},{20... | collective-permute-start | bytes 1769480 | tf_op jit(solution)/shard_map/ppermute | solution.py:19
  42.2 6.2 %collective-permute-start.6 = (bf16[384,768]{1,0:T(8,128)(2,1)S(1)}, bf16[384,768]{1,0:T(8,128)(2,1)S(1)}, u32[]{:S(2)}, u32[]{:S(2)}) collective-permute-start(bf16[384,768]{1,0:T(8,128)(2,1)S(1)} %collective-permute-done.1.refs_5_), channel_id=1, source_target_pairs={{0,16},{16,0},{1,17},{17,1},{2,18},{18,2},{3,19},{19,3},{4,20},{20... | collective-permute-start | bytes 1769480 | tf_op jit(solution)/shard_map/ppermute | solution.py:19
  42.3 6.1 %collective-permute-start.8 = (bf16[384,768]{1,0:T(8,128)(2,1)S(1)}, bf16[384,768]{1,0:T(8,128)(2,1)S(1)}, u32[]{:S(2)}, u32[]{:S(2)}) collective-permute-start(bf16[384,768]{1,0:T(8,128)(2,1)S(1)} %collective-permute-done.7.refs_8_), channel_id=1, source_target_pairs={{0,16},{16,0},{1,17},{17,1},{2,18},{18,2},{3,19},{19,3},{4,20},{20... | collective-permute-start | bytes 1769480 | tf_op jit(solution)/shard_map/ppermute | solution.py:19
  47.2 4.0 %collective-permute-start.10 = (bf16[384,768]{1,0:T(8,128)(2,1)S(1)}, bf16[384,768]{1,0:T(8,128)(2,1)S(1)}, u32[]{:S(2)}, u32[]{:S(2)}) collective-permute-start(bf16[384,768]{1,0:T(8,128)(2,1)S(1)} %collective-permute-done.9.refs_2_.refs_10_), channel_id=1, source_target_pairs={{0,16},{16,0},{1,17},{17,1},{2,18},{18,2},{3,19},{19,3},{4,20},{20... | collective-permute-start | bytes 1769480 | tf_op jit(solution)/shard_map/ppermute | solution.py:19
  51.2 2.7 %copy-start.1 = (bf16[64,768]{1,0:T(8,128)(2,1)S(1)}, bf16[64,768]{1,0:T(8,128)(2,1)}, u32[]{:S(2)}) copy-start(bf16[64,768]{1,0:T(8,128)(2,1)} %refs_0_.3) | copy-start | bytes 294916
  51.9 7.0 %collective-permute-start.11 = (bf16[128,768]{1,0:T(8,128)(2,1)S(1)}, bf16[128,768]{1,0:T(8,128)(2,1)S(1)}, u32[]{:S(2)}, u32[]{:S(2)}) collective-permute-start(bf16[128,768]{1,0:T(8,128)(2,1)S(1)} %shard_map.143), channel_id=1, source_target_pairs={{0,4},{1,5},{2,6},{3,7},{4,0},{5,1},{6,2},{7,3},{8,12},{9,13},{10,... | collective-permute-start | bytes 589832 | tf_op jit(solution)/shard_map/ppermute | solution.py:19
  53.9 2.8 %collective-permute-start.12 = (bf16[64,768]{1,0:T(8,128)(2,1)S(1)}, bf16[64,768]{1,0:T(8,128)(2,1)S(1)}, u32[]{:S(2)}, u32[]{:S(2)}) collective-permute-start(bf16[64,768]{1,0:T(8,128)(2,1)S(1)} %copy-done.1), channel_id=1, source_target_pairs={{0,16},{16,0},{1,17},{17,1},{2,18},{18,2},{3,19},{19,3},{4,20},{20... | collective-permute-start | bytes 294920 | tf_op jit(solution)/shard_map/ppermute | solution.py:19
  59.7 1.4 %collective-permute-start.13 = (bf16[64,768]{1,0:T(8,128)(2,1)S(1)}, bf16[64,768]{1,0:T(8,128)(2,1)S(1)}, u32[]{:S(2)}, u32[]{:S(2)}) collective-permute-start(bf16[64,768]{1,0:T(8,128)(2,1)S(1)} %get-tuple-element.53), channel_id=1, source_target_pairs={{0,16},{16,0},{1,17},{17,1},{2,18},{18,2},{3,19},{19,3},{4,20},{20... | collective-permute-start | bytes 294920 | tf_op jit(solution)/shard_map/ppermute | solution.py:19
  61.1 4.7 %collective-permute-start.14 = (bf16[64,768]{1,0:T(8,128)(2,1)S(1)}, bf16[64,768]{1,0:T(8,128)(2,1)S(1)}, u32[]{:S(2)}, u32[]{:S(2)}) collective-permute-start(bf16[64,768]{1,0:T(8,128)(2,1)S(1)} %add_convert_fusion.3), channel_id=1, source_target_pairs={{1,0},{0,1},{3,2},{2,3},{5,4},{4,5},{7,6},{6,7},{9,8},{8,9},{11,10... | collective-permute-start | bytes 294920 | tf_op jit(solution)/shard_map/ppermute | solution.py:30
  65.9 4.7 %collective-permute-start.15 = (bf16[64,768]{1,0:T(8,128)(2,1)S(1)}, bf16[64,768]{1,0:T(8,128)(2,1)S(1)}, u32[]{:S(2)}, u32[]{:S(2)}) collective-permute-start(bf16[64,768]{1,0:T(8,128)(2,1)S(1)} %add_convert_fusion.2), channel_id=1, source_target_pairs={{2,0},{3,1},{0,2},{1,3},{6,4},{7,5},{4,6},{5,7},{10,8},{11,9},{8,1... | collective-permute-start | bytes 294920 | tf_op jit(solution)/shard_map/ppermute | solution.py:30
  70.6 4.7 %collective-permute-start.16 = (bf16[64,768]{1,0:T(8,128)(2,1)S(1)}, bf16[64,768]{1,0:T(8,128)(2,1)S(1)}, u32[]{:S(2)}, u32[]{:S(2)}) collective-permute-start(bf16[64,768]{1,0:T(8,128)(2,1)S(1)} %add_convert_fusion.1), channel_id=1, source_target_pairs={{4,0},{5,1},{6,2},{7,3},{0,4},{1,5},{2,6},{3,7},{12,8},{13,9},{14,... | collective-permute-start | bytes 294920 | tf_op jit(solution)/shard_map/ppermute | solution.py:30
  75.3 5.6 %collective-permute-start.17 = (bf16[64,768]{1,0:T(8,128)(2,1)S(1)}, bf16[64,768]{1,0:T(8,128)(2,1)S(1)}, u32[]{:S(2)}, u32[]{:S(2)}) collective-permute-start(bf16[64,768]{1,0:T(8,128)(2,1)S(1)} %add_convert_fusion), channel_id=1, source_target_pairs={{8,0},{9,1},{10,2},{11,3},{12,4},{13,5},{14,6},{15,7},{0,8},{1,9},... | collective-permute-start | bytes 294920 | tf_op jit(solution)/shard_map/ppermute | solution.py:30
